TPU v7x, 32 devices: a whole 2x2x4 slice. The times are simulated.
32 devices in a mesh: row: 8 (over y, x, core), col: 4 (over z).
Axes of the slice: x: 2, y: 2, z: 4, core: 2. Of those that a mesh axis runs over, the one named last changes fastest.
Arguments:
- tokens: bfloat16 [512, 8192], P('col', 'row'), may hold values from -6 to 6
- w_packed: bfloat16 [8, 4, 448, 128, 128], P('row', 'col'), may hold values from -0.09375 to 0.09375
- kept_rows: int32 [8, 4, 448], P('row', 'col'), may hold values from 0 to 7, as said below
- kept_cols: int32 [8, 4, 448], P('row', 'col'), may hold values from 0 to 55, as said below
- kept_count: int32 [8, 4], P('row', 'col'), may hold values from 1 to 448, as said below
- grad_act: bfloat16 [512, 28672], P('row', 'col'), may hold values from -6 to 6
Outputs:
- activation: bfloat16 [512, 28672], P('row', 'col')
- input_grad: bfloat16 [512, 8192], P('col', 'row')
- weight_grad: bfloat16 [8, 4, 448, 128, 128], P('row', 'col')
Inputs may be any that keep to these rules, and one draw needn't show every extreme that they name: Within each tile, the 448 slots name every block of the tile once (kept_rows[r, c, s] * 56 + kept_cols[r, c, s] runs over all block places). `kept_cols`: see kept_rows. `kept_count`: some tile in every draw keeps all 448 blocks.
All inputs are finite; a program needn't handle non-finite values.
Results may differ from a plain program's by a relative error of at most 0.0049.
Values may be sent and summed in bfloat16 or wider, within the bound.
No kernel may reach another device: no remote copies, remote signals or barrier semaphores. Data moves between devices by JAX's collectives and lax.ppermute only.
A program may use at most 384 MiB of HBM per device.

v0:
```python
import functools

import jax
import jax.numpy as jnp
import numpy as np
from jax import lax
from jax.experimental import pallas as pl
from jax.experimental.pallas import tpu as pltpu
from jax.sharding import PartitionSpec as P

gelu_scale = 0.7978845608
gelu_cubic = 0.044715
token_parts = 2
column_parts = 2
vmem_limit = 16 * 1024 * 1024
in_vmem = pl.BlockSpec(memory_space=pltpu.VMEM)
in_smem = pl.BlockSpec(memory_space=pltpu.SMEM)
anywhere = pl.BlockSpec(memory_space=pltpu.HBM)


def gelu_pair(hidden, cotangent):
    inner = gelu_scale * (hidden + gelu_cubic * hidden * hidden * hidden)
    tangent = jnp.tanh(inner)
    activation = (0.5 * hidden * (1.0 + tangent)).astype(jnp.bfloat16)
    slope = 0.5 * (1.0 + tangent) + 0.5 * hidden * (1.0 - tangent * tangent) * gelu_scale * (
        1.0 + 3.0 * gelu_cubic * hidden * hidden
    )
    slope_grad = (cotangent.astype(jnp.float32) * slope).astype(jnp.bfloat16)
    return (activation, slope_grad)


def group_of(blocks, goal):
    return max(n for n in range(1, goal + 1) if blocks % n == 0)


class Core:
    def __init__(self):
        self.turn = None

    def __call__(self, kernel, name, out_shape, out_specs, in_specs, operands, scratch=(), aliases=None):
        homes = {id(in_vmem): pltpu.VMEM, id(anywhere): pltpu.HBM}
        in_specs, operands = list(in_specs), list(operands)
        if self.turn is not None:
            in_specs.append(in_vmem)
            operands.append(self.turn)
        taken = len(operands)
        given = len(out_shape)
        extra = self.turn is not None

        def body(*refs):
            refs[taken + given][...] = jnp.zeros((8, 128), jnp.float32)
            kernel(*refs[: taken - extra], *refs[taken : taken + given], *refs[taken + given + 1 :])

        placed = [
            pltpu.with_memory_space_constraint(x, homes[id(spec)]) if id(spec) in homes else x
            for x, spec in zip(operands, in_specs)
        ]
        *out, self.turn = pl.pallas_call(
            body,
            out_shape=[*out_shape, pltpu.VMEM((8, 128), jnp.float32)],
            in_specs=in_specs,
            out_specs=[*out_specs, in_vmem],
            scratch_shapes=list(scratch),
            input_output_aliases=aliases or {},
            compiler_params=pltpu.CompilerParams(vmem_limit_bytes=vmem_limit),
            cost_estimate=pl.CostEstimate(flops=1, transcendentals=0, bytes_accessed=1),
            name=name,
        )(*placed)
        return out


def dense_kernel(row_blocks, col_blocks, code, w_ref, out_ref, empty, sem):
    blk = w_ref.shape[-1]
    empty[...] = jnp.zeros_like(empty)

    def load(at, carry):
        for r in range(row_blocks):
            entry = code[r * col_blocks + at]
            start = pl.multiple_of(at * blk, blk)
            target = out_ref.at[pl.ds(r * blk, blk), pl.ds(start, blk)]

            @pl.when(lax.rem(entry, 2) == 1)
            def _():
                pltpu.make_async_copy(w_ref.at[0, 0, lax.div(entry, 2)], target, sem).start()

            @pl.when(lax.rem(entry, 2) == 0)
            def _():
                pltpu.make_async_copy(empty, target, sem).start()

        return carry

    lax.fori_loop(0, col_blocks, load, 0)
    pltpu.make_async_copy(out_ref, out_ref, sem).wait()


def dense_tile(core, w_packed, code, row_blocks, col_blocks):
    blk = w_packed.shape[-1]
    [weight] = core(
        functools.partial(dense_kernel, row_blocks, col_blocks),
        "dense_tile",
        [pltpu.VMEM((row_blocks * blk, col_blocks * blk), w_packed.dtype)],
        [in_vmem],
        [in_smem, anywhere],
        (code, w_packed),
        scratch=[pltpu.VMEM((blk, blk), w_packed.dtype), pltpu.SemaphoreType.DMA],
    )
    return weight


def arrange_kernel(groups, rows, pieces, pick, *refs):
    out_ref, turned_ref, all_ref = refs[pieces:]
    each = groups // pieces
    for m in range(pieces):
        for j in range(each):
            all_ref[m * each + j] = refs[m][j]
    for t in range(groups):
        out_ref[pl.ds(t * rows, rows), :] = all_ref[pick[t]]
    turned_ref[...] = out_ref[...].T


def arrange(core, pieces, pick):
    groups = pick.shape[0]
    rows, tall = pieces[0].shape[1:]
    kind = pieces[0].dtype
    return core(
        functools.partial(arrange_kernel, groups, rows, len(pieces)),
        "arrange",
        [pltpu.VMEM((groups * rows, tall), kind), pltpu.VMEM((tall, groups * rows), kind)],
        [in_vmem, in_vmem],
        [in_smem] + [in_vmem] * len(pieces),
        (pick, *pieces),
        scratch=[pltpu.VMEM((groups, rows, tall), kind)],
    )


def forward_kernel(first, wide, x_ref, w_ref, keep_ref, send_ref):
    half, width = keep_ref.shape
    for at in range(0, width, wide):
        product = jnp.dot(
            x_ref[...], w_ref[:, first + at : first + at + wide], preferred_element_type=jnp.float32
        )
        keep_ref[:, at : at + wide] = product[:half]
        send_ref[:, at : at + wide] = product[half:].astype(jnp.bfloat16)


def forward(core, features, weight, first, width):
    half = features.shape[0] // 2
    wide = 128 * group_of(width // 128, 4)
    return core(
        functools.partial(forward_kernel, first, wide),
        "forward",
        [pltpu.VMEM((half, width), jnp.float32), pltpu.VMEM((half, width), jnp.bfloat16)],
        [in_vmem, in_vmem],
        [in_vmem, in_vmem],
        (features, weight),
    )


def sides(left, bit):
    at = len(left) - 1 - left.index(bit)
    names = range(1 << len(left))
    return [g for g in names if not g >> at & 1], [g for g in names if g >> at & 1]


def add_kernel(rows, stay, leave, keep_ref, arrived_ref, next_ref, send_ref):
    for out_ref, groups in ((next_ref, stay), (send_ref, leave)):
        for at, g in enumerate(groups):
            here = slice(g * rows, (g + 1) * rows)
            total = keep_ref[here, :] + arrived_ref[here, :].astype(jnp.float32)
            out_ref[at * rows : (at + 1) * rows, :] = total.astype(out_ref.dtype)


def add_step(core, keep, arrived, left, bit):
    rows = keep.shape[0] >> len(left)
    half = (keep.shape[0] // 2, keep.shape[1])
    return core(
        functools.partial(add_kernel, rows, *sides(left, bit)),
        "add_step",
        [pltpu.VMEM(half, jnp.float32), pltpu.VMEM(half, jnp.bfloat16)],
        [in_vmem, in_vmem],
        [in_vmem, in_vmem],
        (keep, arrived),
    )


def join_kernel(rows, stay, come, near_ref, arrived_ref, out_ref):
    for in_ref, groups in ((near_ref, stay), (arrived_ref, come)):
        for at, g in enumerate(groups):
            out_ref[g * rows : (g + 1) * rows, :] = in_ref[at * rows : (at + 1) * rows, :]


def join_step(core, near, arrived, held, bit):
    rows = 2 * near.shape[0] >> len(held)
    [out] = core(
        functools.partial(join_kernel, rows, *sides(held, bit)),
        "join_step",
        [pltpu.VMEM((2 * near.shape[0], near.shape[1]), near.dtype)],
        [in_vmem],
        [in_vmem, in_vmem],
        (near, arrived),
    )
    return out


def gelu_kernel(top, first, keep_ref, arrived_ref, cotangent_ref, activation_ref, slope_ref):
    rows, width = keep_ref.shape
    hidden = keep_ref[...] + arrived_ref[...].astype(jnp.float32)
    cotangent = cotangent_ref[top : top + rows, first : first + width]
    activation_ref[...], slope_ref[...] = gelu_pair(hidden, cotangent)


def gelu(core, keep, arrived, cotangent, top, first):
    out = pltpu.VMEM(keep.shape, jnp.bfloat16)
    return core(
        functools.partial(gelu_kernel, top, first),
        "gelu",
        [out, out],
        [in_vmem, in_vmem],
        [in_vmem] * 3,
        (keep, arrived, cotangent),
    )


def input_kernel(first, groups, has_before, finished, given, place, near_ref, far_ref, w_ref, *refs):
    half, width = near_ref.shape
    rows = 2 * half // groups
    tall = w_ref.shape[0]
    before = refs[0] if has_before else None
    outs = refs[has_before : has_before + given]
    scratch = refs[has_before + given :]
    turned = scratch[0]
    total = scratch[1] if finished else outs[0]
    wide = 128 * group_of(width // 128, 4)
    for at in range(0, width, wide):
        here = slice(at, at + wide)
        grad = jnp.concatenate([near_ref[:, here], far_ref[:, here]], axis=0)
        turned[here, :] = grad.T
    high = 128 * group_of(tall // 128, 4)
    for at in range(0, tall, high):
        here = slice(at, at + high)
        product = jnp.dot(
            w_ref[here, first : first + width], turned[...], preferred_element_type=jnp.float32
        )
        total[here, :] = product + before[here, :] if has_before else product
    if finished:
        upright = scratch[2]
        upright[...] = total[...].T
        each = groups // given
        for i in range(groups):
            start = pl.multiple_of(place[i] * rows, rows)
            out_ref = outs[i // each]
            at = i % each * rows
            out_ref[at : at + rows, :] = upright[pl.ds(start, rows), :].astype(out_ref.dtype)


def input_partial(core, near, far, weight, first, place, before, pieces):
    half, width = near.shape
    tall = weight.shape[0]
    both = 2 * half
    if pieces:
        outs = [pltpu.VMEM((both // pieces, tall), jnp.float32)]
        outs += [pltpu.VMEM((both // pieces, tall), jnp.bfloat16)] * (pieces - 1)
    else:
        outs = [pltpu.VMEM((tall, both), jnp.float32)]
    has_before = before is not None
    scratch = [pltpu.VMEM((width, both), near.dtype)]
    if pieces:
        scratch += [pltpu.VMEM((tall, both), jnp.float32), pltpu.VMEM((both, tall), jnp.float32)]
    return core(
        functools.partial(
            input_kernel, first, place.shape[0], has_before, pieces > 0, len(outs)
        ),
        "input_partial",
        outs,
        [in_vmem] * len(outs),
        [in_smem] + [in_vmem] * (4 if has_before else 3),
        (place, near, far, weight) + ((before,) if has_before else ()),
        scratch=scratch,
    )


def weight_kernel(row_blocks, col_blocks, first, parts, has_before, code, *refs):
    turned = refs[:parts]
    grads = refs[parts : 3 * parts]
    out_ref, made, sem = refs[3 * parts + has_before :]
    blk = made.shape[-1]
    width = grads[0].shape[1]
    here = width // blk
    per_step = group_of(here, 2)
    wide = per_step * blk
    for j in range(here // per_step):
        features = jnp.concatenate([t[...] for t in turned], axis=1)
        grad = jnp.concatenate([g[:, j * wide : (j + 1) * wide] for g in grads], axis=0)
        product = jnp.dot(features, grad, preferred_element_type=jnp.float32)
        for r in range(row_blocks):
            for c in range(per_step):
                entry = code[r * col_blocks + first // blk + j * per_step + c]
                live = lax.rem(entry, 2).astype(jnp.float32)
                at = (j * row_blocks + r) * per_step + c
                block = product[r * blk : (r + 1) * blk, c * blk : (c + 1) * blk] * live
                made[at] = block.astype(made.dtype)
                pltpu.make_async_copy(
                    made.at[at], out_ref.at[0, 0, lax.div(entry, 2)], sem
                ).start()
    pltpu.make_async_copy(made, out_ref.at[0, 0, pl.ds(0, made.shape[0])], sem).wait()


def weight_gradient(core, turned, grads, code, first, row_blocks, col_blocks, blk, before):
    parts = len(turned)
    has_before = before is not None
    here = row_blocks * grads[0].shape[1] // blk
    arrays = [*turned, *grads]
    [out] = core(
        functools.partial(weight_kernel, row_blocks, col_blocks, first, parts, has_before),
        "weight_gradient",
        [jax.ShapeDtypeStruct((1, 1, row_blocks * col_blocks, blk, blk), jnp.bfloat16)],
        [anywhere],
        [in_smem] + [in_vmem] * len(arrays) + [anywhere] * has_before,
        (code, *arrays) + ((before,) if has_before else ()),
        scratch=[pltpu.VMEM((here, blk, blk), jnp.bfloat16), pltpu.SemaphoreType.DMA],
        aliases={1 + len(arrays): 0} if has_before else None,
    )
    return out


def swap(array, axis, size, bit):
    return lax.ppermute(array, axis, [(i, i ^ bit) for i in range(size)])


def on_device(tokens, w_packed, kept_rows, kept_cols, kept_count, grad_act):
    blk = w_packed.shape[-1]
    slot_count = w_packed.shape[2]
    tall = tokens.shape[1]
    row_tokens, hidden_here = grad_act.shape
    row_blocks = tall // blk
    col_blocks = hidden_here // blk
    n_row = lax.axis_size("row")
    n_col = lax.axis_size("col")
    row_me = lax.axis_index("row")
    col_me = lax.axis_index("col")
    col_groups = tokens.shape[0] // row_tokens
    parts = group_of(max(1, row_tokens // 16), token_parts)
    rows = row_tokens // parts
    slabs = group_of(col_blocks, column_parts)
    width = hidden_here // slabs
    direct = n_col <= 8
    core = Core()

    places = kept_rows[0, 0] * col_blocks + kept_cols[0, 0]
    slots = jnp.arange(slot_count, dtype=jnp.int32)
    coded = slots * 2 + (slots < kept_count[0, 0]).astype(jnp.int32)
    code = jnp.sum(jnp.where(places[None, :] == slots[:, None], coded[None, :], 0), axis=1)

    apart = row_me ^ (col_me * col_groups) if direct else row_me
    everyone = np.arange(n_row)
    order = np.concatenate([everyone[::2], everyone[1::2]]).astype(np.int32)
    pick = (jnp.asarray(order) ^ apart).astype(jnp.int32)
    distance = jnp.asarray(everyone.astype(np.int32)) ^ apart
    place = ((distance & 1) * (n_row // 2) + (distance >> 1)).astype(jnp.int32)

    mine = tokens.reshape(col_groups, parts, rows, tall)
    pieces = []
    for k in range(parts):
        if direct:
            pieces.append(
                [mine[:, k]] + [swap(mine[:, k], "col", n_col, m) for m in range(1, n_col)]
            )
        else:
            pieces.append([lax.all_gather(mine[:, k], "col", axis=0, tiled=True)])
    weight = dense_tile(core, w_packed, code, row_blocks, col_blocks)

    far_bits = [1 << b for b in range(1, n_row.bit_length() - 1)]
    units = [(k, c) for k in range(parts) for c in range(slabs)]
    paths = [far_bits if at % 2 == 0 else far_bits[::-1] for at in range(len(units))]
    state = {}
    full, turned = {}, {}
    activations, sums, input_grads = {}, {}, {}

    def begin(k, c, path):
        if c == 0:
            full[k], turned[k] = arrange(core, pieces[k], pick)
        keep, send = forward(core, full[k], weight, c * width, width)
        state[k, c] = (keep, swap(send, "row", n_row, 1))

    def add(at, k, c, path):
        left = sorted(path[at:], reverse=True)
        keep, send = add_step(core, *state[k, c], left, path[at])
        state[k, c] = (keep, swap(send, "row", n_row, path[at]))

    def bend(k, c, path):
        activations[k, c], near = gelu(core, *state[k, c], grad_act, k * rows, c * width)
        state[k, c] = (near, swap(near, "row", n_row, ([1] + path)[-1]))

    def join(at, k, c, path):
        held = sorted(path[at:], reverse=True)
        near = join_step(core, *state[k, c], held, path[at])
        state[k, c] = (near, swap(near, "row", n_row, ([1] + path)[at]))

    def finish(k, c, path):
        last = c + 1 == slabs
        cut = (n_col if direct else 1) * last
        found = input_partial(
            core, *state[k, c], weight, c * width, place, sums.get((k, c - 1)), cut
        )
        sums[k, c] = found[0]
        if last and direct:
            total = found[0]
            for m in range(1, n_col):
                total = total + swap(found[m], "col", n_col, m).astype(jnp.float32)
        elif last:
            total = found[0].reshape(n_col, col_groups * rows, tall)
            total = lax.psum_scatter(total, "col", scatter_dimension=0, tiled=True)[0]
        if last:
            total = total.astype(jnp.bfloat16)
            input_grads[k] = total.reshape(col_groups, 1, rows, tall)

    hops = len(far_bits)
    stages = [begin] + [functools.partial(add, at) for at in range(hops)] + [bend]
    stages += [functools.partial(join, at) for at in reversed(range(hops))] + [finish]
    plan = []
    if parts == 2 and hops == 2:
        plan = [(0, 0), (0, 1), (0, 2), (1, 0), (1, 1), (0, 3), (1, 2), (0, 4), (1, 3)]
        plan += [(0, 5), (1, 4), (0, 6), (1, 5), (1, 6)]
    else:
        plan = [(k, at) for at in range(len(stages)) for k in range(parts)]
    for k, at in plan:
        for c in range(slabs):
            stages[at](k, c, paths[units.index((k, c))])
    weight_grad = None
    for c in range(slabs):
        weight_grad = weight_gradient(
            core,
            [turned[k] for k in range(parts)],
            [g for k in range(parts) for g in state[k, c]],
            code,
            c * width,
            row_blocks,
            col_blocks,
            blk,
            weight_grad,
        )
    activation = jnp.concatenate(
        [jnp.concatenate([activations[k, c] for c in range(slabs)], axis=1) for k in range(parts)],
        axis=0,
    )
    input_grad = jnp.concatenate([input_grads[k] for k in range(parts)], axis=1).reshape(tokens.shape)
    return (activation, input_grad, weight_grad)


def solution(mesh):
    placed = (
        P("col", "row"),
        P("row", "col", None, None, None),
        P("row", "col", None),
        P("row", "col", None),
        P("row", "col"),
        P("row", "col"),
    )
    return jax.shard_map(
        on_device,
        mesh=mesh,
        in_specs=placed,
        out_specs=(P("row", "col"), P("col", "row"), P("row", "col", None, None, None)),
        check_vma=False,
    )
```

profile of v0, /device:TPU:0, one launch (start us, length us, event | category | flops | bytes accessed | tf_op | source)
XLA Modules:
  0.0 137.6 jit_solution(3417312067386221107)
XLA Ops:
  1.6 5.1 %collective-permute-start.2 = (bf16[2,32,1024]{2,1,0:T(8,128)(2,1)S(1)}, bf16[2,32,1024]{2,1,0:T(8,128)(2,1)S(1)}, u32[]{:S(2)}, u32[]{:S(2)}) collective-permute-start(bf16[2,32,1024]{2,1,0:T(8,128)(2,1)S(1)} %get-tuple-element.181.refs_1_), channel_id=1, source_target_pairs={{0,3},{1,2},{2,1},{3,0},{4,7},{5,6},{6,5},{7,4},{8,11},{9,10},{10,... | collective-permute-start | bytes 393224 | tf_op jit(solution)/shard_map/ppermute | solution.py:327
  9.0 7.4 %dense_tile.1 = (bf16[1024,7168]{1,0:T(8,128)(2,1)S(1)}, f32[8,128]{1,0:T(8,128)S(1)}) custom-call(s32[448]{0:T(512)S(1)} %select_reduce_fusion.refs_0_, bf16[1,1,448,128,128]{4,3,2,1,0:T(8,128)(2,1)} %refs_1_.1), custom_call_target="tpu_custom_call" | custom-call | flops 1 | bytes 1 | tf_op jit(solution)/shard_map/dense_tile/pallas_call | solution.py:58
  18.6 2.1 %forward.4 = (f32[128,3584]{1,0:T(8,128)S(1)}, bf16[128,3584]{1,0:T(8,128)(2,1)S(1)}, f32[8,128]{1,0:T(8,128)S(1)}) custom-call(bf16[256,1024]{1,0:T(8,128)(2,1)S(1)} %get-tuple-element.93.refs_0_, bf16[1024,7168]{1,0:T(8,128)(2,1)S(1)} %get-tuple-element.94.refs_1_.refs_3_, f32[8,128]{1,0:T(8,128)S(1)} %get-tuple-element.95.refs_2_), custom_call_target="tpu_custom_call" | custom-call | flops 1 | bytes 1 | tf_op jit(solution)/shard_map/forward/pallas_call | solution.py:58
  20.8 2.1 %forward.5 = (f32[128,3584]{1,0:T(8,128)S(1)}, bf16[128,3584]{1,0:T(8,128)(2,1)S(1)}, f32[8,128]{1,0:T(8,128)S(1)}) custom-call(bf16[256,1024]{1,0:T(8,128)(2,1)S(1)} %get-tuple-element.93.refs_0_, bf16[1024,7168]{1,0:T(8,128)(2,1)S(1)} %get-tuple-element.94.refs_1_.refs_3_, f32[8,128]{1,0:T(8,128)S(1)} %get-tuple-element.98.refs_2_), custom_call_target="tpu_custom_call" | custom-call | flops 1 | bytes 1 | tf_op jit(solution)/shard_map/forward/pallas_call | solution.py:58
  23.7 1.6 %collective-permute-start.4 = (bf16[64,3584]{1,0:T(8,128)(2,1)S(1)}, bf16[64,3584]{1,0:T(8,128)(2,1)S(1)}, u32[]{:S(2)}, u32[]{:S(2)}) collective-permute-start(bf16[64,3584]{1,0:T(8,128)(2,1)S(1)} %get-tuple-element.101), channel_id=1, source_target_pairs={{0,8},{4,12},{8,0},{12,4},{16,24},{20,28},{24,16},{28,20},{1,9},{5... | collective-permute-start | bytes 1376264 | tf_op jit(solution)/shard_map/ppermute | solution.py:327
  25.8 1.6 %collective-permute-start.10 = (bf16[64,3584]{1,0:T(8,128)(2,1)S(1)}, bf16[64,3584]{1,0:T(8,128)(2,1)S(1)}, u32[]{:S(2)}, u32[]{:S(2)}) collective-permute-start(bf16[64,3584]{1,0:T(8,128)(2,1)S(1)} %get-tuple-element.109), channel_id=1, source_target_pairs={{0,16},{4,20},{8,24},{12,28},{16,0},{20,4},{24,8},{28,12},{1,17},{... | collective-permute-start | bytes 1376264 | tf_op jit(solution)/shard_map/ppermute | solution.py:327
  27.4 2.5 %collective-permute-start.9 = (bf16[2,32,1024]{2,1,0:T(8,128)(2,1)S(1)}, bf16[2,32,1024]{2,1,0:T(8,128)(2,1)S(1)}, u32[]{:S(2)}, u32[]{:S(2)}) collective-permute-start(bf16[2,32,1024]{2,1,0:T(8,128)(2,1)S(1)} %get-tuple-element.182.refs_1_), channel_id=1, source_target_pairs={{0,3},{1,2},{2,1},{3,0},{4,7},{5,6},{6,5},{7,4},{8,11},{9,10},{10,... | collective-permute-start | bytes 393224 | tf_op jit(solution)/shard_map/ppermute | solution.py:327
  29.9 1.9 %collective-permute-start.7 = (bf16[2,32,1024]{2,1,0:T(8,128)(2,1)S(1)}, bf16[2,32,1024]{2,1,0:T(8,128)(2,1)S(1)}, u32[]{:S(2)}, u32[]{:S(2)}) collective-permute-start(bf16[2,32,1024]{2,1,0:T(8,128)(2,1)S(1)} %get-tuple-element.182.refs_1_), channel_id=1, source_target_pairs={{0,1},{1,0},{2,3},{3,2},{4,5},{5,4},{6,7},{7,6},{8,9},{9,8},{10,11... | collective-permute-start | bytes 393224 | tf_op jit(solution)/shard_map/ppermute | solution.py:327
  31.8 4.4 %collective-permute-done.4.refs_1_ = bf16[64,3584]{1,0:T(8,128)(2,1)S(1)} collective-permute-done((bf16[64,3584]{1,0:T(8,128)(2,1)S(1)}, bf16[64,3584]{1,0:T(8,128)(2,1)S(1)}, u32[]{:S(2)}, u32[]{:S(2)}) %collective-permute-start.4) | collective-permute-done | bytes 458784 | tf_op jit(solution)/shard_map/ppermute | solution.py:327
  36.3 2.3 %collective-permute-done.10.refs_1_ = bf16[64,3584]{1,0:T(8,128)(2,1)S(1)} collective-permute-done((bf16[64,3584]{1,0:T(8,128)(2,1)S(1)}, bf16[64,3584]{1,0:T(8,128)(2,1)S(1)}, u32[]{:S(2)}, u32[]{:S(2)}) %collective-permute-start.10) | collective-permute-done | bytes 458784 | tf_op jit(solution)/shard_map/ppermute | solution.py:327
  38.7 2.4 %collective-permute-done.8.refs_3_ = bf16[2,32,1024]{2,1,0:T(8,128)(2,1)S(1)} collective-permute-done((bf16[2,32,1024]{2,1,0:T(8,128)(2,1)S(1)}, bf16[2,32,1024]{2,1,0:T(8,128)(2,1)S(1)}, u32[]{:S(2)}, u32[]{:S(2)}) %collective-permute-start.8) | collective-permute-done | bytes 131104 | tf_op jit(solution)/shard_map/ppermute | solution.py:327
  41.9 2.1 %forward.6 = (f32[128,3584]{1,0:T(8,128)S(1)}, bf16[128,3584]{1,0:T(8,128)(2,1)S(1)}, f32[8,128]{1,0:T(8,128)S(1)}) custom-call(bf16[256,1024]{1,0:T(8,128)(2,1)S(1)} %get-tuple-element.112.refs_0_, bf16[1024,7168]{1,0:T(8,128)(2,1)S(1)} %get-tuple-element.94.refs_1_.refs_3_, f32[8,128]{1,0:T(8,128)S(1)} %get-tuple-element.113.refs_2_), custom_call_target="tpu_custom_call" | custom-call | flops 1 | bytes 1 | tf_op jit(solution)/shard_map/forward/pallas_call | solution.py:58
  44.1 2.1 %forward.7 = (f32[128,3584]{1,0:T(8,128)S(1)}, bf16[128,3584]{1,0:T(8,128)(2,1)S(1)}, f32[8,128]{1,0:T(8,128)S(1)}) custom-call(bf16[256,1024]{1,0:T(8,128)(2,1)S(1)} %get-tuple-element.112.refs_0_, bf16[1024,7168]{1,0:T(8,128)(2,1)S(1)} %get-tuple-element.94.refs_1_.refs_3_, f32[8,128]{1,0:T(8,128)S(1)} %get-tuple-element.114.refs_2_), custom_call_target="tpu_custom_call" | custom-call | flops 1 | bytes 1 | tf_op jit(solution)/shard_map/forward/pallas_call | solution.py:58
  47.3 1.6 %collective-permute-start.14 = (bf16[64,3584]{1,0:T(8,128)(2,1)S(1)}, bf16[64,3584]{1,0:T(8,128)(2,1)S(1)}, u32[]{:S(2)}, u32[]{:S(2)}) collective-permute-start(bf16[64,3584]{1,0:T(8,128)(2,1)S(1)} %get-tuple-element.128), channel_id=1, source_target_pairs={{0,8},{4,12},{8,0},{12,4},{16,24},{20,28},{24,16},{28,20},{1,9},{5... | collective-permute-start | bytes 1376264 | tf_op jit(solution)/shard_map/ppermute | solution.py:327
  51.4 3.8 %collective-permute-done.6.refs_1_ = bf16[32,3584]{1,0:T(8,128)(2,1)S(1)} collective-permute-done((bf16[32,3584]{1,0:T(8,128)(2,1)S(1)}, bf16[32,3584]{1,0:T(8,128)(2,1)S(1)}, u32[]{:S(2)}, u32[]{:S(2)}) %collective-permute-start.6) | collective-permute-done | bytes 229408 | tf_op jit(solution)/shard_map/ppermute | solution.py:327
  56.0 8.5 %collective-permute-done.13.refs_1_ = bf16[32,3584]{1,0:T(8,128)(2,1)S(1)} collective-permute-done((bf16[32,3584]{1,0:T(8,128)(2,1)S(1)}, bf16[32,3584]{1,0:T(8,128)(2,1)S(1)}, u32[]{:S(2)}, u32[]{:S(2)}) %collective-permute-start.13) | collective-permute-done | bytes 229408 | tf_op jit(solution)/shard_map/ppermute | solution.py:327
  64.9 1.6 %collective-permute-start.16 = (bf16[32,3584]{1,0:T(8,128)(2,1)S(1)}, bf16[32,3584]{1,0:T(8,128)(2,1)S(1)}, u32[]{:S(2)}, u32[]{:S(2)}) collective-permute-start(bf16[32,3584]{1,0:T(8,128)(2,1)S(1)} %get-tuple-element.132.refs_0_), channel_id=1, source_target_pairs={{0,8},{4,12},{8,0},{12,4},{16,24},{20,28},{24,16},{28,20},{1,9},{5... | collective-permute-start | bytes 688136 | tf_op jit(solution)/shard_map/ppermute | solution.py:327
  66.8 2.3 %collective-permute-done.17.refs_1_ = bf16[32,3584]{1,0:T(8,128)(2,1)S(1)} collective-permute-done((bf16[32,3584]{1,0:T(8,128)(2,1)S(1)}, bf16[32,3584]{1,0:T(8,128)(2,1)S(1)}, u32[]{:S(2)}, u32[]{:S(2)}) %collective-permute-start.17) | collective-permute-done | bytes 229408 | tf_op jit(solution)/shard_map/ppermute | solution.py:327
  71.8 3.1 %collective-permute-start.20 = (bf16[64,3584]{1,0:T(8,128)(2,1)S(1)}, bf16[64,3584]{1,0:T(8,128)(2,1)S(1)}, u32[]{:S(2)}, u32[]{:S(2)}) collective-permute-start(bf16[64,3584]{1,0:T(8,128)(2,1)S(1)} %get-tuple-element.145.refs_0_), channel_id=1, source_target_pairs={{0,16},{4,20},{8,24},{12,28},{16,0},{20,4},{24,8},{28,12},{1,17},{... | collective-permute-start | bytes 1376264 | tf_op jit(solution)/shard_map/ppermute | solution.py:327
  75.9 11.0 %collective-permute-done.15.refs_1_ = bf16[32,3584]{1,0:T(8,128)(2,1)S(1)} collective-permute-done((bf16[32,3584]{1,0:T(8,128)(2,1)S(1)}, bf16[32,3584]{1,0:T(8,128)(2,1)S(1)}, u32[]{:S(2)}, u32[]{:S(2)}) %collective-permute-start.15) | collective-permute-done | bytes 229408 | tf_op jit(solution)/shard_map/ppermute | solution.py:327
  88.5 1.7 %collective-permute-start.25 = (bf16[32,3584]{1,0:T(8,128)(2,1)S(1)}, bf16[32,3584]{1,0:T(8,128)(2,1)S(1)}, u32[]{:S(2)}, u32[]{:S(2)}) collective-permute-start(bf16[32,3584]{1,0:T(8,128)(2,1)S(1)} %get-tuple-element.152.refs_0_), channel_id=1, source_target_pairs={{0,16},{4,20},{8,24},{12,28},{16,0},{20,4},{24,8},{28,12},{1,17},{... | collective-permute-start | bytes 688136 | tf_op jit(solution)/shard_map/ppermute | solution.py:327
  91.3 4.8 %collective-permute-done.25.refs_1_ = bf16[32,3584]{1,0:T(8,128)(2,1)S(1)} collective-permute-done((bf16[32,3584]{1,0:T(8,128)(2,1)S(1)}, bf16[32,3584]{1,0:T(8,128)(2,1)S(1)}, u32[]{:S(2)}, u32[]{:S(2)}) %collective-permute-start.25) | collective-permute-done | bytes 229408 | tf_op jit(solution)/shard_map/ppermute | solution.py:327
  96.1 1.6 %collective-permute-start.30 = (bf16[64,3584]{1,0:T(8,128)(2,1)S(1)}, bf16[64,3584]{1,0:T(8,128)(2,1)S(1)}, u32[]{:S(2)}, u32[]{:S(2)}) collective-permute-start(bf16[64,3584]{1,0:T(8,128)(2,1)S(1)} %get-tuple-element.163.refs_0_), channel_id=1, source_target_pairs={{0,8},{4,12},{8,0},{12,4},{16,24},{20,28},{24,16},{28,20},{1,9},{5... | collective-permute-start | bytes 1376264 | tf_op jit(solution)/shard_map/ppermute | solution.py:327
  99.1 2.9 %input_partial.4 = (f32[1024,256]{1,0:T(8,128)S(1)}, f32[8,128]{1,0:T(8,128)S(1)}) custom-call(s32[8]{0:T(128)S(1)} %shift-right-arithmetic_add_fusion.refs_0_, bf16[128,3584]{1,0:T(8,128)(2,1)S(1)} %get-tuple-element.150.refs_1_.refs_3_, bf16[128,3584]{1,0:T(8,128)(2,1)S(1)} %collective-permute-done.23.refs_2_.refs_4_, ...), custom_call_target="tpu_custom_call" | custom-call | flops 1 | bytes 1 | tf_op jit(solution)/shard_map/input_partial/pallas_call | solution.py:58
  101.9 2.9 %input_partial.5 = (f32[64,1024]{1,0:T(8,128)S(1)}, bf16[64,1024]{1,0:T(8,128)(2,1)S(1)}, bf16[64,1024]{1,0:T(8,128)(2,1)S(1)}, bf16[64,1024]{1,0:T(8,128)(2,1)S(1)}, f32[8,128]{1,0:T(8,128)S(1)}) custom-call(s32[8]{0:T(128)S(1)} %shift-right-arithmetic_add_fusion.refs_0_, bf16[128,3584]{1,0:T(8,128)(2,1)S(1)} %get-tuple-element.149.refs_1_.refs_3_, ...), custom_call_target="tpu_custom_call" | custom-call | flops 1 | bytes 1 | tf_op jit(solution)/shard_map/input_partial/pallas_call | solution.py:58
  104.9 3.0 %collective-permute-done.30.refs_1_ = bf16[64,3584]{1,0:T(8,128)(2,1)S(1)} collective-permute-done((bf16[64,3584]{1,0:T(8,128)(2,1)S(1)}, bf16[64,3584]{1,0:T(8,128)(2,1)S(1)}, u32[]{:S(2)}, u32[]{:S(2)}) %collective-permute-start.30) | collective-permute-done | bytes 458784 | tf_op jit(solution)/shard_map/ppermute | solution.py:327
  109.4 2.9 %collective-permute-start.27 = (bf16[64,1024]{1,0:T(8,128)(2,1)S(1)}, bf16[64,1024]{1,0:T(8,128)(2,1)S(1)}, u32[]{:S(2)}, u32[]{:S(2)}) collective-permute-start(bf16[64,1024]{1,0:T(8,128)(2,1)S(1)} %get-tuple-element.160), channel_id=1, source_target_pairs={{0,2},{1,3},{2,0},{3,1},{4,6},{5,7},{6,4},{7,5},{8,10},{9,11},{10,... | collective-permute-start | bytes 393224 | tf_op jit(solution)/shard_map/ppermute | solution.py:327
  114.8 2.7 %input_partial.6 = (f32[1024,256]{1,0:T(8,128)S(1)}, f32[8,128]{1,0:T(8,128)S(1)}) custom-call(s32[8]{0:T(128)S(1)} %shift-right-arithmetic_add_fusion.refs_0_, bf16[128,3584]{1,0:T(8,128)(2,1)S(1)} %get-tuple-element.167.refs_1_.refs_5_, bf16[128,3584]{1,0:T(8,128)(2,1)S(1)} %collective-permute-done.32.refs_2_.refs_6_, ...), custom_call_target="tpu_custom_call" | custom-call | flops 1 | bytes 1 | tf_op jit(solution)/shard_map/input_partial/pallas_call | solution.py:58
  117.4 2.9 %input_partial.7 = (f32[64,1024]{1,0:T(8,128)S(1)}, bf16[64,1024]{1,0:T(8,128)(2,1)S(1)}, bf16[64,1024]{1,0:T(8,128)(2,1)S(1)}, bf16[64,1024]{1,0:T(8,128)(2,1)S(1)}, f32[8,128]{1,0:T(8,128)S(1)}) custom-call(s32[8]{0:T(128)S(1)} %shift-right-arithmetic_add_fusion.refs_0_, bf16[128,3584]{1,0:T(8,128)(2,1)S(1)} %get-tuple-element.166.refs_1_.refs_5_, ...), custom_call_target="tpu_custom_call" | custom-call | flops 1 | bytes 1 | tf_op jit(solution)/shard_map/input_partial/pallas_call | solution.py:58
  120.4 2.9 %collective-permute-start.34 = (bf16[64,1024]{1,0:T(8,128)(2,1)S(1)}, bf16[64,1024]{1,0:T(8,128)(2,1)S(1)}, u32[]{:S(2)}, u32[]{:S(2)}) collective-permute-start(bf16[64,1024]{1,0:T(8,128)(2,1)S(1)} %get-tuple-element.173), channel_id=1, source_target_pairs={{0,2},{1,3},{2,0},{3,1},{4,6},{5,7},{6,4},{7,5},{8,10},{9,11},{10,... | collective-permute-start | bytes 393224 | tf_op jit(solution)/shard_map/ppermute | solution.py:327
  124.9 5.6 %weight_gradient.2 = (bf16[1,1,448,128,128]{4,3,2,1,0:T(8,128)(2,1)}, f32[8,128]{1,0:T(8,128)S(1)}) custom-call(s32[448]{0:T(512)S(1)} %select_reduce_fusion.refs_0_, bf16[1024,256]{1,0:T(8,128)(2,1)S(1)} %get-tuple-element.175.refs_1_, bf16[1024,256]{1,0:T(8,128)(2,1)S(1)} %get-tuple-element.176.refs_2_, ...), custom_call_target="tpu_custom_call" | custom-call | flops 1 | bytes 1 | tf_op jit(solution)/shard_map/weight_gradient/pallas_call | solution.py:58
  130.5 6.2 %weight_gradient.3 = (bf16[1,1,448,128,128]{4,3,2,1,0:T(8,128)(2,1)}, f32[8,128]{1,0:T(8,128)}) custom-call(s32[448]{0:T(512)S(1)} %select_reduce_fusion.refs_0_, bf16[1024,256]{1,0:T(8,128)(2,1)S(1)} %get-tuple-element.175.refs_1_, bf16[1024,256]{1,0:T(8,128)(2,1)S(1)} %get-tuple-element.176.refs_2_, ...), custom_call_target="tpu_custom_call", output_to_operand_aliasing={{0}: (7, {})} | custom-call | flops 1 | bytes 1 | tf_op jit(solution)/shard_map/weight_gradient/pallas_call | solution.py:58
  (88 shorter events, 26.4 us)
Async XLA Ops:
  1.6 14.8 %collective-permute-start.2 = (bf16[2,32,1024]{2,1,0:T(8,128)(2,1)S(1)}, bf16[2,32,1024]{2,1,0:T(8,128)(2,1)S(1)}, u32[]{:S(2)}, u32[]{:S(2)}) collective-permute-start(bf16[2,32,1024]{2,1,0:T(8,128)(2,1)S(1)} %get-tuple-element.181.refs_1_), channel_id=1, source_target_pairs={{0,3},{1,2},{2,1},{3,0},{4,7},{5,6},{6,5},{7,4},{8,11},{9,10},{10,... | collective-permute-start | bytes 393224 | tf_op jit(solution)/shard_map/ppermute | solution.py:327
  6.7 11.1 %collective-permute-start.1 = (bf16[2,32,1024]{2,1,0:T(8,128)(2,1)S(1)}, bf16[2,32,1024]{2,1,0:T(8,128)(2,1)S(1)}, u32[]{:S(2)}, u32[]{:S(2)}) collective-permute-start(bf16[2,32,1024]{2,1,0:T(8,128)(2,1)S(1)} %get-tuple-element.181.refs_1_), channel_id=1, source_target_pairs={{0,2},{1,3},{2,0},{3,1},{4,6},{5,7},{6,4},{7,5},{8,10},{9,11},{10,... | collective-permute-start | bytes 393224 | tf_op jit(solution)/shard_map/ppermute | solution.py:327
  6.7 11.1 %collective-permute-start = (bf16[2,32,1024]{2,1,0:T(8,128)(2,1)S(1)}, bf16[2,32,1024]{2,1,0:T(8,128)(2,1)S(1)}, u32[]{:S(2)}, u32[]{:S(2)}) collective-permute-start(bf16[2,32,1024]{2,1,0:T(8,128)(2,1)S(1)} %get-tuple-element.181.refs_1_), channel_id=1, source_target_pairs={{0,1},{1,0},{2,3},{3,2},{4,5},{5,4},{6,7},{7,6},{8,9},{9,8},{10,11... | collective-permute-start | bytes 393224 | tf_op jit(solution)/shard_map/ppermute | solution.py:327
  23.7 12.5 %collective-permute-start.4 = (bf16[64,3584]{1,0:T(8,128)(2,1)S(1)}, bf16[64,3584]{1,0:T(8,128)(2,1)S(1)}, u32[]{:S(2)}, u32[]{:S(2)}) collective-permute-start(bf16[64,3584]{1,0:T(8,128)(2,1)S(1)} %get-tuple-element.101), channel_id=1, source_target_pairs={{0,8},{4,12},{8,0},{12,4},{16,24},{20,28},{24,16},{28,20},{1,9},{5... | collective-permute-start | bytes 1376264 | tf_op jit(solution)/shard_map/ppermute | solution.py:327
  25.8 12.9 %collective-permute-start.10 = (bf16[64,3584]{1,0:T(8,128)(2,1)S(1)}, bf16[64,3584]{1,0:T(8,128)(2,1)S(1)}, u32[]{:S(2)}, u32[]{:S(2)}) collective-permute-start(bf16[64,3584]{1,0:T(8,128)(2,1)S(1)} %get-tuple-element.109), channel_id=1, source_target_pairs={{0,16},{4,20},{8,24},{12,28},{16,0},{20,4},{24,8},{28,12},{1,17},{... | collective-permute-start | bytes 1376264 | tf_op jit(solution)/shard_map/ppermute | solution.py:327
  27.4 11.3 %collective-permute-start.9 = (bf16[2,32,1024]{2,1,0:T(8,128)(2,1)S(1)}, bf16[2,32,1024]{2,1,0:T(8,128)(2,1)S(1)}, u32[]{:S(2)}, u32[]{:S(2)}) collective-permute-start(bf16[2,32,1024]{2,1,0:T(8,128)(2,1)S(1)} %get-tuple-element.182.refs_1_), channel_id=1, source_target_pairs={{0,3},{1,2},{2,1},{3,0},{4,7},{5,6},{6,5},{7,4},{8,11},{9,10},{10,... | collective-permute-start | bytes 393224 | tf_op jit(solution)/shard_map/ppermute | solution.py:327
  29.9 11.2 %collective-permute-start.8 = (bf16[2,32,1024]{2,1,0:T(8,128)(2,1)S(1)}, bf16[2,32,1024]{2,1,0:T(8,128)(2,1)S(1)}, u32[]{:S(2)}, u32[]{:S(2)}) collective-permute-start(bf16[2,32,1024]{2,1,0:T(8,128)(2,1)S(1)} %get-tuple-element.182.refs_1_), channel_id=1, source_target_pairs={{0,2},{1,3},{2,0},{3,1},{4,6},{5,7},{6,4},{7,5},{8,10},{9,11},{10,... | collective-permute-start | bytes 393224 | tf_op jit(solution)/shard_map/ppermute | solution.py:327
  29.9 11.2 %collective-permute-start.7 = (bf16[2,32,1024]{2,1,0:T(8,128)(2,1)S(1)}, bf16[2,32,1024]{2,1,0:T(8,128)(2,1)S(1)}, u32[]{:S(2)}, u32[]{:S(2)}) collective-permute-start(bf16[2,32,1024]{2,1,0:T(8,128)(2,1)S(1)} %get-tuple-element.182.refs_1_), channel_id=1, source_target_pairs={{0,1},{1,0},{2,3},{3,2},{4,5},{5,4},{6,7},{7,6},{8,9},{9,8},{10,11... | collective-permute-start | bytes 393224 | tf_op jit(solution)/shard_map/ppermute | solution.py:327
  46.7 8.5 %collective-permute-start.6 = (bf16[32,3584]{1,0:T(8,128)(2,1)S(1)}, bf16[32,3584]{1,0:T(8,128)(2,1)S(1)}, u32[]{:S(2)}, u32[]{:S(2)}) collective-permute-start(bf16[32,3584]{1,0:T(8,128)(2,1)S(1)} %get-tuple-element.107), channel_id=1, source_target_pairs={{0,16},{4,20},{8,24},{12,28},{16,0},{20,4},{24,8},{28,12},{1,17},{... | collective-permute-start | bytes 688136 | tf_op jit(solution)/shard_map/ppermute | solution.py:327
  47.3 19.2 %collective-permute-start.14 = (bf16[64,3584]{1,0:T(8,128)(2,1)S(1)}, bf16[64,3584]{1,0:T(8,128)(2,1)S(1)}, u32[]{:S(2)}, u32[]{:S(2)}) collective-permute-start(bf16[64,3584]{1,0:T(8,128)(2,1)S(1)} %get-tuple-element.128), channel_id=1, source_target_pairs={{0,8},{4,12},{8,0},{12,4},{16,24},{20,28},{24,16},{28,20},{1,9},{5... | collective-permute-start | bytes 1376264 | tf_op jit(solution)/shard_map/ppermute | solution.py:327
  49.2 17.5 %collective-permute-start.18 = (bf16[64,3584]{1,0:T(8,128)(2,1)S(1)}, bf16[64,3584]{1,0:T(8,128)(2,1)S(1)}, u32[]{:S(2)}, u32[]{:S(2)}) collective-permute-start(bf16[64,3584]{1,0:T(8,128)(2,1)S(1)} %get-tuple-element.135), channel_id=1, source_target_pairs={{0,16},{4,20},{8,24},{12,28},{16,0},{20,4},{24,8},{28,12},{1,17},{... | collective-permute-start | bytes 1376264 | tf_op jit(solution)/shard_map/ppermute | solution.py:327
  50.5 14.1 %collective-permute-start.13 = (bf16[32,3584]{1,0:T(8,128)(2,1)S(1)}, bf16[32,3584]{1,0:T(8,128)(2,1)S(1)}, u32[]{:S(2)}, u32[]{:S(2)}) collective-permute-start(bf16[32,3584]{1,0:T(8,128)(2,1)S(1)} %get-tuple-element.124), channel_id=1, source_target_pairs={{0,8},{4,12},{8,0},{12,4},{16,24},{20,28},{24,16},{28,20},{1,9},{5... | collective-permute-start | bytes 688136 | tf_op jit(solution)/shard_map/ppermute | solution.py:327
  55.6 13.5 %collective-permute-start.17 = (bf16[32,3584]{1,0:T(8,128)(2,1)S(1)}, bf16[32,3584]{1,0:T(8,128)(2,1)S(1)}, u32[]{:S(2)}, u32[]{:S(2)}) collective-permute-start(bf16[32,3584]{1,0:T(8,128)(2,1)S(1)} %get-tuple-element.133.refs_0_), channel_id=1, source_target_pairs={{0,16},{4,20},{8,24},{12,28},{16,0},{20,4},{24,8},{28,12},{1,17},{... | collective-permute-start | bytes 688136 | tf_op jit(solution)/shard_map/ppermute | solution.py:327
  64.9 6.9 %collective-permute-start.16 = (bf16[32,3584]{1,0:T(8,128)(2,1)S(1)}, bf16[32,3584]{1,0:T(8,128)(2,1)S(1)}, u32[]{:S(2)}, u32[]{:S(2)}) collective-permute-start(bf16[32,3584]{1,0:T(8,128)(2,1)S(1)} %get-tuple-element.132.refs_0_), channel_id=1, source_target_pairs={{0,8},{4,12},{8,0},{12,4},{16,24},{20,28},{24,16},{28,20},{1,9},{5... | collective-permute-start | bytes 688136 | tf_op jit(solution)/shard_map/ppermute | solution.py:327
  69.1 18.6 %collective-permute-start.21 = (bf16[64,3584]{1,0:T(8,128)(2,1)S(1)}, bf16[64,3584]{1,0:T(8,128)(2,1)S(1)}, u32[]{:S(2)}, u32[]{:S(2)}) collective-permute-start(bf16[64,3584]{1,0:T(8,128)(2,1)S(1)} %get-tuple-element.146.refs_0_), channel_id=1, source_target_pairs={{0,8},{4,12},{8,0},{12,4},{16,24},{20,28},{24,16},{28,20},{1,9},{5... | collective-permute-start | bytes 1376264 | tf_op jit(solution)/shard_map/ppermute | solution.py:327
  71.8 16.0 %collective-permute-start.20 = (bf16[64,3584]{1,0:T(8,128)(2,1)S(1)}, bf16[64,3584]{1,0:T(8,128)(2,1)S(1)}, u32[]{:S(2)}, u32[]{:S(2)}) collective-permute-start(bf16[64,3584]{1,0:T(8,128)(2,1)S(1)} %get-tuple-element.145.refs_0_), channel_id=1, source_target_pairs={{0,16},{4,20},{8,24},{12,28},{16,0},{20,4},{24,8},{28,12},{1,17},{... | collective-permute-start | bytes 1376264 | tf_op jit(solution)/shard_map/ppermute | solution.py:327
  74.9 12.0 %collective-permute-start.15 = (bf16[32,3584]{1,0:T(8,128)(2,1)S(1)}, bf16[32,3584]{1,0:T(8,128)(2,1)S(1)}, u32[]{:S(2)}, u32[]{:S(2)}) collective-permute-start(bf16[32,3584]{1,0:T(8,128)(2,1)S(1)} %get-tuple-element.131), channel_id=1, source_target_pairs={{0,16},{4,20},{8,24},{12,28},{16,0},{20,4},{24,8},{28,12},{1,17},{... | collective-permute-start | bytes 688136 | tf_op jit(solution)/shard_map/ppermute | solution.py:327
  75.0 12.3 %collective-permute-start.19 = (bf16[32,3584]{1,0:T(8,128)(2,1)S(1)}, bf16[32,3584]{1,0:T(8,128)(2,1)S(1)}, u32[]{:S(2)}, u32[]{:S(2)}) collective-permute-start(bf16[32,3584]{1,0:T(8,128)(2,1)S(1)} %get-tuple-element.142), channel_id=1, source_target_pairs={{0,8},{4,12},{8,0},{12,4},{16,24},{20,28},{24,16},{28,20},{1,9},{5... | collective-permute-start | bytes 688136 | tf_op jit(solution)/shard_map/ppermute | solution.py:327
  87.8 11.3 %collective-permute-start.23 = (bf16[128,3584]{1,0:T(8,128)(2,1)S(1)}, bf16[128,3584]{1,0:T(8,128)(2,1)S(1)}, u32[]{:S(2)}, u32[]{:S(2)}) collective-permute-start(bf16[128,3584]{1,0:T(8,128)(2,1)S(1)} %get-tuple-element.150.refs_1_.refs_3_), channel_id=1, source_target_pairs={{0,4},{4,0},{8,12},{12,8},{16,20},{20,16},{24,28},{28,24},{1,5},{5... | collective-permute-start | bytes 2752520 | tf_op jit(solution)/shard_map/ppermute | solution.py:327
  87.9 14.0 %collective-permute-start.22 = (bf16[128,3584]{1,0:T(8,128)(2,1)S(1)}, bf16[128,3584]{1,0:T(8,128)(2,1)S(1)}, u32[]{:S(2)}, u32[]{:S(2)}) collective-permute-start(bf16[128,3584]{1,0:T(8,128)(2,1)S(1)} %get-tuple-element.149.refs_1_.refs_3_), channel_id=1, source_target_pairs={{0,4},{4,0},{8,12},{12,8},{16,20},{20,16},{24,28},{28,24},{1,5},{5... | collective-permute-start | bytes 2752520 | tf_op jit(solution)/shard_map/ppermute | solution.py:327
  88.5 7.6 %collective-permute-start.25 = (bf16[32,3584]{1,0:T(8,128)(2,1)S(1)}, bf16[32,3584]{1,0:T(8,128)(2,1)S(1)}, u32[]{:S(2)}, u32[]{:S(2)}) collective-permute-start(bf16[32,3584]{1,0:T(8,128)(2,1)S(1)} %get-tuple-element.152.refs_0_), channel_id=1, source_target_pairs={{0,16},{4,20},{8,24},{12,28},{16,0},{20,4},{24,8},{28,12},{1,17},{... | collective-permute-start | bytes 688136 | tf_op jit(solution)/shard_map/ppermute | solution.py:327
  90.1 7.6 %collective-permute-start.24 = (bf16[32,3584]{1,0:T(8,128)(2,1)S(1)}, bf16[32,3584]{1,0:T(8,128)(2,1)S(1)}, u32[]{:S(2)}, u32[]{:S(2)}) collective-permute-start(bf16[32,3584]{1,0:T(8,128)(2,1)S(1)} %get-tuple-element.151.refs_0_), channel_id=1, source_target_pairs={{0,8},{4,12},{8,0},{12,4},{16,24},{20,28},{24,16},{28,20},{1,9},{5... | collective-permute-start | bytes 688136 | tf_op jit(solution)/shard_map/ppermute | solution.py:327
  96.1 11.7 %collective-permute-start.30 = (bf16[64,3584]{1,0:T(8,128)(2,1)S(1)}, bf16[64,3584]{1,0:T(8,128)(2,1)S(1)}, u32[]{:S(2)}, u32[]{:S(2)}) collective-permute-start(bf16[64,3584]{1,0:T(8,128)(2,1)S(1)} %get-tuple-element.163.refs_0_), channel_id=1, source_target_pairs={{0,8},{4,12},{8,0},{12,4},{16,24},{20,28},{24,16},{28,20},{1,9},{5... | collective-permute-start | bytes 1376264 | tf_op jit(solution)/shard_map/ppermute | solution.py:327
  97.7 11.4 %collective-permute-start.29 = (bf16[64,3584]{1,0:T(8,128)(2,1)S(1)}, bf16[64,3584]{1,0:T(8,128)(2,1)S(1)}, u32[]{:S(2)}, u32[]{:S(2)}) collective-permute-start(bf16[64,3584]{1,0:T(8,128)(2,1)S(1)} %get-tuple-element.162.refs_0_), channel_id=1, source_target_pairs={{0,16},{4,20},{8,24},{12,28},{16,0},{20,4},{24,8},{28,12},{1,17},{... | collective-permute-start | bytes 1376264 | tf_op jit(solution)/shard_map/ppermute | solution.py:327
  107.9 6.9 %collective-permute-start.32 = (bf16[128,3584]{1,0:T(8,128)(2,1)S(1)}, bf16[128,3584]{1,0:T(8,128)(2,1)S(1)}, u32[]{:S(2)}, u32[]{:S(2)}) collective-permute-start(bf16[128,3584]{1,0:T(8,128)(2,1)S(1)} %get-tuple-element.167.refs_1_.refs_5_), channel_id=1, source_target_pairs={{0,4},{4,0},{8,12},{12,8},{16,20},{20,16},{24,28},{28,24},{1,5},{5... | collective-permute-start | bytes 2752520 | tf_op jit(solution)/shard_map/ppermute | solution.py:327
  109.3 8.2 %collective-permute-start.31 = (bf16[128,3584]{1,0:T(8,128)(2,1)S(1)}, bf16[128,3584]{1,0:T(8,128)(2,1)S(1)}, u32[]{:S(2)}, u32[]{:S(2)}) collective-permute-start(bf16[128,3584]{1,0:T(8,128)(2,1)S(1)} %get-tuple-element.166.refs_1_.refs_5_), channel_id=1, source_target_pairs={{0,4},{4,0},{8,12},{12,8},{16,20},{20,16},{24,28},{28,24},{1,5},{5... | collective-permute-start | bytes 2752520 | tf_op jit(solution)/shard_map/ppermute | solution.py:327
  109.3 14.0 %collective-permute-start.26 = (bf16[64,1024]{1,0:T(8,128)(2,1)S(1)}, bf16[64,1024]{1,0:T(8,128)(2,1)S(1)}, u32[]{:S(2)}, u32[]{:S(2)}) collective-permute-start(bf16[64,1024]{1,0:T(8,128)(2,1)S(1)} %get-tuple-element.159), channel_id=1, source_target_pairs={{0,1},{1,0},{2,3},{3,2},{4,5},{5,4},{6,7},{7,6},{8,9},{9,8},{10,11... | collective-permute-start | bytes 393224 | tf_op jit(solution)/shard_map/ppermute | solution.py:327
  109.4 15.4 %collective-permute-start.27 = (bf16[64,1024]{1,0:T(8,128)(2,1)S(1)}, bf16[64,1024]{1,0:T(8,128)(2,1)S(1)}, u32[]{:S(2)}, u32[]{:S(2)}) collective-permute-start(bf16[64,1024]{1,0:T(8,128)(2,1)S(1)} %get-tuple-element.160), channel_id=1, source_target_pairs={{0,2},{1,3},{2,0},{3,1},{4,6},{5,7},{6,4},{7,5},{8,10},{9,11},{10,... | collective-permute-start | bytes 393224 | tf_op jit(solution)/shard_map/ppermute | solution.py:327
  112.3 12.5 %collective-permute-start.28 = (bf16[64,1024]{1,0:T(8,128)(2,1)S(1)}, bf16[64,1024]{1,0:T(8,128)(2,1)S(1)}, u32[]{:S(2)}, u32[]{:S(2)}) collective-permute-start(bf16[64,1024]{1,0:T(8,128)(2,1)S(1)} %get-tuple-element.161), channel_id=1, source_target_pairs={{0,3},{1,2},{2,1},{3,0},{4,7},{5,6},{6,5},{7,4},{8,11},{9,10},{10,... | collective-permute-start | bytes 393224 | tf_op jit(solution)/shard_map/ppermute | solution.py:327
  120.4 16.3 %collective-permute-start.33 = (bf16[64,1024]{1,0:T(8,128)(2,1)S(1)}, bf16[64,1024]{1,0:T(8,128)(2,1)S(1)}, u32[]{:S(2)}, u32[]{:S(2)}) collective-permute-start(bf16[64,1024]{1,0:T(8,128)(2,1)S(1)} %get-tuple-element.172), channel_id=1, source_target_pairs={{0,1},{1,0},{2,3},{3,2},{4,5},{5,4},{6,7},{7,6},{8,9},{9,8},{10,11... | collective-permute-start | bytes 393224 | tf_op jit(solution)/shard_map/ppermute | solution.py:327
  120.4 16.3 %collective-permute-start.34 = (bf16[64,1024]{1,0:T(8,128)(2,1)S(1)}, bf16[64,1024]{1,0:T(8,128)(2,1)S(1)}, u32[]{:S(2)}, u32[]{:S(2)}) collective-permute-start(bf16[64,1024]{1,0:T(8,128)(2,1)S(1)} %get-tuple-element.173), channel_id=1, source_target_pairs={{0,2},{1,3},{2,0},{3,1},{4,6},{5,7},{6,4},{7,5},{8,10},{9,11},{10,... | collective-permute-start | bytes 393224 | tf_op jit(solution)/shard_map/ppermute | solution.py:327
  123.4 13.4 %collective-permute-start.35 = (bf16[64,1024]{1,0:T(8,128)(2,1)S(1)}, bf16[64,1024]{1,0:T(8,128)(2,1)S(1)}, u32[]{:S(2)}, u32[]{:S(2)}) collective-permute-start(bf16[64,1024]{1,0:T(8,128)(2,1)S(1)} %get-tuple-element.174), channel_id=1, source_target_pairs={{0,3},{1,2},{2,1},{3,0},{4,7},{5,6},{6,5},{7,4},{8,11},{9,10},{10,... | collective-permute-start | bytes 393224 | tf_op jit(solution)/shard_map/ppermute | solution.py:327
  (6 other events, 26.6 us)
where the time goes:
time: 138 us
  waiting for transfers between devices  47 us (34%)
  Pallas kernels  43.7 us (32%)
  starting transfers between devices  41.4 us (30%)
  other arithmetic  2.05 us (1%)
  local copies, waits for them, and re-layouts  1.72 us (1%)
  between operations  1.69 us (1%)
    ppermute x36, waiting for transfers between devices, swap(): return lax.ppermute(array, axis, [(i, i ^ bit) for i in range(size)])  47 us
    pallas_call x33, Pallas kernels, __call__(): pl.pallas_call(body, out_shape=[*out_shape, pltpu.VMEM((8, 128), jnp.floa...  43.7 us
    ppermute x36, starting transfers between devices, swap(): return lax.ppermute(array, axis, [(i, i ^ bit) for i in range(size)])  41.4 us
  transfers between devices with their start and end apart: 36, of which 13 were waited for; matrix products, arithmetic and copies ran while one was open for 1% of the time, Pallas kernels for 28%

commit v1 on v0

--- a/solution.py
+++ b/solution.py
@@ -10,7 +10,7 @@
 
 gelu_scale = 0.7978845608
 gelu_cubic = 0.044715
-token_parts = 2
+token_split = (3, 1)
 column_parts = 2
 vmem_limit = 16 * 1024 * 1024
 in_vmem = pl.BlockSpec(memory_space=pltpu.VMEM)
@@ -339,8 +339,11 @@
     row_me = lax.axis_index("row")
     col_me = lax.axis_index("col")
     col_groups = tokens.shape[0] // row_tokens
-    parts = group_of(max(1, row_tokens // 16), token_parts)
-    rows = row_tokens // parts
+    tiles = row_tokens // 16
+    shares = token_split if tiles % sum(token_split) == 0 else (1,)
+    sizes = [16 * (tiles // sum(shares)) * share for share in shares]
+    starts = [sum(sizes[:k]) for k in range(len(sizes))]
+    parts = len(sizes)
     slabs = group_of(col_blocks, column_parts)
     width = hidden_here // slabs
     direct = n_col <= 8
@@ -358,15 +361,13 @@
     distance = jnp.asarray(everyone.astype(np.int32)) ^ apart
     place = ((distance & 1) * (n_row // 2) + (distance >> 1)).astype(jnp.int32)
 
-    mine = tokens.reshape(col_groups, parts, rows, tall)
     pieces = []
-    for k in range(parts):
+    for start, rows in zip(starts, sizes):
+        mine = tokens.reshape(col_groups, row_tokens, tall)[:, start : start + rows]
         if direct:
-            pieces.append(
-                [mine[:, k]] + [swap(mine[:, k], "col", n_col, m) for m in range(1, n_col)]
-            )
+            pieces.append([mine] + [swap(mine, "col", n_col, m) for m in range(1, n_col)])
         else:
-            pieces.append([lax.all_gather(mine[:, k], "col", axis=0, tiled=True)])
+            pieces.append([lax.all_gather(mine, "col", axis=0, tiled=True)])
     weight = dense_tile(core, w_packed, code, row_blocks, col_blocks)
 
     far_bits = [1 << b for b in range(1, n_row.bit_length() - 1)]
@@ -388,7 +389,7 @@
         state[k, c] = (keep, swap(send, "row", n_row, path[at]))
 
     def bend(k, c, path):
-        activations[k, c], near = gelu(core, *state[k, c], grad_act, k * rows, c * width)
+        activations[k, c], near = gelu(core, *state[k, c], grad_act, starts[k], c * width)
         state[k, c] = (near, swap(near, "row", n_row, ([1] + path)[-1]))
 
     def join(at, k, c, path):
@@ -408,19 +409,19 @@
             for m in range(1, n_col):
                 total = total + swap(found[m], "col", n_col, m).astype(jnp.float32)
         elif last:
-            total = found[0].reshape(n_col, col_groups * rows, tall)
+            total = found[0].reshape(n_col, col_groups * sizes[k], tall)
             total = lax.psum_scatter(total, "col", scatter_dimension=0, tiled=True)[0]
         if last:
             total = total.astype(jnp.bfloat16)
-            input_grads[k] = total.reshape(col_groups, 1, rows, tall)
+            input_grads[k] = total.reshape(col_groups, sizes[k], tall)
 
     hops = len(far_bits)
     stages = [begin] + [functools.partial(add, at) for at in range(hops)] + [bend]
     stages += [functools.partial(join, at) for at in reversed(range(hops))] + [finish]
     plan = []
     if parts == 2 and hops == 2:
-        plan = [(0, 0), (0, 1), (0, 2), (1, 0), (1, 1), (0, 3), (1, 2), (0, 4), (1, 3)]
-        plan += [(0, 5), (1, 4), (0, 6), (1, 5), (1, 6)]
+        plan = [(0, 0), (0, 1), (1, 0), (1, 1), (0, 2), (1, 2), (0, 3), (1, 3), (0, 4), (1, 4)]
+        plan += [(0, 5), (0, 6), (1, 5), (1, 6)]
     else:
         plan = [(k, at) for at in range(len(stages)) for k in range(parts)]
     for k, at in plan:

time: 138 us -> 149 us (1.080); the launches traced: 138 us -> 146 us
  waiting for transfers between devices: 47 us -> 53 us
  Pallas kernels: 43.7 us -> 48.3 us
  starting transfers between devices: 41.4 us -> 38.8 us
    ppermute x36, waiting for transfers between devices: 47 us -> 53 us  [swap(): return lax.ppermute(array, axis, [(i, i ^ bit) for i in range(size)])]
    pallas_call x33, Pallas kernels: 43.7 us -> 48.3 us  [__call__(): pl.pallas_call(body, out_shape=[*out_shape, pltpu.VMEM((8, 128), jnp.floa...]
    ppermute x36, starting transfers between devices: 41.4 us -> 38.8 us  [swap(): return lax.ppermute(array, axis, [(i, i ^ bit) for i in range(size)])]
    slice x0 -> x2, local copies, waits for them, and re-layouts: none -> 1.79 us  [on_device(): mine = tokens.reshape(col_groups, row_tokens, tall)[:, start:start + rows]]
  transfers between devices with their start and end apart: 36 -> 36, of which waited for: 13 -> 13; matrix products, arithmetic and copies ran while one was open for 1% -> 2% of each run, Pallas kernels for 28% -> 30%
where the time goes in v1:
time: 149 us; the launch traced here: 146 us
  waiting for transfers between devices  53 us (36%)
  Pallas kernels  48.3 us (32%)
  starting transfers between devices  38.8 us (26%)
  other arithmetic  2.75 us (2%)
  local copies, waits for them, and re-layouts  1.8 us (1%)
  between operations  1.7 us (1%)
    ppermute x36, waiting for transfers between devices, swap(): return lax.ppermute(array, axis, [(i, i ^ bit) for i in range(size)])  53 us
    pallas_call x33, Pallas kernels, __call__(): pl.pallas_call(body, out_shape=[*out_shape, pltpu.VMEM((8, 128), jnp.floa...  48.3 us
    ppermute x36, starting transfers between devices, swap(): return lax.ppermute(array, axis, [(i, i ^ bit) for i in range(size)])  38.8 us
  transfers between devices with their start and end apart: 36, of which 13 were waited for; matrix products, arithmetic and copies ran while one was open for 2% of the time, Pallas kernels for 30%

profile of v1, /device:TPU:0, one launch (start us, length us, event | category | flops | bytes accessed | tf_op | source)
XLA Modules:
  0.0 146.4 jit_solution(1646426762016953937)
XLA Ops:
  1.6 5.1 %collective-permute-start.2 = (bf16[2,48,1024]{2,1,0:T(8,128)(2,1)S(1)}, bf16[2,48,1024]{2,1,0:T(8,128)(2,1)S(1)}, u32[]{:S(2)}, u32[]{:S(2)}) collective-permute-start(bf16[2,48,1024]{2,1,0:T(8,128)(2,1)S(1)} %slice.8.refs_1_), channel_id=1, source_target_pairs={{0,3},{1,2},{2,1},{3,0},{4,7},{5,6},{6,5},{7,4},{8,11},{9,10},{10,... | collective-permute-start | bytes 589832 | tf_op jit(solution)/shard_map/ppermute | solution.py:327
  8.9 7.7 %dense_tile.1 = (bf16[1024,7168]{1,0:T(8,128)(2,1)S(1)}, f32[8,128]{1,0:T(8,128)S(1)}) custom-call(s32[448]{0:T(512)S(1)} %select_reduce_fusion.refs_0_, bf16[1,1,448,128,128]{4,3,2,1,0:T(8,128)(2,1)} %refs_1_.1), custom_call_target="tpu_custom_call" | custom-call | flops 1 | bytes 1 | tf_op jit(solution)/shard_map/dense_tile/pallas_call | solution.py:58
  16.7 6.7 %collective-permute-done.1.refs_3_ = bf16[2,48,1024]{2,1,0:T(8,128)(2,1)S(1)} collective-permute-done((bf16[2,48,1024]{2,1,0:T(8,128)(2,1)S(1)}, bf16[2,48,1024]{2,1,0:T(8,128)(2,1)S(1)}, u32[]{:S(2)}, u32[]{:S(2)}) %collective-permute-start.1) | collective-permute-done | bytes 196640 | tf_op jit(solution)/shard_map/ppermute | solution.py:327
  24.2 3.1 %forward.4 = (f32[192,3584]{1,0:T(8,128)S(1)}, bf16[192,3584]{1,0:T(8,128)(2,1)S(1)}, f32[8,128]{1,0:T(8,128)S(1)}) custom-call(bf16[384,1024]{1,0:T(8,128)(2,1)S(1)} %get-tuple-element.93.refs_0_, bf16[1024,7168]{1,0:T(8,128)(2,1)S(1)} %get-tuple-element.94.refs_1_.refs_3_, f32[8,128]{1,0:T(8,128)S(1)} %get-tuple-element.95.refs_2_), custom_call_target="tpu_custom_call" | custom-call | flops 1 | bytes 1 | tf_op jit(solution)/shard_map/forward/pallas_call | solution.py:58
  27.4 3.1 %forward.5 = (f32[192,3584]{1,0:T(8,128)S(1)}, bf16[192,3584]{1,0:T(8,128)(2,1)S(1)}, f32[8,128]{1,0:T(8,128)S(1)}) custom-call(bf16[384,1024]{1,0:T(8,128)(2,1)S(1)} %get-tuple-element.93.refs_0_, bf16[1024,7168]{1,0:T(8,128)(2,1)S(1)} %get-tuple-element.94.refs_1_.refs_3_, f32[8,128]{1,0:T(8,128)S(1)} %get-tuple-element.98.refs_2_), custom_call_target="tpu_custom_call" | custom-call | flops 1 | bytes 1 | tf_op jit(solution)/shard_map/forward/pallas_call | solution.py:58
  31.3 1.6 %collective-permute-start.4 = (bf16[96,3584]{1,0:T(8,128)(2,1)S(1)}, bf16[96,3584]{1,0:T(8,128)(2,1)S(1)}, u32[]{:S(2)}, u32[]{:S(2)}) collective-permute-start(bf16[96,3584]{1,0:T(8,128)(2,1)S(1)} %get-tuple-element.101), channel_id=1, source_target_pairs={{0,8},{4,12},{8,0},{12,4},{16,24},{20,28},{24,16},{28,20},{1,9},{5... | collective-permute-start | bytes 2064392 | tf_op jit(solution)/shard_map/ppermute | solution.py:327
  34.0 1.6 %collective-permute-start.14 = (bf16[96,3584]{1,0:T(8,128)(2,1)S(1)}, bf16[96,3584]{1,0:T(8,128)(2,1)S(1)}, u32[]{:S(2)}, u32[]{:S(2)}) collective-permute-start(bf16[96,3584]{1,0:T(8,128)(2,1)S(1)} %get-tuple-element.123), channel_id=1, source_target_pairs={{0,16},{4,20},{8,24},{12,28},{16,0},{20,4},{24,8},{28,12},{1,17},{... | collective-permute-start | bytes 2064392 | tf_op jit(solution)/shard_map/ppermute | solution.py:327
  36.5 2.5 %collective-permute-start.7 = (bf16[2,16,1024]{2,1,0:T(8,128)(2,1)S(1)}, bf16[2,16,1024]{2,1,0:T(8,128)(2,1)S(1)}, u32[]{:S(2)}, u32[]{:S(2)}) collective-permute-start(bf16[2,16,1024]{2,1,0:T(8,128)(2,1)S(1)} %slice.9.refs_1_), channel_id=1, source_target_pairs={{0,3},{1,2},{2,1},{3,0},{4,7},{5,6},{6,5},{7,4},{8,11},{9,10},{10,... | collective-permute-start | bytes 196616 | tf_op jit(solution)/shard_map/ppermute | solution.py:327
  38.9 1.9 %collective-permute-start.5 = (bf16[2,16,1024]{2,1,0:T(8,128)(2,1)S(1)}, bf16[2,16,1024]{2,1,0:T(8,128)(2,1)S(1)}, u32[]{:S(2)}, u32[]{:S(2)}) collective-permute-start(bf16[2,16,1024]{2,1,0:T(8,128)(2,1)S(1)} %slice.9.refs_1_), channel_id=1, source_target_pairs={{0,1},{1,0},{2,3},{3,2},{4,5},{5,4},{6,7},{7,6},{8,9},{9,8},{10,11... | collective-permute-start | bytes 196616 | tf_op jit(solution)/shard_map/ppermute | solution.py:327
  40.9 2.3 %collective-permute-done.7.refs_4_ = bf16[2,16,1024]{2,1,0:T(8,128)(2,1)S(1)} collective-permute-done((bf16[2,16,1024]{2,1,0:T(8,128)(2,1)S(1)}, bf16[2,16,1024]{2,1,0:T(8,128)(2,1)S(1)}, u32[]{:S(2)}, u32[]{:S(2)}) %collective-permute-start.7) | collective-permute-done | bytes 65568 | tf_op jit(solution)/shard_map/ppermute | solution.py:327
  43.1 2.0 %collective-permute-done.6.refs_3_ = bf16[2,16,1024]{2,1,0:T(8,128)(2,1)S(1)} collective-permute-done((bf16[2,16,1024]{2,1,0:T(8,128)(2,1)S(1)}, bf16[2,16,1024]{2,1,0:T(8,128)(2,1)S(1)}, u32[]{:S(2)}, u32[]{:S(2)}) %collective-permute-start.6) | collective-permute-done | bytes 65568 | tf_op jit(solution)/shard_map/ppermute | solution.py:327
  49.0 1.3 collective-permute-done.9.refs_1_
  52.0 1.6 %collective-permute-start.15 = (bf16[48,3584]{1,0:T(8,128)(2,1)S(1)}, bf16[48,3584]{1,0:T(8,128)(2,1)S(1)}, u32[]{:S(2)}, u32[]{:S(2)}) collective-permute-start(bf16[48,3584]{1,0:T(8,128)(2,1)S(1)} %get-tuple-element.130), channel_id=1, source_target_pairs={{0,8},{4,12},{8,0},{12,4},{16,24},{20,28},{24,16},{28,20},{1,9},{5... | collective-permute-start | bytes 1032200 | tf_op jit(solution)/shard_map/ppermute | solution.py:327
  54.0 1.5 %collective-permute-start.12 = (bf16[32,3584]{1,0:T(8,128)(2,1)S(1)}, bf16[32,3584]{1,0:T(8,128)(2,1)S(1)}, u32[]{:S(2)}, u32[]{:S(2)}) collective-permute-start(bf16[32,3584]{1,0:T(8,128)(2,1)S(1)} %get-tuple-element.119), channel_id=1, source_target_pairs={{0,16},{4,20},{8,24},{12,28},{16,0},{20,4},{24,8},{28,12},{1,17},{... | collective-permute-start | bytes 688136 | tf_op jit(solution)/shard_map/ppermute | solution.py:327
  55.6 10.9 %collective-permute-done.13.refs_1_ = bf16[32,3584]{1,0:T(8,128)(2,1)S(1)} collective-permute-done((bf16[32,3584]{1,0:T(8,128)(2,1)S(1)}, bf16[32,3584]{1,0:T(8,128)(2,1)S(1)}, u32[]{:S(2)}, u32[]{:S(2)}) %collective-permute-start.13) | collective-permute-done | bytes 229408 | tf_op jit(solution)/shard_map/ppermute | solution.py:327
  67.2 1.6 %collective-permute-start.19 = (bf16[48,3584]{1,0:T(8,128)(2,1)S(1)}, bf16[48,3584]{1,0:T(8,128)(2,1)S(1)}, u32[]{:S(2)}, u32[]{:S(2)}) collective-permute-start(bf16[48,3584]{1,0:T(8,128)(2,1)S(1)} %get-tuple-element.142.refs_0_), channel_id=1, source_target_pairs={{0,16},{4,20},{8,24},{12,28},{16,0},{20,4},{24,8},{28,12},{1,17},{... | collective-permute-start | bytes 1032200 | tf_op jit(solution)/shard_map/ppermute | solution.py:327
  69.4 1.6 %collective-permute-start.18 = (bf16[48,3584]{1,0:T(8,128)(2,1)S(1)}, bf16[48,3584]{1,0:T(8,128)(2,1)S(1)}, u32[]{:S(2)}, u32[]{:S(2)}) collective-permute-start(bf16[48,3584]{1,0:T(8,128)(2,1)S(1)} %get-tuple-element.141.refs_0_), channel_id=1, source_target_pairs={{0,8},{4,12},{8,0},{12,4},{16,24},{20,28},{24,16},{28,20},{1,9},{5... | collective-permute-start | bytes 1032200 | tf_op jit(solution)/shard_map/ppermute | solution.py:327
  72.0 6.6 %collective-permute-done.16.refs_1_ = bf16[16,3584]{1,0:T(8,128)(2,1)S(1)} collective-permute-done((bf16[16,3584]{1,0:T(8,128)(2,1)S(1)}, bf16[16,3584]{1,0:T(8,128)(2,1)S(1)}, u32[]{:S(2)}, u32[]{:S(2)}) %collective-permute-start.16) | collective-permute-done | bytes 114720 | tf_op jit(solution)/shard_map/ppermute | solution.py:327
  78.8 1.4 collective-permute-done.17.refs_1_
  80.5 1.6 %collective-permute-start.21 = (bf16[96,3584]{1,0:T(8,128)(2,1)S(1)}, bf16[96,3584]{1,0:T(8,128)(2,1)S(1)}, u32[]{:S(2)}, u32[]{:S(2)}) collective-permute-start(bf16[96,3584]{1,0:T(8,128)(2,1)S(1)} %get-tuple-element.146.refs_0_), channel_id=1, source_target_pairs={{0,8},{4,12},{8,0},{12,4},{16,24},{20,28},{24,16},{28,20},{1,9},{5... | collective-permute-start | bytes 2064392 | tf_op jit(solution)/shard_map/ppermute | solution.py:327
  84.7 14.4 %collective-permute-done.23.refs_1_ = bf16[16,3584]{1,0:T(8,128)(2,1)S(1)} collective-permute-done((bf16[16,3584]{1,0:T(8,128)(2,1)S(1)}, bf16[16,3584]{1,0:T(8,128)(2,1)S(1)}, u32[]{:S(2)}, u32[]{:S(2)}) %collective-permute-start.23) | collective-permute-done | bytes 114720 | tf_op jit(solution)/shard_map/ppermute | solution.py:327
  102.5 4.9 %input_partial.4 = (f32[1024,384]{1,0:T(8,128)S(1)}, f32[8,128]{1,0:T(8,128)S(1)}) custom-call(s32[8]{0:T(128)S(1)} %shift-right-arithmetic_add_fusion.refs_0_, bf16[192,3584]{1,0:T(8,128)(2,1)S(1)} %get-tuple-element.154.refs_1_.refs_3_, bf16[192,3584]{1,0:T(8,128)(2,1)S(1)} %collective-permute-done.25.refs_2_.refs_4_, ...), custom_call_target="tpu_custom_call" | custom-call | flops 1 | bytes 1 | tf_op jit(solution)/shard_map/input_partial/pallas_call | solution.py:58
  107.4 5.0 %input_partial.5 = (f32[96,1024]{1,0:T(8,128)S(1)}, bf16[96,1024]{1,0:T(8,128)(2,1)S(1)}, bf16[96,1024]{1,0:T(8,128)(2,1)S(1)}, bf16[96,1024]{1,0:T(8,128)(2,1)S(1)}, f32[8,128]{1,0:T(8,128)S(1)}) custom-call(s32[8]{0:T(128)S(1)} %shift-right-arithmetic_add_fusion.refs_0_, bf16[192,3584]{1,0:T(8,128)(2,1)S(1)} %get-tuple-element.153.refs_1_.refs_3_, ...), custom_call_target="tpu_custom_call" | custom-call | flops 1 | bytes 1 | tf_op jit(solution)/shard_map/input_partial/pallas_call | solution.py:58
  112.4 1.8 %collective-permute-start.26 = (bf16[96,1024]{1,0:T(8,128)(2,1)S(1)}, bf16[96,1024]{1,0:T(8,128)(2,1)S(1)}, u32[]{:S(2)}, u32[]{:S(2)}) collective-permute-start(bf16[96,1024]{1,0:T(8,128)(2,1)S(1)} %get-tuple-element.159), channel_id=1, source_target_pairs={{0,1},{1,0},{2,3},{3,2},{4,5},{5,4},{6,7},{7,6},{8,9},{9,8},{10,11... | collective-permute-start | bytes 589832 | tf_op jit(solution)/shard_map/ppermute | solution.py:327
  115.5 1.3 collective-permute-start.28
  119.5 2.7 %input_partial.6 = (f32[1024,128]{1,0:T(8,128)S(1)}, f32[8,128]{1,0:T(8,128)S(1)}) custom-call(s32[8]{0:T(128)S(1)} %shift-right-arithmetic_add_fusion.refs_0_, bf16[64,3584]{1,0:T(8,128)(2,1)S(1)} %get-tuple-element.167.refs_1_.refs_5_, bf16[64,3584]{1,0:T(8,128)(2,1)S(1)} %collective-permute-done.32.refs_2_.refs_6_, ...), custom_call_target="tpu_custom_call" | custom-call | flops 1 | bytes 1 | tf_op jit(solution)/shard_map/input_partial/pallas_call | solution.py:58
  122.2 2.8 %input_partial.7 = (f32[32,1024]{1,0:T(8,128)S(1)}, bf16[32,1024]{1,0:T(8,128)(2,1)S(1)}, bf16[32,1024]{1,0:T(8,128)(2,1)S(1)}, bf16[32,1024]{1,0:T(8,128)(2,1)S(1)}, f32[8,128]{1,0:T(8,128)S(1)}) custom-call(s32[8]{0:T(128)S(1)} %shift-right-arithmetic_add_fusion.refs_0_, bf16[64,3584]{1,0:T(8,128)(2,1)S(1)} %get-tuple-element.166.refs_1_.refs_5_, ...), custom_call_target="tpu_custom_call" | custom-call | flops 1 | bytes 1 | tf_op jit(solution)/shard_map/input_partial/pallas_call | solution.py:58
  126.0 2.2 %collective-permute-start.34 = (bf16[32,1024]{1,0:T(8,128)(2,1)S(1)}, bf16[32,1024]{1,0:T(8,128)(2,1)S(1)}, u32[]{:S(2)}, u32[]{:S(2)}) collective-permute-start(bf16[32,1024]{1,0:T(8,128)(2,1)S(1)} %get-tuple-element.173), channel_id=1, source_target_pairs={{0,2},{1,3},{2,0},{3,1},{4,6},{5,7},{6,4},{7,5},{8,10},{9,11},{10,... | collective-permute-start | bytes 196616 | tf_op jit(solution)/shard_map/ppermute | solution.py:327
  128.1 1.3 collective-permute-start.35
  129.5 4.0 %collective-permute-done.27 = bf16[96,1024]{1,0:T(8,128)(2,1)S(1)} collective-permute-done((bf16[96,1024]{1,0:T(8,128)(2,1)S(1)}, bf16[96,1024]{1,0:T(8,128)(2,1)S(1)}, u32[]{:S(2)}, u32[]{:S(2)}) %collective-permute-start.27) | collective-permute-done | bytes 196640 | tf_op jit(solution)/shard_map/ppermute | solution.py:327
  133.5 5.9 %weight_gradient.2 = (bf16[1,1,448,128,128]{4,3,2,1,0:T(8,128)(2,1)}, f32[8,128]{1,0:T(8,128)S(1)}) custom-call(s32[448]{0:T(512)S(1)} %select_reduce_fusion.refs_0_, bf16[1024,384]{1,0:T(8,128)(2,1)S(1)} %get-tuple-element.175.refs_1_, bf16[1024,128]{1,0:T(8,128)(2,1)S(1)} %get-tuple-element.176.refs_2_, ...), custom_call_target="tpu_custom_call" | custom-call | flops 1 | bytes 1 | tf_op jit(solution)/shard_map/weight_gradient/pallas_call | solution.py:58
  139.4 6.2 %weight_gradient.3 = (bf16[1,1,448,128,128]{4,3,2,1,0:T(8,128)(2,1)}, f32[8,128]{1,0:T(8,128)}) custom-call(s32[448]{0:T(512)S(1)} %select_reduce_fusion.refs_0_, bf16[1024,384]{1,0:T(8,128)(2,1)S(1)} %get-tuple-element.175.refs_1_, bf16[1024,128]{1,0:T(8,128)(2,1)S(1)} %get-tuple-element.176.refs_2_, ...), custom_call_target="tpu_custom_call", output_to_operand_aliasing={{0}: (7, {})} | custom-call | flops 1 | bytes 1 | tf_op jit(solution)/shard_map/weight_gradient/pallas_call | solution.py:58
  (88 shorter events, 26.7 us)
Async XLA Ops:
  1.6 15.1 %collective-permute-start.2 = (bf16[2,48,1024]{2,1,0:T(8,128)(2,1)S(1)}, bf16[2,48,1024]{2,1,0:T(8,128)(2,1)S(1)}, u32[]{:S(2)}, u32[]{:S(2)}) collective-permute-start(bf16[2,48,1024]{2,1,0:T(8,128)(2,1)S(1)} %slice.8.refs_1_), channel_id=1, source_target_pairs={{0,3},{1,2},{2,1},{3,0},{4,7},{5,6},{6,5},{7,4},{8,11},{9,10},{10,... | collective-permute-start | bytes 589832 | tf_op jit(solution)/shard_map/ppermute | solution.py:327
  6.7 16.7 %collective-permute-start.1 = (bf16[2,48,1024]{2,1,0:T(8,128)(2,1)S(1)}, bf16[2,48,1024]{2,1,0:T(8,128)(2,1)S(1)}, u32[]{:S(2)}, u32[]{:S(2)}) collective-permute-start(bf16[2,48,1024]{2,1,0:T(8,128)(2,1)S(1)} %slice.8.refs_1_), channel_id=1, source_target_pairs={{0,2},{1,3},{2,0},{3,1},{4,6},{5,7},{6,4},{7,5},{8,10},{9,11},{10,... | collective-permute-start | bytes 589832 | tf_op jit(solution)/shard_map/ppermute | solution.py:327
  6.7 16.7 %collective-permute-start = (bf16[2,48,1024]{2,1,0:T(8,128)(2,1)S(1)}, bf16[2,48,1024]{2,1,0:T(8,128)(2,1)S(1)}, u32[]{:S(2)}, u32[]{:S(2)}) collective-permute-start(bf16[2,48,1024]{2,1,0:T(8,128)(2,1)S(1)} %slice.8.refs_1_), channel_id=1, source_target_pairs={{0,1},{1,0},{2,3},{3,2},{4,5},{5,4},{6,7},{7,6},{8,9},{9,8},{10,11... | collective-permute-start | bytes 589832 | tf_op jit(solution)/shard_map/ppermute | solution.py:327
  27.3 3.7 %collective-permute-start.3 = (bf16[192,3584]{1,0:T(8,128)(2,1)S(1)}, bf16[192,3584]{1,0:T(8,128)(2,1)S(1)}, u32[]{:S(2)}, u32[]{:S(2)}) collective-permute-start(bf16[192,3584]{1,0:T(8,128)(2,1)S(1)} %get-tuple-element.97), channel_id=1, source_target_pairs={{0,4},{4,0},{8,12},{12,8},{16,20},{20,16},{24,28},{28,24},{1,5},{5... | collective-permute-start | bytes 4128776 | tf_op jit(solution)/shard_map/ppermute | solution.py:327
  30.5 3.3 %collective-permute-start.8 = (bf16[192,3584]{1,0:T(8,128)(2,1)S(1)}, bf16[192,3584]{1,0:T(8,128)(2,1)S(1)}, u32[]{:S(2)}, u32[]{:S(2)}) collective-permute-start(bf16[192,3584]{1,0:T(8,128)(2,1)S(1)} %get-tuple-element.103), channel_id=1, source_target_pairs={{0,4},{4,0},{8,12},{12,8},{16,20},{20,16},{24,28},{28,24},{1,5},{5... | collective-permute-start | bytes 4128776 | tf_op jit(solution)/shard_map/ppermute | solution.py:327
  31.3 19.1 %collective-permute-start.4 = (bf16[96,3584]{1,0:T(8,128)(2,1)S(1)}, bf16[96,3584]{1,0:T(8,128)(2,1)S(1)}, u32[]{:S(2)}, u32[]{:S(2)}) collective-permute-start(bf16[96,3584]{1,0:T(8,128)(2,1)S(1)} %get-tuple-element.101), channel_id=1, source_target_pairs={{0,8},{4,12},{8,0},{12,4},{16,24},{20,28},{24,16},{28,20},{1,9},{5... | collective-permute-start | bytes 2064392 | tf_op jit(solution)/shard_map/ppermute | solution.py:327
  34.0 17.8 %collective-permute-start.14 = (bf16[96,3584]{1,0:T(8,128)(2,1)S(1)}, bf16[96,3584]{1,0:T(8,128)(2,1)S(1)}, u32[]{:S(2)}, u32[]{:S(2)}) collective-permute-start(bf16[96,3584]{1,0:T(8,128)(2,1)S(1)} %get-tuple-element.123), channel_id=1, source_target_pairs={{0,16},{4,20},{8,24},{12,28},{16,0},{20,4},{24,8},{28,12},{1,17},{... | collective-permute-start | bytes 2064392 | tf_op jit(solution)/shard_map/ppermute | solution.py:327
  36.5 6.7 %collective-permute-start.7 = (bf16[2,16,1024]{2,1,0:T(8,128)(2,1)S(1)}, bf16[2,16,1024]{2,1,0:T(8,128)(2,1)S(1)}, u32[]{:S(2)}, u32[]{:S(2)}) collective-permute-start(bf16[2,16,1024]{2,1,0:T(8,128)(2,1)S(1)} %slice.9.refs_1_), channel_id=1, source_target_pairs={{0,3},{1,2},{2,1},{3,0},{4,7},{5,6},{6,5},{7,4},{8,11},{9,10},{10,... | collective-permute-start | bytes 196616 | tf_op jit(solution)/shard_map/ppermute | solution.py:327
  38.9 6.2 %collective-permute-start.6 = (bf16[2,16,1024]{2,1,0:T(8,128)(2,1)S(1)}, bf16[2,16,1024]{2,1,0:T(8,128)(2,1)S(1)}, u32[]{:S(2)}, u32[]{:S(2)}) collective-permute-start(bf16[2,16,1024]{2,1,0:T(8,128)(2,1)S(1)} %slice.9.refs_1_), channel_id=1, source_target_pairs={{0,2},{1,3},{2,0},{3,1},{4,6},{5,7},{6,4},{7,5},{8,10},{9,11},{10,... | collective-permute-start | bytes 196616 | tf_op jit(solution)/shard_map/ppermute | solution.py:327
  38.9 6.2 %collective-permute-start.5 = (bf16[2,16,1024]{2,1,0:T(8,128)(2,1)S(1)}, bf16[2,16,1024]{2,1,0:T(8,128)(2,1)S(1)}, u32[]{:S(2)}, u32[]{:S(2)}) collective-permute-start(bf16[2,16,1024]{2,1,0:T(8,128)(2,1)S(1)} %slice.9.refs_1_), channel_id=1, source_target_pairs={{0,1},{1,0},{2,3},{3,2},{4,5},{5,4},{6,7},{7,6},{8,9},{9,8},{10,11... | collective-permute-start | bytes 196616 | tf_op jit(solution)/shard_map/ppermute | solution.py:327
  50.6 16.0 %collective-permute-start.11 = (bf16[48,3584]{1,0:T(8,128)(2,1)S(1)}, bf16[48,3584]{1,0:T(8,128)(2,1)S(1)}, u32[]{:S(2)}, u32[]{:S(2)}) collective-permute-start(bf16[48,3584]{1,0:T(8,128)(2,1)S(1)} %get-tuple-element.117), channel_id=1, source_target_pairs={{0,16},{4,20},{8,24},{12,28},{16,0},{20,4},{24,8},{28,12},{1,17},{... | collective-permute-start | bytes 1032200 | tf_op jit(solution)/shard_map/ppermute | solution.py:327
  52.0 16.8 %collective-permute-start.15 = (bf16[48,3584]{1,0:T(8,128)(2,1)S(1)}, bf16[48,3584]{1,0:T(8,128)(2,1)S(1)}, u32[]{:S(2)}, u32[]{:S(2)}) collective-permute-start(bf16[48,3584]{1,0:T(8,128)(2,1)S(1)} %get-tuple-element.130), channel_id=1, source_target_pairs={{0,8},{4,12},{8,0},{12,4},{16,24},{20,28},{24,16},{28,20},{1,9},{5... | collective-permute-start | bytes 1032200 | tf_op jit(solution)/shard_map/ppermute | solution.py:327
  53.5 12.9 %collective-permute-start.13 = (bf16[32,3584]{1,0:T(8,128)(2,1)S(1)}, bf16[32,3584]{1,0:T(8,128)(2,1)S(1)}, u32[]{:S(2)}, u32[]{:S(2)}) collective-permute-start(bf16[32,3584]{1,0:T(8,128)(2,1)S(1)} %get-tuple-element.121), channel_id=1, source_target_pairs={{0,8},{4,12},{8,0},{12,4},{16,24},{20,28},{24,16},{28,20},{1,9},{5... | collective-permute-start | bytes 688136 | tf_op jit(solution)/shard_map/ppermute | solution.py:327
  54.0 12.5 %collective-permute-start.12 = (bf16[32,3584]{1,0:T(8,128)(2,1)S(1)}, bf16[32,3584]{1,0:T(8,128)(2,1)S(1)}, u32[]{:S(2)}, u32[]{:S(2)}) collective-permute-start(bf16[32,3584]{1,0:T(8,128)(2,1)S(1)} %get-tuple-element.119), channel_id=1, source_target_pairs={{0,16},{4,20},{8,24},{12,28},{16,0},{20,4},{24,8},{28,12},{1,17},{... | collective-permute-start | bytes 688136 | tf_op jit(solution)/shard_map/ppermute | solution.py:327
  67.2 13.2 %collective-permute-start.19 = (bf16[48,3584]{1,0:T(8,128)(2,1)S(1)}, bf16[48,3584]{1,0:T(8,128)(2,1)S(1)}, u32[]{:S(2)}, u32[]{:S(2)}) collective-permute-start(bf16[48,3584]{1,0:T(8,128)(2,1)S(1)} %get-tuple-element.142.refs_0_), channel_id=1, source_target_pairs={{0,16},{4,20},{8,24},{12,28},{16,0},{20,4},{24,8},{28,12},{1,17},{... | collective-permute-start | bytes 1032200 | tf_op jit(solution)/shard_map/ppermute | solution.py:327
  69.4 12.7 %collective-permute-start.18 = (bf16[48,3584]{1,0:T(8,128)(2,1)S(1)}, bf16[48,3584]{1,0:T(8,128)(2,1)S(1)}, u32[]{:S(2)}, u32[]{:S(2)}) collective-permute-start(bf16[48,3584]{1,0:T(8,128)(2,1)S(1)} %get-tuple-element.141.refs_0_), channel_id=1, source_target_pairs={{0,8},{4,12},{8,0},{12,4},{16,24},{20,28},{24,16},{28,20},{1,9},{5... | collective-permute-start | bytes 1032200 | tf_op jit(solution)/shard_map/ppermute | solution.py:327
  70.9 7.7 %collective-permute-start.16 = (bf16[16,3584]{1,0:T(8,128)(2,1)S(1)}, bf16[16,3584]{1,0:T(8,128)(2,1)S(1)}, u32[]{:S(2)}, u32[]{:S(2)}) collective-permute-start(bf16[16,3584]{1,0:T(8,128)(2,1)S(1)} %get-tuple-element.134), channel_id=1, source_target_pairs={{0,16},{4,20},{8,24},{12,28},{16,0},{20,4},{24,8},{28,12},{1,17},{... | collective-permute-start | bytes 344072 | tf_op jit(solution)/shard_map/ppermute | solution.py:327
  71.4 8.8 %collective-permute-start.17 = (bf16[16,3584]{1,0:T(8,128)(2,1)S(1)}, bf16[16,3584]{1,0:T(8,128)(2,1)S(1)}, u32[]{:S(2)}, u32[]{:S(2)}) collective-permute-start(bf16[16,3584]{1,0:T(8,128)(2,1)S(1)} %get-tuple-element.138), channel_id=1, source_target_pairs={{0,8},{4,12},{8,0},{12,4},{16,24},{20,28},{24,16},{28,20},{1,9},{5... | collective-permute-start | bytes 344072 | tf_op jit(solution)/shard_map/ppermute | solution.py:327
  80.5 18.7 %collective-permute-start.21 = (bf16[96,3584]{1,0:T(8,128)(2,1)S(1)}, bf16[96,3584]{1,0:T(8,128)(2,1)S(1)}, u32[]{:S(2)}, u32[]{:S(2)}) collective-permute-start(bf16[96,3584]{1,0:T(8,128)(2,1)S(1)} %get-tuple-element.146.refs_0_), channel_id=1, source_target_pairs={{0,8},{4,12},{8,0},{12,4},{16,24},{20,28},{24,16},{28,20},{1,9},{5... | collective-permute-start | bytes 2064392 | tf_op jit(solution)/shard_map/ppermute | solution.py:327
  82.1 17.3 %collective-permute-start.20 = (bf16[96,3584]{1,0:T(8,128)(2,1)S(1)}, bf16[96,3584]{1,0:T(8,128)(2,1)S(1)}, u32[]{:S(2)}, u32[]{:S(2)}) collective-permute-start(bf16[96,3584]{1,0:T(8,128)(2,1)S(1)} %get-tuple-element.145.refs_0_), channel_id=1, source_target_pairs={{0,16},{4,20},{8,24},{12,28},{16,0},{20,4},{24,8},{28,12},{1,17},{... | collective-permute-start | bytes 2064392 | tf_op jit(solution)/shard_map/ppermute | solution.py:327
  83.0 16.2 %collective-permute-start.23 = (bf16[16,3584]{1,0:T(8,128)(2,1)S(1)}, bf16[16,3584]{1,0:T(8,128)(2,1)S(1)}, u32[]{:S(2)}, u32[]{:S(2)}) collective-permute-start(bf16[16,3584]{1,0:T(8,128)(2,1)S(1)} %get-tuple-element.148.refs_0_), channel_id=1, source_target_pairs={{0,16},{4,20},{8,24},{12,28},{16,0},{20,4},{24,8},{28,12},{1,17},{... | collective-permute-start | bytes 344072 | tf_op jit(solution)/shard_map/ppermute | solution.py:327
  84.2 15.0 %collective-permute-start.22 = (bf16[16,3584]{1,0:T(8,128)(2,1)S(1)}, bf16[16,3584]{1,0:T(8,128)(2,1)S(1)}, u32[]{:S(2)}, u32[]{:S(2)}) collective-permute-start(bf16[16,3584]{1,0:T(8,128)(2,1)S(1)} %get-tuple-element.147.refs_0_), channel_id=1, source_target_pairs={{0,8},{4,12},{8,0},{12,4},{16,24},{20,28},{24,16},{28,20},{1,9},{5... | collective-permute-start | bytes 344072 | tf_op jit(solution)/shard_map/ppermute | solution.py:327
  99.5 7.9 %collective-permute-start.24 = (bf16[192,3584]{1,0:T(8,128)(2,1)S(1)}, bf16[192,3584]{1,0:T(8,128)(2,1)S(1)}, u32[]{:S(2)}, u32[]{:S(2)}) collective-permute-start(bf16[192,3584]{1,0:T(8,128)(2,1)S(1)} %get-tuple-element.153.refs_1_.refs_3_), channel_id=1, source_target_pairs={{0,4},{4,0},{8,12},{12,8},{16,20},{20,16},{24,28},{28,24},{1,5},{5... | collective-permute-start | bytes 4128776 | tf_op jit(solution)/shard_map/ppermute | solution.py:327
  100.0 16.8 %collective-permute-start.30 = (bf16[32,3584]{1,0:T(8,128)(2,1)S(1)}, bf16[32,3584]{1,0:T(8,128)(2,1)S(1)}, u32[]{:S(2)}, u32[]{:S(2)}) collective-permute-start(bf16[32,3584]{1,0:T(8,128)(2,1)S(1)} %get-tuple-element.163.refs_0_), channel_id=1, source_target_pairs={{0,8},{4,12},{8,0},{12,4},{16,24},{20,28},{24,16},{28,20},{1,9},{5... | collective-permute-start | bytes 688136 | tf_op jit(solution)/shard_map/ppermute | solution.py:327
  100.6 16.3 %collective-permute-start.29 = (bf16[32,3584]{1,0:T(8,128)(2,1)S(1)}, bf16[32,3584]{1,0:T(8,128)(2,1)S(1)}, u32[]{:S(2)}, u32[]{:S(2)}) collective-permute-start(bf16[32,3584]{1,0:T(8,128)(2,1)S(1)} %get-tuple-element.162.refs_0_), channel_id=1, source_target_pairs={{0,16},{4,20},{8,24},{12,28},{16,0},{20,4},{24,8},{28,12},{1,17},{... | collective-permute-start | bytes 688136 | tf_op jit(solution)/shard_map/ppermute | solution.py:327
  112.4 15.8 %collective-permute-start.26 = (bf16[96,1024]{1,0:T(8,128)(2,1)S(1)}, bf16[96,1024]{1,0:T(8,128)(2,1)S(1)}, u32[]{:S(2)}, u32[]{:S(2)}) collective-permute-start(bf16[96,1024]{1,0:T(8,128)(2,1)S(1)} %get-tuple-element.159), channel_id=1, source_target_pairs={{0,1},{1,0},{2,3},{3,2},{4,5},{5,4},{6,7},{7,6},{8,9},{9,8},{10,11... | collective-permute-start | bytes 589832 | tf_op jit(solution)/shard_map/ppermute | solution.py:327
  114.2 19.2 %collective-permute-start.27 = (bf16[96,1024]{1,0:T(8,128)(2,1)S(1)}, bf16[96,1024]{1,0:T(8,128)(2,1)S(1)}, u32[]{:S(2)}, u32[]{:S(2)}) collective-permute-start(bf16[96,1024]{1,0:T(8,128)(2,1)S(1)} %get-tuple-element.160), channel_id=1, source_target_pairs={{0,2},{1,3},{2,0},{3,1},{4,6},{5,7},{6,4},{7,5},{8,10},{9,11},{10,... | collective-permute-start | bytes 589832 | tf_op jit(solution)/shard_map/ppermute | solution.py:327
  115.5 18.0 %collective-permute-start.28 = (bf16[96,1024]{1,0:T(8,128)(2,1)S(1)}, bf16[96,1024]{1,0:T(8,128)(2,1)S(1)}, u32[]{:S(2)}, u32[]{:S(2)}) collective-permute-start(bf16[96,1024]{1,0:T(8,128)(2,1)S(1)} %get-tuple-element.161), channel_id=1, source_target_pairs={{0,3},{1,2},{2,1},{3,0},{4,7},{5,6},{6,5},{7,4},{8,11},{9,10},{10,... | collective-permute-start | bytes 589832 | tf_op jit(solution)/shard_map/ppermute | solution.py:327
  116.9 5.3 %collective-permute-start.31 = (bf16[64,3584]{1,0:T(8,128)(2,1)S(1)}, bf16[64,3584]{1,0:T(8,128)(2,1)S(1)}, u32[]{:S(2)}, u32[]{:S(2)}) collective-permute-start(bf16[64,3584]{1,0:T(8,128)(2,1)S(1)} %get-tuple-element.166.refs_1_.refs_5_), channel_id=1, source_target_pairs={{0,4},{4,0},{8,12},{12,8},{16,20},{20,16},{24,28},{28,24},{1,5},{5... | collective-permute-start | bytes 1376264 | tf_op jit(solution)/shard_map/ppermute | solution.py:327
  125.0 20.6 %collective-permute-start.33 = (bf16[32,1024]{1,0:T(8,128)(2,1)S(1)}, bf16[32,1024]{1,0:T(8,128)(2,1)S(1)}, u32[]{:S(2)}, u32[]{:S(2)}) collective-permute-start(bf16[32,1024]{1,0:T(8,128)(2,1)S(1)} %get-tuple-element.172), channel_id=1, source_target_pairs={{0,1},{1,0},{2,3},{3,2},{4,5},{5,4},{6,7},{7,6},{8,9},{9,8},{10,11... | collective-permute-start | bytes 196616 | tf_op jit(solution)/shard_map/ppermute | solution.py:327
  126.0 19.7 %collective-permute-start.34 = (bf16[32,1024]{1,0:T(8,128)(2,1)S(1)}, bf16[32,1024]{1,0:T(8,128)(2,1)S(1)}, u32[]{:S(2)}, u32[]{:S(2)}) collective-permute-start(bf16[32,1024]{1,0:T(8,128)(2,1)S(1)} %get-tuple-element.173), channel_id=1, source_target_pairs={{0,2},{1,3},{2,0},{3,1},{4,6},{5,7},{6,4},{7,5},{8,10},{9,11},{10,... | collective-permute-start | bytes 196616 | tf_op jit(solution)/shard_map/ppermute | solution.py:327
  128.1 17.5 %collective-permute-start.35 = (bf16[32,1024]{1,0:T(8,128)(2,1)S(1)}, bf16[32,1024]{1,0:T(8,128)(2,1)S(1)}, u32[]{:S(2)}, u32[]{:S(2)}) collective-permute-start(bf16[32,1024]{1,0:T(8,128)(2,1)S(1)} %get-tuple-element.174), channel_id=1, source_target_pairs={{0,3},{1,2},{2,1},{3,0},{4,7},{5,6},{6,5},{7,4},{8,11},{9,10},{10,... | collective-permute-start | bytes 196616 | tf_op jit(solution)/shard_map/ppermute | solution.py:327
  (6 other events, 33.3 us)

commit v2 on v1

--- a/solution.py
+++ b/solution.py
@@ -10,7 +10,7 @@
 
 gelu_scale = 0.7978845608
 gelu_cubic = 0.044715
-token_split = (3, 1)
+token_split = (1, 1)
 column_parts = 2
 vmem_limit = 16 * 1024 * 1024
 in_vmem = pl.BlockSpec(memory_space=pltpu.VMEM)
@@ -279,46 +279,117 @@
     )
 
 
-def weight_kernel(row_blocks, col_blocks, first, parts, has_before, code, *refs):
+def weight_kernel(row_blocks, col_blocks, parts, slabs, code, *refs):
     turned = refs[:parts]
-    grads = refs[parts : 3 * parts]
-    out_ref, made, sem = refs[3 * parts + has_before :]
+    grads = refs[parts : parts + 2 * parts * slabs]
+    out_ref, made, sems = refs[parts + 2 * parts * slabs :]
     blk = made.shape[-1]
-    width = grads[0].shape[1]
-    here = width // blk
+    here = col_blocks // slabs
     per_step = group_of(here, 2)
     wide = per_step * blk
-    for j in range(here // per_step):
-        features = jnp.concatenate([t[...] for t in turned], axis=1)
-        grad = jnp.concatenate([g[:, j * wide : (j + 1) * wide] for g in grads], axis=0)
+    per_slot = row_blocks * per_step
+    depth = made.shape[0] // per_slot
+
+    def drain(at):
+        pltpu.make_async_copy(
+            made.at[pl.ds(at * per_slot, per_slot)],
+            out_ref.at[0, 0, pl.ds(0, per_slot)],
+            sems.at[at],
+        ).wait()
+
+    features = jnp.concatenate([t[...] for t in turned], axis=1)
+    steps = [(slab, j) for slab in range(slabs) for j in range(here // per_step)]
+    for step, (slab, j) in enumerate(steps):
+        slot = step % depth
+        if step >= depth:
+            drain(slot)
+        mine = grads[2 * parts * slab : 2 * parts * (slab + 1)]
+        grad = jnp.concatenate([g[:, j * wide : (j + 1) * wide] for g in mine], axis=0)
         product = jnp.dot(features, grad, preferred_element_type=jnp.float32)
         for r in range(row_blocks):
             for c in range(per_step):
-                entry = code[r * col_blocks + first // blk + j * per_step + c]
+                entry = code[r * col_blocks + slab * here + j * per_step + c]
                 live = lax.rem(entry, 2).astype(jnp.float32)
-                at = (j * row_blocks + r) * per_step + c
+                at = slot * per_slot + r * per_step + c
                 block = product[r * blk : (r + 1) * blk, c * blk : (c + 1) * blk] * live
                 made[at] = block.astype(made.dtype)
                 pltpu.make_async_copy(
-                    made.at[at], out_ref.at[0, 0, lax.div(entry, 2)], sem
+                    made.at[at], out_ref.at[0, 0, lax.div(entry, 2)], sems.at[slot]
                 ).start()
-    pltpu.make_async_copy(made, out_ref.at[0, 0, pl.ds(0, made.shape[0])], sem).wait()
-
-
-def weight_gradient(core, turned, grads, code, first, row_blocks, col_blocks, blk, before):
+    for slot in range(min(depth, len(steps))):
+        drain(slot)
+
+
+def weight_gradient(core, turned, grads, code, row_blocks, col_blocks, blk, slabs):
     parts = len(turned)
-    has_before = before is not None
-    here = row_blocks * grads[0].shape[1] // blk
     arrays = [*turned, *grads]
+    per_slot = row_blocks * group_of(col_blocks // slabs, 2)
+    depth = 6
     [out] = core(
-        functools.partial(weight_kernel, row_blocks, col_blocks, first, parts, has_before),
+        functools.partial(weight_kernel, row_blocks, col_blocks, parts, slabs),
         "weight_gradient",
         [jax.ShapeDtypeStruct((1, 1, row_blocks * col_blocks, blk, blk), jnp.bfloat16)],
         [anywhere],
-        [in_smem] + [in_vmem] * len(arrays) + [anywhere] * has_before,
-        (code, *arrays) + ((before,) if has_before else ()),
-        scratch=[pltpu.VMEM((here, blk, blk), jnp.bfloat16), pltpu.SemaphoreType.DMA],
-        aliases={1 + len(arrays): 0} if has_before else None,
+        [in_smem] + [in_vmem] * len(arrays),
+        (code, *arrays),
+        scratch=[
+            pltpu.VMEM((depth * per_slot, blk, blk), jnp.bfloat16),
+            pltpu.SemaphoreType.DMA((depth,)),
+        ],
+    )
+    return out
+
+
+def place_kernel(spots, *refs):
+    blocks = refs[: len(spots)]
+    out_ref, sems = refs[len(spots) :]
+    copies = []
+    for at, (top, first) in enumerate(spots):
+        rows, width = blocks[at].shape
+        target = out_ref.at[pl.ds(top, rows), pl.ds(first, width)]
+        copies.append(pltpu.make_async_copy(blocks[at], target, sems.at[at]))
+        copies[-1].start()
+    for copy in copies:
+        copy.wait()
+
+
+def place_activation(core, blocks, spots, shape):
+    [out] = core(
+        functools.partial(place_kernel, spots),
+        "place_activation",
+        [jax.ShapeDtypeStruct(shape, jnp.bfloat16)],
+        [anywhere],
+        [in_vmem] * len(blocks),
+        blocks,
+        scratch=[pltpu.SemaphoreType.DMA((len(blocks),))],
+    )
+    return out
+
+
+def total_kernel(each, many, starts, sizes, *refs):
+    out_ref = refs[-1]
+    own = sum(sizes)
+    for k, (start, rows) in enumerate(zip(starts, sizes)):
+        found = refs[k * many : (k + 1) * many]
+        for j in range(each):
+            here = slice(j * rows, (j + 1) * rows)
+            total = found[0][here, :]
+            for piece in found[1:]:
+                total = total + piece[here, :].astype(jnp.float32)
+            top = j * own + start
+            out_ref[top : top + rows, :] = total.astype(jnp.bfloat16)
+
+
+def total_input(core, found, each, starts, sizes):
+    arrays = [x for part in found for x in part]
+    shape = (each * sum(sizes), arrays[0].shape[1])
+    [out] = core(
+        functools.partial(total_kernel, each, len(found[0]), starts, sizes),
+        "total_input",
+        [jax.ShapeDtypeStruct(shape, jnp.bfloat16)],
+        [pl.BlockSpec(shape, lambda: (0, 0))],
+        [in_vmem] * len(arrays),
+        arrays,
     )
     return out
 
@@ -405,46 +476,42 @@
         )
         sums[k, c] = found[0]
         if last and direct:
-            total = found[0]
-            for m in range(1, n_col):
-                total = total + swap(found[m], "col", n_col, m).astype(jnp.float32)
+            input_grads[k] = [found[0]]
+            input_grads[k] += [swap(found[m], "col", n_col, m) for m in range(1, n_col)]
         elif last:
             total = found[0].reshape(n_col, col_groups * sizes[k], tall)
             total = lax.psum_scatter(total, "col", scatter_dimension=0, tiled=True)[0]
-        if last:
-            total = total.astype(jnp.bfloat16)
-            input_grads[k] = total.reshape(col_groups, sizes[k], tall)
+            input_grads[k] = [total]
 
     hops = len(far_bits)
     stages = [begin] + [functools.partial(add, at) for at in range(hops)] + [bend]
     stages += [functools.partial(join, at) for at in reversed(range(hops))] + [finish]
-    plan = []
+    plan = [(k, at) for at in range(len(stages)) for k in range(parts)]
     if parts == 2 and hops == 2:
-        plan = [(0, 0), (0, 1), (1, 0), (1, 1), (0, 2), (1, 2), (0, 3), (1, 3), (0, 4), (1, 4)]
-        plan += [(0, 5), (0, 6), (1, 5), (1, 6)]
-    else:
-        plan = [(k, at) for at in range(len(stages)) for k in range(parts)]
+        plan = [(0, 0), (0, 1), (0, 2), (1, 0), (0, 3), (1, 1), (0, 4), (1, 2), (0, 5), (1, 3), (1, 4), (0, 6), (1, 5), (1, 6)]
     for k, at in plan:
         for c in range(slabs):
             stages[at](k, c, paths[units.index((k, c))])
-    weight_grad = None
-    for c in range(slabs):
-        weight_grad = weight_gradient(
-            core,
-            [turned[k] for k in range(parts)],
-            [g for k in range(parts) for g in state[k, c]],
-            code,
-            c * width,
-            row_blocks,
-            col_blocks,
-            blk,
-            weight_grad,
-        )
-    activation = jnp.concatenate(
-        [jnp.concatenate([activations[k, c] for c in range(slabs)], axis=1) for k in range(parts)],
-        axis=0,
-    )
-    input_grad = jnp.concatenate([input_grads[k] for k in range(parts)], axis=1).reshape(tokens.shape)
+        if (k, at) == (parts - 1, len(stages) - 3):
+            activation = place_activation(
+                core,
+                [activations[k, c] for k, c in units],
+                [(starts[k], c * width) for k, c in units],
+                grad_act.shape,
+            )
+    weight_grad = weight_gradient(
+        core,
+        [turned[k] for k in range(parts)],
+        [g for c in range(slabs) for k in range(parts) for g in state[k, c]],
+        code,
+        row_blocks,
+        col_blocks,
+        blk,
+        slabs,
+    )
+    input_grad = total_input(
+        core, [input_grads[k] for k in range(parts)], col_groups, starts, sizes
+    )
     return (activation, input_grad, weight_grad)
 
 

time: 149 us -> 140 us (0.940); the launches traced: 146 us -> 140 us
  waiting for transfers between devices: 53 us -> 45 us
  Pallas kernels: 48.3 us -> 52 us
  other arithmetic: 2.75 us -> 0.91 us
    ppermute x36, waiting for transfers between devices: 53 us -> 45 us  [swap(): return lax.ppermute(array, axis, [(i, i ^ bit) for i in range(size)])]
    pallas_call x33 -> x34, Pallas kernels: 48.3 us -> 52 us  [__call__(): pl.pallas_call(body, out_shape=[*out_shape, pltpu.VMEM((8, 128), jnp.floa...]
    concatenate x2 -> x0, other arithmetic: 1.71 us -> none  [the longest x1 0.99 us: on_device(): jnp.concatenate([jnp.concatenate([activations[k, c] for c in range(slabs)...]
  transfers between devices with their start and end apart: 36 -> 36, of which waited for: 13 -> 14; matrix products, arithmetic and copies ran while one was open for 2% -> 1% of each run, Pallas kernels for 30% -> 32%
where the time goes in v2:
time: 140 us
  Pallas kernels  52 us (37%)
  waiting for transfers between devices  45 us (32%)
  starting transfers between devices  39.1 us (28%)
  between operations  1.66 us (1%)
    pallas_call x34, Pallas kernels, __call__(): pl.pallas_call(body, out_shape=[*out_shape, pltpu.VMEM((8, 128), jnp.floa...  52 us
    ppermute x36, waiting for transfers between devices, swap(): return lax.ppermute(array, axis, [(i, i ^ bit) for i in range(size)])  45 us
    ppermute x36, starting transfers between devices, swap(): return lax.ppermute(array, axis, [(i, i ^ bit) for i in range(size)])  39.1 us
  transfers between devices with their start and end apart: 36, of which 14 were waited for; matrix products, arithmetic and copies ran while one was open for 1% of the time, Pallas kernels for 32%

profile of v2, /device:TPU:0, one launch (start us, length us, event | category | flops | bytes accessed | tf_op | source)
XLA Modules:
  0.0 139.6 jit_solution(17061306562259833847)
XLA Ops:
  1.6 5.1 %collective-permute-start.2 = (bf16[2,32,1024]{2,1,0:T(8,128)(2,1)S(1)}, bf16[2,32,1024]{2,1,0:T(8,128)(2,1)S(1)}, u32[]{:S(2)}, u32[]{:S(2)}) collective-permute-start(bf16[2,32,1024]{2,1,0:T(8,128)(2,1)S(1)} %get-tuple-element.186.refs_1_), channel_id=1, source_target_pairs={{0,3},{1,2},{2,1},{3,0},{4,7},{5,6},{6,5},{7,4},{8,11},{9,10},{10,... | collective-permute-start | bytes 393224 | tf_op jit(solution)/shard_map/ppermute | solution.py:398
  9.0 7.0 %dense_tile.1 = (bf16[1024,7168]{1,0:T(8,128)(2,1)S(1)}, f32[8,128]{1,0:T(8,128)S(1)}) custom-call(s32[448]{0:T(512)S(1)} %select_reduce_fusion.refs_0_, bf16[1,1,448,128,128]{4,3,2,1,0:T(8,128)(2,1)} %refs_1_.1), custom_call_target="tpu_custom_call" | custom-call | flops 1 | bytes 1 | tf_op jit(solution)/shard_map/dense_tile/pallas_call | solution.py:58
  16.0 1.8 %collective-permute-done.1.refs_3_ = bf16[2,32,1024]{2,1,0:T(8,128)(2,1)S(1)} collective-permute-done((bf16[2,32,1024]{2,1,0:T(8,128)(2,1)S(1)}, bf16[2,32,1024]{2,1,0:T(8,128)(2,1)S(1)}, u32[]{:S(2)}, u32[]{:S(2)}) %collective-permute-start.1) | collective-permute-done | bytes 131104 | tf_op jit(solution)/shard_map/ppermute | solution.py:398
  18.6 2.1 %forward.4 = (f32[128,3584]{1,0:T(8,128)S(1)}, bf16[128,3584]{1,0:T(8,128)(2,1)S(1)}, f32[8,128]{1,0:T(8,128)S(1)}) custom-call(bf16[256,1024]{1,0:T(8,128)(2,1)S(1)} %get-tuple-element.95.refs_0_, bf16[1024,7168]{1,0:T(8,128)(2,1)S(1)} %get-tuple-element.96.refs_1_.refs_3_, f32[8,128]{1,0:T(8,128)S(1)} %get-tuple-element.97.refs_2_), custom_call_target="tpu_custom_call" | custom-call | flops 1 | bytes 1 | tf_op jit(solution)/shard_map/forward/pallas_call | solution.py:58
  20.8 2.1 %forward.5 = (f32[128,3584]{1,0:T(8,128)S(1)}, bf16[128,3584]{1,0:T(8,128)(2,1)S(1)}, f32[8,128]{1,0:T(8,128)S(1)}) custom-call(bf16[256,1024]{1,0:T(8,128)(2,1)S(1)} %get-tuple-element.95.refs_0_, bf16[1024,7168]{1,0:T(8,128)(2,1)S(1)} %get-tuple-element.96.refs_1_.refs_3_, f32[8,128]{1,0:T(8,128)S(1)} %get-tuple-element.100.refs_2_), custom_call_target="tpu_custom_call" | custom-call | flops 1 | bytes 1 | tf_op jit(solution)/shard_map/forward/pallas_call | solution.py:58
  23.7 1.6 %collective-permute-start.4 = (bf16[64,3584]{1,0:T(8,128)(2,1)S(1)}, bf16[64,3584]{1,0:T(8,128)(2,1)S(1)}, u32[]{:S(2)}, u32[]{:S(2)}) collective-permute-start(bf16[64,3584]{1,0:T(8,128)(2,1)S(1)} %get-tuple-element.103), channel_id=1, source_target_pairs={{0,8},{4,12},{8,0},{12,4},{16,24},{20,28},{24,16},{28,20},{1,9},{5... | collective-permute-start | bytes 1376264 | tf_op jit(solution)/shard_map/ppermute | solution.py:398
  25.8 1.6 %collective-permute-start.10 = (bf16[64,3584]{1,0:T(8,128)(2,1)S(1)}, bf16[64,3584]{1,0:T(8,128)(2,1)S(1)}, u32[]{:S(2)}, u32[]{:S(2)}) collective-permute-start(bf16[64,3584]{1,0:T(8,128)(2,1)S(1)} %get-tuple-element.111), channel_id=1, source_target_pairs={{0,16},{4,20},{8,24},{12,28},{16,0},{20,4},{24,8},{28,12},{1,17},{... | collective-permute-start | bytes 1376264 | tf_op jit(solution)/shard_map/ppermute | solution.py:398
  27.4 2.5 %collective-permute-start.9 = (bf16[2,32,1024]{2,1,0:T(8,128)(2,1)S(1)}, bf16[2,32,1024]{2,1,0:T(8,128)(2,1)S(1)}, u32[]{:S(2)}, u32[]{:S(2)}) collective-permute-start(bf16[2,32,1024]{2,1,0:T(8,128)(2,1)S(1)} %get-tuple-element.185.refs_1_), channel_id=1, source_target_pairs={{0,3},{1,2},{2,1},{3,0},{4,7},{5,6},{6,5},{7,4},{8,11},{9,10},{10,... | collective-permute-start | bytes 393224 | tf_op jit(solution)/shard_map/ppermute | solution.py:398
  29.9 1.9 %collective-permute-start.7 = (bf16[2,32,1024]{2,1,0:T(8,128)(2,1)S(1)}, bf16[2,32,1024]{2,1,0:T(8,128)(2,1)S(1)}, u32[]{:S(2)}, u32[]{:S(2)}) collective-permute-start(bf16[2,32,1024]{2,1,0:T(8,128)(2,1)S(1)} %get-tuple-element.185.refs_1_), channel_id=1, source_target_pairs={{0,1},{1,0},{2,3},{3,2},{4,5},{5,4},{6,7},{7,6},{8,9},{9,8},{10,11... | collective-permute-start | bytes 393224 | tf_op jit(solution)/shard_map/ppermute | solution.py:398
  31.8 4.4 %collective-permute-done.4.refs_1_ = bf16[64,3584]{1,0:T(8,128)(2,1)S(1)} collective-permute-done((bf16[64,3584]{1,0:T(8,128)(2,1)S(1)}, bf16[64,3584]{1,0:T(8,128)(2,1)S(1)}, u32[]{:S(2)}, u32[]{:S(2)}) %collective-permute-start.4) | collective-permute-done | bytes 458784 | tf_op jit(solution)/shard_map/ppermute | solution.py:398
  36.3 2.3 %collective-permute-done.10.refs_1_ = bf16[64,3584]{1,0:T(8,128)(2,1)S(1)} collective-permute-done((bf16[64,3584]{1,0:T(8,128)(2,1)S(1)}, bf16[64,3584]{1,0:T(8,128)(2,1)S(1)}, u32[]{:S(2)}, u32[]{:S(2)}) %collective-permute-start.10) | collective-permute-done | bytes 458784 | tf_op jit(solution)/shard_map/ppermute | solution.py:398
  38.7 2.2 %collective-permute-done.8.refs_3_ = bf16[2,32,1024]{2,1,0:T(8,128)(2,1)S(1)} collective-permute-done((bf16[2,32,1024]{2,1,0:T(8,128)(2,1)S(1)}, bf16[2,32,1024]{2,1,0:T(8,128)(2,1)S(1)}, u32[]{:S(2)}, u32[]{:S(2)}) %collective-permute-start.8) | collective-permute-done | bytes 131104 | tf_op jit(solution)/shard_map/ppermute | solution.py:398
  41.7 2.1 %forward.6 = (f32[128,3584]{1,0:T(8,128)S(1)}, bf16[128,3584]{1,0:T(8,128)(2,1)S(1)}, f32[8,128]{1,0:T(8,128)S(1)}) custom-call(bf16[256,1024]{1,0:T(8,128)(2,1)S(1)} %get-tuple-element.114.refs_0_, bf16[1024,7168]{1,0:T(8,128)(2,1)S(1)} %get-tuple-element.96.refs_1_.refs_3_, f32[8,128]{1,0:T(8,128)S(1)} %get-tuple-element.115.refs_2_), custom_call_target="tpu_custom_call" | custom-call | flops 1 | bytes 1 | tf_op jit(solution)/shard_map/forward/pallas_call | solution.py:58
  43.9 2.1 %forward.7 = (f32[128,3584]{1,0:T(8,128)S(1)}, bf16[128,3584]{1,0:T(8,128)(2,1)S(1)}, f32[8,128]{1,0:T(8,128)S(1)}) custom-call(bf16[256,1024]{1,0:T(8,128)(2,1)S(1)} %get-tuple-element.114.refs_0_, bf16[1024,7168]{1,0:T(8,128)(2,1)S(1)} %get-tuple-element.96.refs_1_.refs_3_, f32[8,128]{1,0:T(8,128)S(1)} %get-tuple-element.116.refs_2_), custom_call_target="tpu_custom_call" | custom-call | flops 1 | bytes 1 | tf_op jit(solution)/shard_map/forward/pallas_call | solution.py:58
  48.3 5.9 %collective-permute-done.6.refs_1_ = bf16[32,3584]{1,0:T(8,128)(2,1)S(1)} collective-permute-done((bf16[32,3584]{1,0:T(8,128)(2,1)S(1)}, bf16[32,3584]{1,0:T(8,128)(2,1)S(1)}, u32[]{:S(2)}, u32[]{:S(2)}) %collective-permute-start.6) | collective-permute-done | bytes 229408 | tf_op jit(solution)/shard_map/ppermute | solution.py:398
  58.1 1.6 %collective-permute-start.20 = (bf16[64,3584]{1,0:T(8,128)(2,1)S(1)}, bf16[64,3584]{1,0:T(8,128)(2,1)S(1)}, u32[]{:S(2)}, u32[]{:S(2)}) collective-permute-start(bf16[64,3584]{1,0:T(8,128)(2,1)S(1)} %get-tuple-element.141), channel_id=1, source_target_pairs={{0,16},{4,20},{8,24},{12,28},{16,0},{20,4},{24,8},{28,12},{1,17},{... | collective-permute-start | bytes 1376264 | tf_op jit(solution)/shard_map/ppermute | solution.py:398
  59.7 3.5 %collective-permute-done.15.refs_1_ = bf16[32,3584]{1,0:T(8,128)(2,1)S(1)} collective-permute-done((bf16[32,3584]{1,0:T(8,128)(2,1)S(1)}, bf16[32,3584]{1,0:T(8,128)(2,1)S(1)}, u32[]{:S(2)}, u32[]{:S(2)}) %collective-permute-start.15) | collective-permute-done | bytes 229408 | tf_op jit(solution)/shard_map/ppermute | solution.py:398
  63.3 1.4 %collective-permute-start.19 = (bf16[64,3584]{1,0:T(8,128)(2,1)S(1)}, bf16[64,3584]{1,0:T(8,128)(2,1)S(1)}, u32[]{:S(2)}, u32[]{:S(2)}) collective-permute-start(bf16[64,3584]{1,0:T(8,128)(2,1)S(1)} %get-tuple-element.139.refs_0_), channel_id=1, source_target_pairs={{0,8},{4,12},{8,0},{12,4},{16,24},{20,28},{24,16},{28,20},{1,9},{5... | collective-permute-start | bytes 1376264 | tf_op jit(solution)/shard_map/ppermute | solution.py:398
  65.8 8.2 %collective-permute-done.13.refs_1_ = bf16[64,3584]{1,0:T(8,128)(2,1)S(1)} collective-permute-done((bf16[64,3584]{1,0:T(8,128)(2,1)S(1)}, bf16[64,3584]{1,0:T(8,128)(2,1)S(1)}, u32[]{:S(2)}, u32[]{:S(2)}) %collective-permute-start.13) | collective-permute-done | bytes 458784 | tf_op jit(solution)/shard_map/ppermute | solution.py:398
  74.1 1.6 %collective-permute-start.17 = (bf16[32,3584]{1,0:T(8,128)(2,1)S(1)}, bf16[32,3584]{1,0:T(8,128)(2,1)S(1)}, u32[]{:S(2)}, u32[]{:S(2)}) collective-permute-start(bf16[32,3584]{1,0:T(8,128)(2,1)S(1)} %get-tuple-element.137), channel_id=1, source_target_pairs={{0,16},{4,20},{8,24},{12,28},{16,0},{20,4},{24,8},{28,12},{1,17},{... | collective-permute-start | bytes 688136 | tf_op jit(solution)/shard_map/ppermute | solution.py:398
  77.2 6.6 %collective-permute-done.19.refs_1_ = bf16[64,3584]{1,0:T(8,128)(2,1)S(1)} collective-permute-done((bf16[64,3584]{1,0:T(8,128)(2,1)S(1)}, bf16[64,3584]{1,0:T(8,128)(2,1)S(1)}, u32[]{:S(2)}, u32[]{:S(2)}) %collective-permute-start.19) | collective-permute-done | bytes 458784 | tf_op jit(solution)/shard_map/ppermute | solution.py:398
  84.6 1.4 %collective-permute-done.17.refs_1_ = bf16[32,3584]{1,0:T(8,128)(2,1)S(1)} collective-permute-done((bf16[32,3584]{1,0:T(8,128)(2,1)S(1)}, bf16[32,3584]{1,0:T(8,128)(2,1)S(1)}, u32[]{:S(2)}, u32[]{:S(2)}) %collective-permute-start.17) | collective-permute-done | bytes 229408 | tf_op jit(solution)/shard_map/ppermute | solution.py:398
  88.6 4.0 %collective-permute-done.23.refs_1_ = bf16[32,3584]{1,0:T(8,128)(2,1)S(1)} collective-permute-done((bf16[32,3584]{1,0:T(8,128)(2,1)S(1)}, bf16[32,3584]{1,0:T(8,128)(2,1)S(1)}, u32[]{:S(2)}, u32[]{:S(2)}) %collective-permute-start.23) | collective-permute-done | bytes 229408 | tf_op jit(solution)/shard_map/ppermute | solution.py:398
  93.9 1.5 %collective-permute-done.22.refs_1_ = bf16[32,3584]{1,0:T(8,128)(2,1)S(1)} collective-permute-done((bf16[32,3584]{1,0:T(8,128)(2,1)S(1)}, bf16[32,3584]{1,0:T(8,128)(2,1)S(1)}, u32[]{:S(2)}, u32[]{:S(2)}) %collective-permute-start.22) | collective-permute-done | bytes 229408 | tf_op jit(solution)/shard_map/ppermute | solution.py:398
  96.7 2.8 %input_partial.4 = (f32[1024,256]{1,0:T(8,128)S(1)}, f32[8,128]{1,0:T(8,128)S(1)}) custom-call(s32[8]{0:T(128)S(1)} %shift-right-arithmetic_add_fusion.refs_0_, bf16[128,3584]{1,0:T(8,128)(2,1)S(1)} %get-tuple-element.158.refs_1_.refs_3_, bf16[128,3584]{1,0:T(8,128)(2,1)S(1)} %collective-permute-done.25.refs_2_.refs_4_, ...), custom_call_target="tpu_custom_call" | custom-call | flops 1 | bytes 1 | tf_op jit(solution)/shard_map/input_partial/pallas_call | solution.py:58
  99.5 2.9 %input_partial.5 = (f32[64,1024]{1,0:T(8,128)S(1)}, bf16[64,1024]{1,0:T(8,128)(2,1)S(1)}, bf16[64,1024]{1,0:T(8,128)(2,1)S(1)}, bf16[64,1024]{1,0:T(8,128)(2,1)S(1)}, f32[8,128]{1,0:T(8,128)S(1)}) custom-call(s32[8]{0:T(128)S(1)} %shift-right-arithmetic_add_fusion.refs_0_, bf16[128,3584]{1,0:T(8,128)(2,1)S(1)} %get-tuple-element.157.refs_1_.refs_7_, ...), custom_call_target="tpu_custom_call" | custom-call | flops 1 | bytes 1 | tf_op jit(solution)/shard_map/input_partial/pallas_call | solution.py:58
  102.4 1.7 %collective-permute-done.30.refs_1_ = bf16[64,3584]{1,0:T(8,128)(2,1)S(1)} collective-permute-done((bf16[64,3584]{1,0:T(8,128)(2,1)S(1)}, bf16[64,3584]{1,0:T(8,128)(2,1)S(1)}, u32[]{:S(2)}, u32[]{:S(2)}) %collective-permute-start.30) | collective-permute-done | bytes 458784 | tf_op jit(solution)/shard_map/ppermute | solution.py:398
  105.6 2.9 %collective-permute-start.27 = (bf16[64,1024]{1,0:T(8,128)(2,1)S(1)}, bf16[64,1024]{1,0:T(8,128)(2,1)S(1)}, u32[]{:S(2)}, u32[]{:S(2)}) collective-permute-start(bf16[64,1024]{1,0:T(8,128)(2,1)S(1)} %get-tuple-element.164), channel_id=1, source_target_pairs={{0,2},{1,3},{2,0},{3,1},{4,6},{5,7},{6,4},{7,5},{8,10},{9,11},{10,... | collective-permute-start | bytes 393224 | tf_op jit(solution)/shard_map/ppermute | solution.py:398
  110.0 2.6 %input_partial.6 = (f32[1024,256]{1,0:T(8,128)S(1)}, f32[8,128]{1,0:T(8,128)S(1)}) custom-call(s32[8]{0:T(128)S(1)} %shift-right-arithmetic_add_fusion.refs_0_, bf16[128,3584]{1,0:T(8,128)(2,1)S(1)} %get-tuple-element.171.refs_1_.refs_5_, bf16[128,3584]{1,0:T(8,128)(2,1)S(1)} %collective-permute-done.32.refs_2_.refs_6_, ...), custom_call_target="tpu_custom_call" | custom-call | flops 1 | bytes 1 | tf_op jit(solution)/shard_map/input_partial/pallas_call | solution.py:58
  112.6 2.9 %input_partial.7 = (f32[64,1024]{1,0:T(8,128)S(1)}, bf16[64,1024]{1,0:T(8,128)(2,1)S(1)}, bf16[64,1024]{1,0:T(8,128)(2,1)S(1)}, bf16[64,1024]{1,0:T(8,128)(2,1)S(1)}, f32[8,128]{1,0:T(8,128)S(1)}) custom-call(s32[8]{0:T(128)S(1)} %shift-right-arithmetic_add_fusion.refs_0_, bf16[128,3584]{1,0:T(8,128)(2,1)S(1)} %get-tuple-element.170.refs_1_.refs_9_, ...), custom_call_target="tpu_custom_call" | custom-call | flops 1 | bytes 1 | tf_op jit(solution)/shard_map/input_partial/pallas_call | solution.py:58
  115.6 3.0 %collective-permute-start.34 = (bf16[64,1024]{1,0:T(8,128)(2,1)S(1)}, bf16[64,1024]{1,0:T(8,128)(2,1)S(1)}, u32[]{:S(2)}, u32[]{:S(2)}) collective-permute-start(bf16[64,1024]{1,0:T(8,128)(2,1)S(1)} %get-tuple-element.177), channel_id=1, source_target_pairs={{0,2},{1,3},{2,0},{3,1},{4,6},{5,7},{6,4},{7,5},{8,10},{9,11},{10,... | collective-permute-start | bytes 393224 | tf_op jit(solution)/shard_map/ppermute | solution.py:398
  120.0 18.7 %weight_gradient.1 = (bf16[1,1,448,128,128]{4,3,2,1,0:T(8,128)(2,1)}, f32[8,128]{1,0:T(8,128)S(1)}) custom-call(s32[448]{0:T(512)S(1)} %select_reduce_fusion.refs_0_, bf16[1024,256]{1,0:T(8,128)(2,1)S(1)} %get-tuple-element.179.refs_1_, bf16[1024,256]{1,0:T(8,128)(2,1)S(1)} %get-tuple-element.180.refs_2_, ...), custom_call_target="tpu_custom_call" | custom-call | flops 1 | bytes 1 | tf_op jit(solution)/shard_map/weight_gradient/pallas_call | solution.py:58
  (84 shorter events, 25.7 us)
Async XLA Ops:
  1.6 14.4 %collective-permute-start.2 = (bf16[2,32,1024]{2,1,0:T(8,128)(2,1)S(1)}, bf16[2,32,1024]{2,1,0:T(8,128)(2,1)S(1)}, u32[]{:S(2)}, u32[]{:S(2)}) collective-permute-start(bf16[2,32,1024]{2,1,0:T(8,128)(2,1)S(1)} %get-tuple-element.186.refs_1_), channel_id=1, source_target_pairs={{0,3},{1,2},{2,1},{3,0},{4,7},{5,6},{6,5},{7,4},{8,11},{9,10},{10,... | collective-permute-start | bytes 393224 | tf_op jit(solution)/shard_map/ppermute | solution.py:398
  6.7 11.1 %collective-permute-start.1 = (bf16[2,32,1024]{2,1,0:T(8,128)(2,1)S(1)}, bf16[2,32,1024]{2,1,0:T(8,128)(2,1)S(1)}, u32[]{:S(2)}, u32[]{:S(2)}) collective-permute-start(bf16[2,32,1024]{2,1,0:T(8,128)(2,1)S(1)} %get-tuple-element.186.refs_1_), channel_id=1, source_target_pairs={{0,2},{1,3},{2,0},{3,1},{4,6},{5,7},{6,4},{7,5},{8,10},{9,11},{10,... | collective-permute-start | bytes 393224 | tf_op jit(solution)/shard_map/ppermute | solution.py:398
  6.7 11.1 %collective-permute-start = (bf16[2,32,1024]{2,1,0:T(8,128)(2,1)S(1)}, bf16[2,32,1024]{2,1,0:T(8,128)(2,1)S(1)}, u32[]{:S(2)}, u32[]{:S(2)}) collective-permute-start(bf16[2,32,1024]{2,1,0:T(8,128)(2,1)S(1)} %get-tuple-element.186.refs_1_), channel_id=1, source_target_pairs={{0,1},{1,0},{2,3},{3,2},{4,5},{5,4},{6,7},{7,6},{8,9},{9,8},{10,11... | collective-permute-start | bytes 393224 | tf_op jit(solution)/shard_map/ppermute | solution.py:398
  23.7 12.5 %collective-permute-start.4 = (bf16[64,3584]{1,0:T(8,128)(2,1)S(1)}, bf16[64,3584]{1,0:T(8,128)(2,1)S(1)}, u32[]{:S(2)}, u32[]{:S(2)}) collective-permute-start(bf16[64,3584]{1,0:T(8,128)(2,1)S(1)} %get-tuple-element.103), channel_id=1, source_target_pairs={{0,8},{4,12},{8,0},{12,4},{16,24},{20,28},{24,16},{28,20},{1,9},{5... | collective-permute-start | bytes 1376264 | tf_op jit(solution)/shard_map/ppermute | solution.py:398
  25.8 12.9 %collective-permute-start.10 = (bf16[64,3584]{1,0:T(8,128)(2,1)S(1)}, bf16[64,3584]{1,0:T(8,128)(2,1)S(1)}, u32[]{:S(2)}, u32[]{:S(2)}) collective-permute-start(bf16[64,3584]{1,0:T(8,128)(2,1)S(1)} %get-tuple-element.111), channel_id=1, source_target_pairs={{0,16},{4,20},{8,24},{12,28},{16,0},{20,4},{24,8},{28,12},{1,17},{... | collective-permute-start | bytes 1376264 | tf_op jit(solution)/shard_map/ppermute | solution.py:398
  27.4 11.3 %collective-permute-start.9 = (bf16[2,32,1024]{2,1,0:T(8,128)(2,1)S(1)}, bf16[2,32,1024]{2,1,0:T(8,128)(2,1)S(1)}, u32[]{:S(2)}, u32[]{:S(2)}) collective-permute-start(bf16[2,32,1024]{2,1,0:T(8,128)(2,1)S(1)} %get-tuple-element.185.refs_1_), channel_id=1, source_target_pairs={{0,3},{1,2},{2,1},{3,0},{4,7},{5,6},{6,5},{7,4},{8,11},{9,10},{10,... | collective-permute-start | bytes 393224 | tf_op jit(solution)/shard_map/ppermute | solution.py:398
  29.9 11.1 %collective-permute-start.8 = (bf16[2,32,1024]{2,1,0:T(8,128)(2,1)S(1)}, bf16[2,32,1024]{2,1,0:T(8,128)(2,1)S(1)}, u32[]{:S(2)}, u32[]{:S(2)}) collective-permute-start(bf16[2,32,1024]{2,1,0:T(8,128)(2,1)S(1)} %get-tuple-element.185.refs_1_), channel_id=1, source_target_pairs={{0,2},{1,3},{2,0},{3,1},{4,6},{5,7},{6,4},{7,5},{8,10},{9,11},{10,... | collective-permute-start | bytes 393224 | tf_op jit(solution)/shard_map/ppermute | solution.py:398
  29.9 11.1 %collective-permute-start.7 = (bf16[2,32,1024]{2,1,0:T(8,128)(2,1)S(1)}, bf16[2,32,1024]{2,1,0:T(8,128)(2,1)S(1)}, u32[]{:S(2)}, u32[]{:S(2)}) collective-permute-start(bf16[2,32,1024]{2,1,0:T(8,128)(2,1)S(1)} %get-tuple-element.185.refs_1_), channel_id=1, source_target_pairs={{0,1},{1,0},{2,3},{3,2},{4,5},{5,4},{6,7},{7,6},{8,9},{9,8},{10,11... | collective-permute-start | bytes 393224 | tf_op jit(solution)/shard_map/ppermute | solution.py:398
  43.9 13.0 %collective-permute-start.12 = (bf16[128,3584]{1,0:T(8,128)(2,1)S(1)}, bf16[128,3584]{1,0:T(8,128)(2,1)S(1)}, u32[]{:S(2)}, u32[]{:S(2)}) collective-permute-start(bf16[128,3584]{1,0:T(8,128)(2,1)S(1)} %get-tuple-element.124), channel_id=1, source_target_pairs={{0,4},{4,0},{8,12},{12,8},{16,20},{20,16},{24,28},{28,24},{1,5},{5... | collective-permute-start | bytes 2752520 | tf_op jit(solution)/shard_map/ppermute | solution.py:398
  46.1 11.8 %collective-permute-start.16 = (bf16[128,3584]{1,0:T(8,128)(2,1)S(1)}, bf16[128,3584]{1,0:T(8,128)(2,1)S(1)}, u32[]{:S(2)}, u32[]{:S(2)}) collective-permute-start(bf16[128,3584]{1,0:T(8,128)(2,1)S(1)} %get-tuple-element.131), channel_id=1, source_target_pairs={{0,4},{4,0},{8,12},{12,8},{16,20},{20,16},{24,28},{28,24},{1,5},{5... | collective-permute-start | bytes 2752520 | tf_op jit(solution)/shard_map/ppermute | solution.py:398
  46.6 7.6 %collective-permute-start.6 = (bf16[32,3584]{1,0:T(8,128)(2,1)S(1)}, bf16[32,3584]{1,0:T(8,128)(2,1)S(1)}, u32[]{:S(2)}, u32[]{:S(2)}) collective-permute-start(bf16[32,3584]{1,0:T(8,128)(2,1)S(1)} %get-tuple-element.109), channel_id=1, source_target_pairs={{0,16},{4,20},{8,24},{12,28},{16,0},{20,4},{24,8},{28,12},{1,17},{... | collective-permute-start | bytes 688136 | tf_op jit(solution)/shard_map/ppermute | solution.py:398
  47.1 8.1 %collective-permute-start.11 = (bf16[32,3584]{1,0:T(8,128)(2,1)S(1)}, bf16[32,3584]{1,0:T(8,128)(2,1)S(1)}, u32[]{:S(2)}, u32[]{:S(2)}) collective-permute-start(bf16[32,3584]{1,0:T(8,128)(2,1)S(1)} %get-tuple-element.120), channel_id=1, source_target_pairs={{0,8},{4,12},{8,0},{12,4},{16,24},{20,28},{24,16},{28,20},{1,9},{5... | collective-permute-start | bytes 688136 | tf_op jit(solution)/shard_map/ppermute | solution.py:398
  54.6 8.6 %collective-permute-start.15 = (bf16[32,3584]{1,0:T(8,128)(2,1)S(1)}, bf16[32,3584]{1,0:T(8,128)(2,1)S(1)}, u32[]{:S(2)}, u32[]{:S(2)}) collective-permute-start(bf16[32,3584]{1,0:T(8,128)(2,1)S(1)} %get-tuple-element.129.refs_0_), channel_id=1, source_target_pairs={{0,16},{4,20},{8,24},{12,28},{16,0},{20,4},{24,8},{28,12},{1,17},{... | collective-permute-start | bytes 688136 | tf_op jit(solution)/shard_map/ppermute | solution.py:398
  55.5 9.1 %collective-permute-start.14 = (bf16[32,3584]{1,0:T(8,128)(2,1)S(1)}, bf16[32,3584]{1,0:T(8,128)(2,1)S(1)}, u32[]{:S(2)}, u32[]{:S(2)}) collective-permute-start(bf16[32,3584]{1,0:T(8,128)(2,1)S(1)} %get-tuple-element.128.refs_0_), channel_id=1, source_target_pairs={{0,8},{4,12},{8,0},{12,4},{16,24},{20,28},{24,16},{28,20},{1,9},{5... | collective-permute-start | bytes 688136 | tf_op jit(solution)/shard_map/ppermute | solution.py:398
  57.0 16.9 %collective-permute-start.13 = (bf16[64,3584]{1,0:T(8,128)(2,1)S(1)}, bf16[64,3584]{1,0:T(8,128)(2,1)S(1)}, u32[]{:S(2)}, u32[]{:S(2)}) collective-permute-start(bf16[64,3584]{1,0:T(8,128)(2,1)S(1)} %get-tuple-element.127), channel_id=1, source_target_pairs={{0,8},{4,12},{8,0},{12,4},{16,24},{20,28},{24,16},{28,20},{1,9},{5... | collective-permute-start | bytes 1376264 | tf_op jit(solution)/shard_map/ppermute | solution.py:398
  58.1 17.6 %collective-permute-start.20 = (bf16[64,3584]{1,0:T(8,128)(2,1)S(1)}, bf16[64,3584]{1,0:T(8,128)(2,1)S(1)}, u32[]{:S(2)}, u32[]{:S(2)}) collective-permute-start(bf16[64,3584]{1,0:T(8,128)(2,1)S(1)} %get-tuple-element.141), channel_id=1, source_target_pairs={{0,16},{4,20},{8,24},{12,28},{16,0},{20,4},{24,8},{28,12},{1,17},{... | collective-permute-start | bytes 1376264 | tf_op jit(solution)/shard_map/ppermute | solution.py:398
  63.3 20.6 %collective-permute-start.19 = (bf16[64,3584]{1,0:T(8,128)(2,1)S(1)}, bf16[64,3584]{1,0:T(8,128)(2,1)S(1)}, u32[]{:S(2)}, u32[]{:S(2)}) collective-permute-start(bf16[64,3584]{1,0:T(8,128)(2,1)S(1)} %get-tuple-element.139.refs_0_), channel_id=1, source_target_pairs={{0,8},{4,12},{8,0},{12,4},{16,24},{20,28},{24,16},{28,20},{1,9},{5... | collective-permute-start | bytes 1376264 | tf_op jit(solution)/shard_map/ppermute | solution.py:398
  64.7 19.3 %collective-permute-start.18 = (bf16[64,3584]{1,0:T(8,128)(2,1)S(1)}, bf16[64,3584]{1,0:T(8,128)(2,1)S(1)}, u32[]{:S(2)}, u32[]{:S(2)}) collective-permute-start(bf16[64,3584]{1,0:T(8,128)(2,1)S(1)} %get-tuple-element.138.refs_0_), channel_id=1, source_target_pairs={{0,16},{4,20},{8,24},{12,28},{16,0},{20,4},{24,8},{28,12},{1,17},{... | collective-permute-start | bytes 1376264 | tf_op jit(solution)/shard_map/ppermute | solution.py:398
  74.1 11.9 %collective-permute-start.17 = (bf16[32,3584]{1,0:T(8,128)(2,1)S(1)}, bf16[32,3584]{1,0:T(8,128)(2,1)S(1)}, u32[]{:S(2)}, u32[]{:S(2)}) collective-permute-start(bf16[32,3584]{1,0:T(8,128)(2,1)S(1)} %get-tuple-element.137), channel_id=1, source_target_pairs={{0,16},{4,20},{8,24},{12,28},{16,0},{20,4},{24,8},{28,12},{1,17},{... | collective-permute-start | bytes 688136 | tf_op jit(solution)/shard_map/ppermute | solution.py:398
  75.8 11.1 %collective-permute-start.21 = (bf16[32,3584]{1,0:T(8,128)(2,1)S(1)}, bf16[32,3584]{1,0:T(8,128)(2,1)S(1)}, u32[]{:S(2)}, u32[]{:S(2)}) collective-permute-start(bf16[32,3584]{1,0:T(8,128)(2,1)S(1)} %get-tuple-element.148), channel_id=1, source_target_pairs={{0,8},{4,12},{8,0},{12,4},{16,24},{20,28},{24,16},{28,20},{1,9},{5... | collective-permute-start | bytes 688136 | tf_op jit(solution)/shard_map/ppermute | solution.py:398
  83.9 12.8 %collective-permute-start.25 = (bf16[128,3584]{1,0:T(8,128)(2,1)S(1)}, bf16[128,3584]{1,0:T(8,128)(2,1)S(1)}, u32[]{:S(2)}, u32[]{:S(2)}) collective-permute-start(bf16[128,3584]{1,0:T(8,128)(2,1)S(1)} %get-tuple-element.158.refs_1_.refs_3_), channel_id=1, source_target_pairs={{0,4},{4,0},{8,12},{12,8},{16,20},{20,16},{24,28},{28,24},{1,5},{5... | collective-permute-start | bytes 2752520 | tf_op jit(solution)/shard_map/ppermute | solution.py:398
  84.0 15.5 %collective-permute-start.24 = (bf16[128,3584]{1,0:T(8,128)(2,1)S(1)}, bf16[128,3584]{1,0:T(8,128)(2,1)S(1)}, u32[]{:S(2)}, u32[]{:S(2)}) collective-permute-start(bf16[128,3584]{1,0:T(8,128)(2,1)S(1)} %get-tuple-element.157.refs_1_.refs_7_), channel_id=1, source_target_pairs={{0,4},{4,0},{8,12},{12,8},{16,20},{20,16},{24,28},{28,24},{1,5},{5... | collective-permute-start | bytes 2752520 | tf_op jit(solution)/shard_map/ppermute | solution.py:398
  87.3 8.1 %collective-permute-start.22 = (bf16[32,3584]{1,0:T(8,128)(2,1)S(1)}, bf16[32,3584]{1,0:T(8,128)(2,1)S(1)}, u32[]{:S(2)}, u32[]{:S(2)}) collective-permute-start(bf16[32,3584]{1,0:T(8,128)(2,1)S(1)} %get-tuple-element.151.refs_0_), channel_id=1, source_target_pairs={{0,8},{4,12},{8,0},{12,4},{16,24},{20,28},{24,16},{28,20},{1,9},{5... | collective-permute-start | bytes 688136 | tf_op jit(solution)/shard_map/ppermute | solution.py:398
  92.6 11.5 %collective-permute-start.30 = (bf16[64,3584]{1,0:T(8,128)(2,1)S(1)}, bf16[64,3584]{1,0:T(8,128)(2,1)S(1)}, u32[]{:S(2)}, u32[]{:S(2)}) collective-permute-start(bf16[64,3584]{1,0:T(8,128)(2,1)S(1)} %get-tuple-element.167.refs_0_), channel_id=1, source_target_pairs={{0,8},{4,12},{8,0},{12,4},{16,24},{20,28},{24,16},{28,20},{1,9},{5... | collective-permute-start | bytes 1376264 | tf_op jit(solution)/shard_map/ppermute | solution.py:398
  95.5 9.9 %collective-permute-start.29 = (bf16[64,3584]{1,0:T(8,128)(2,1)S(1)}, bf16[64,3584]{1,0:T(8,128)(2,1)S(1)}, u32[]{:S(2)}, u32[]{:S(2)}) collective-permute-start(bf16[64,3584]{1,0:T(8,128)(2,1)S(1)} %get-tuple-element.166.refs_0_), channel_id=1, source_target_pairs={{0,16},{4,20},{8,24},{12,28},{16,0},{20,4},{24,8},{28,12},{1,17},{... | collective-permute-start | bytes 1376264 | tf_op jit(solution)/shard_map/ppermute | solution.py:398
  105.4 7.2 %collective-permute-start.31 = (bf16[128,3584]{1,0:T(8,128)(2,1)S(1)}, bf16[128,3584]{1,0:T(8,128)(2,1)S(1)}, u32[]{:S(2)}, u32[]{:S(2)}) collective-permute-start(bf16[128,3584]{1,0:T(8,128)(2,1)S(1)} %get-tuple-element.170.refs_1_.refs_9_), channel_id=1, source_target_pairs={{0,4},{4,0},{8,12},{12,8},{16,20},{20,16},{24,28},{28,24},{1,5},{5... | collective-permute-start | bytes 2752520 | tf_op jit(solution)/shard_map/ppermute | solution.py:398
  105.5 13.1 %collective-permute-start.26 = (bf16[64,1024]{1,0:T(8,128)(2,1)S(1)}, bf16[64,1024]{1,0:T(8,128)(2,1)S(1)}, u32[]{:S(2)}, u32[]{:S(2)}) collective-permute-start(bf16[64,1024]{1,0:T(8,128)(2,1)S(1)} %get-tuple-element.163), channel_id=1, source_target_pairs={{0,1},{1,0},{2,3},{3,2},{4,5},{5,4},{6,7},{7,6},{8,9},{9,8},{10,11... | collective-permute-start | bytes 393224 | tf_op jit(solution)/shard_map/ppermute | solution.py:398
  105.6 33.1 %collective-permute-start.27 = (bf16[64,1024]{1,0:T(8,128)(2,1)S(1)}, bf16[64,1024]{1,0:T(8,128)(2,1)S(1)}, u32[]{:S(2)}, u32[]{:S(2)}) collective-permute-start(bf16[64,1024]{1,0:T(8,128)(2,1)S(1)} %get-tuple-element.164), channel_id=1, source_target_pairs={{0,2},{1,3},{2,0},{3,1},{4,6},{5,7},{6,4},{7,5},{8,10},{9,11},{10,... | collective-permute-start | bytes 393224 | tf_op jit(solution)/shard_map/ppermute | solution.py:398
  108.6 30.2 %collective-permute-start.28 = (bf16[64,1024]{1,0:T(8,128)(2,1)S(1)}, bf16[64,1024]{1,0:T(8,128)(2,1)S(1)}, u32[]{:S(2)}, u32[]{:S(2)}) collective-permute-start(bf16[64,1024]{1,0:T(8,128)(2,1)S(1)} %get-tuple-element.165), channel_id=1, source_target_pairs={{0,3},{1,2},{2,1},{3,0},{4,7},{5,6},{6,5},{7,4},{8,11},{9,10},{10,... | collective-permute-start | bytes 393224 | tf_op jit(solution)/shard_map/ppermute | solution.py:398
  115.6 23.2 %collective-permute-start.33 = (bf16[64,1024]{1,0:T(8,128)(2,1)S(1)}, bf16[64,1024]{1,0:T(8,128)(2,1)S(1)}, u32[]{:S(2)}, u32[]{:S(2)}) collective-permute-start(bf16[64,1024]{1,0:T(8,128)(2,1)S(1)} %get-tuple-element.176), channel_id=1, source_target_pairs={{0,1},{1,0},{2,3},{3,2},{4,5},{5,4},{6,7},{7,6},{8,9},{9,8},{10,11... | collective-permute-start | bytes 393224 | tf_op jit(solution)/shard_map/ppermute | solution.py:398
  115.6 23.1 %collective-permute-start.34 = (bf16[64,1024]{1,0:T(8,128)(2,1)S(1)}, bf16[64,1024]{1,0:T(8,128)(2,1)S(1)}, u32[]{:S(2)}, u32[]{:S(2)}) collective-permute-start(bf16[64,1024]{1,0:T(8,128)(2,1)S(1)} %get-tuple-element.177), channel_id=1, source_target_pairs={{0,2},{1,3},{2,0},{3,1},{4,6},{5,7},{6,4},{7,5},{8,10},{9,11},{10,... | collective-permute-start | bytes 393224 | tf_op jit(solution)/shard_map/ppermute | solution.py:398
  118.6 20.2 %collective-permute-start.35 = (bf16[64,1024]{1,0:T(8,128)(2,1)S(1)}, bf16[64,1024]{1,0:T(8,128)(2,1)S(1)}, u32[]{:S(2)}, u32[]{:S(2)}) collective-permute-start(bf16[64,1024]{1,0:T(8,128)(2,1)S(1)} %get-tuple-element.178), channel_id=1, source_target_pairs={{0,3},{1,2},{2,1},{3,0},{4,7},{5,6},{6,5},{7,4},{8,11},{9,10},{10,... | collective-permute-start | bytes 393224 | tf_op jit(solution)/shard_map/ppermute | solution.py:398
  (6 other events, 34.7 us)

commit v3 on v1

--- a/solution.py
+++ b/solution.py
@@ -10,7 +10,7 @@
 
 gelu_scale = 0.7978845608
 gelu_cubic = 0.044715
-token_split = (3, 1)
+token_split = (1, 1)
 column_parts = 2
 vmem_limit = 16 * 1024 * 1024
 in_vmem = pl.BlockSpec(memory_space=pltpu.VMEM)
@@ -107,23 +107,25 @@
     return weight
 
 
-def arrange_kernel(groups, rows, pieces, pick, *refs):
+def arrange_kernel(first, rows, each, pieces, pick, *refs):
     out_ref, turned_ref, all_ref = refs[pieces:]
-    each = groups // pieces
+    groups = all_ref.shape[0]
+    own = pieces * refs[0].shape[0] // groups
     for m in range(pieces):
         for j in range(each):
-            all_ref[m * each + j] = refs[m][j]
+            start = j * own + first
+            all_ref[m * each + j] = refs[m][start : start + rows, :]
     for t in range(groups):
         out_ref[pl.ds(t * rows, rows), :] = all_ref[pick[t]]
     turned_ref[...] = out_ref[...].T
 
 
-def arrange(core, pieces, pick):
+def arrange(core, pieces, pick, first, rows):
     groups = pick.shape[0]
-    rows, tall = pieces[0].shape[1:]
+    tall = pieces[0].shape[1]
     kind = pieces[0].dtype
     return core(
-        functools.partial(arrange_kernel, groups, rows, len(pieces)),
+        functools.partial(arrange_kernel, first, rows, groups // len(pieces), len(pieces)),
         "arrange",
         [pltpu.VMEM((groups * rows, tall), kind), pltpu.VMEM((tall, groups * rows), kind)],
         [in_vmem, in_vmem],
@@ -301,7 +303,7 @@
                 made[at] = block.astype(made.dtype)
                 pltpu.make_async_copy(
                     made.at[at], out_ref.at[0, 0, lax.div(entry, 2)], sem
-                ).start()
+                ).start(priority=at % 2)
     pltpu.make_async_copy(made, out_ref.at[0, 0, pl.ds(0, made.shape[0])], sem).wait()
 
 
@@ -319,6 +321,60 @@
         (code, *arrays) + ((before,) if has_before else ()),
         scratch=[pltpu.VMEM((here, blk, blk), jnp.bfloat16), pltpu.SemaphoreType.DMA],
         aliases={1 + len(arrays): 0} if has_before else None,
+    )
+    return out
+
+
+def place_kernel(spots, *refs):
+    blocks = refs[: len(spots)]
+    out_ref, sems = refs[len(spots) :]
+    copies = []
+    for at, (top, first) in enumerate(spots):
+        rows, width = blocks[at].shape
+        target = out_ref.at[pl.ds(top, rows), pl.ds(first, width)]
+        copies.append(pltpu.make_async_copy(blocks[at], target, sems.at[at]))
+        copies[-1].start()
+    for copy in copies:
+        copy.wait()
+
+
+def place_activation(core, blocks, spots, shape):
+    [out] = core(
+        functools.partial(place_kernel, spots),
+        "place_activation",
+        [jax.ShapeDtypeStruct(shape, jnp.bfloat16)],
+        [anywhere],
+        [in_vmem] * len(blocks),
+        blocks,
+        scratch=[pltpu.SemaphoreType.DMA((len(blocks),))],
+    )
+    return out
+
+
+def total_kernel(each, many, starts, sizes, *refs):
+    out_ref = refs[-1]
+    own = sum(sizes)
+    for k, (start, rows) in enumerate(zip(starts, sizes)):
+        found = refs[k * many : (k + 1) * many]
+        for j in range(each):
+            here = slice(j * rows, (j + 1) * rows)
+            total = found[0][here, :]
+            for piece in found[1:]:
+                total = total + piece[here, :].astype(jnp.float32)
+            top = j * own + start
+            out_ref[top : top + rows, :] = total.astype(jnp.bfloat16)
+
+
+def total_input(core, found, each, starts, sizes):
+    arrays = [x for part in found for x in part]
+    shape = (each * sum(sizes), arrays[0].shape[1])
+    [out] = core(
+        functools.partial(total_kernel, each, len(found[0]), starts, sizes),
+        "total_input",
+        [jax.ShapeDtypeStruct(shape, jnp.bfloat16)],
+        [pl.BlockSpec(shape, lambda: (0, 0))],
+        [in_vmem] * len(arrays),
+        arrays,
     )
     return out
 
@@ -361,13 +417,10 @@
     distance = jnp.asarray(everyone.astype(np.int32)) ^ apart
     place = ((distance & 1) * (n_row // 2) + (distance >> 1)).astype(jnp.int32)
 
-    pieces = []
-    for start, rows in zip(starts, sizes):
-        mine = tokens.reshape(col_groups, row_tokens, tall)[:, start : start + rows]
-        if direct:
-            pieces.append([mine] + [swap(mine, "col", n_col, m) for m in range(1, n_col)])
-        else:
-            pieces.append([lax.all_gather(mine, "col", axis=0, tiled=True)])
+    if direct:
+        pieces = [tokens] + [swap(tokens, "col", n_col, m) for m in range(1, n_col)]
+    else:
+        pieces = [lax.all_gather(tokens, "col", axis=0, tiled=True)]
     weight = dense_tile(core, w_packed, code, row_blocks, col_blocks)
 
     far_bits = [1 << b for b in range(1, n_row.bit_length() - 1)]
@@ -379,7 +432,7 @@
 
     def begin(k, c, path):
         if c == 0:
-            full[k], turned[k] = arrange(core, pieces[k], pick)
+            full[k], turned[k] = arrange(core, pieces, pick, starts[k], sizes[k])
         keep, send = forward(core, full[k], weight, c * width, width)
         state[k, c] = (keep, swap(send, "row", n_row, 1))
 
@@ -405,28 +458,29 @@
         )
         sums[k, c] = found[0]
         if last and direct:
-            total = found[0]
-            for m in range(1, n_col):
-                total = total + swap(found[m], "col", n_col, m).astype(jnp.float32)
+            input_grads[k] = [found[0]]
+            input_grads[k] += [swap(found[m], "col", n_col, m) for m in range(1, n_col)]
         elif last:
             total = found[0].reshape(n_col, col_groups * sizes[k], tall)
             total = lax.psum_scatter(total, "col", scatter_dimension=0, tiled=True)[0]
-        if last:
-            total = total.astype(jnp.bfloat16)
-            input_grads[k] = total.reshape(col_groups, sizes[k], tall)
+            input_grads[k] = [total]
 
     hops = len(far_bits)
     stages = [begin] + [functools.partial(add, at) for at in range(hops)] + [bend]
     stages += [functools.partial(join, at) for at in reversed(range(hops))] + [finish]
-    plan = []
+    plan = [(k, at) for at in range(len(stages)) for k in range(parts)]
     if parts == 2 and hops == 2:
-        plan = [(0, 0), (0, 1), (1, 0), (1, 1), (0, 2), (1, 2), (0, 3), (1, 3), (0, 4), (1, 4)]
-        plan += [(0, 5), (0, 6), (1, 5), (1, 6)]
-    else:
-        plan = [(k, at) for at in range(len(stages)) for k in range(parts)]
+        plan = [(0, 0), (1, 0), (0, 1), (1, 1), (0, 2), (1, 2), (0, 3), (1, 3), (0, 4), (1, 4), (0, 5), (1, 5), (0, 6), (1, 6)]
     for k, at in plan:
         for c in range(slabs):
             stages[at](k, c, paths[units.index((k, c))])
+        if (k, at) == (parts - 1, len(stages) - 3):
+            activation = place_activation(
+                core,
+                [activations[k, c] for k, c in units],
+                [(starts[k], c * width) for k, c in units],
+                grad_act.shape,
+            )
     weight_grad = None
     for c in range(slabs):
         weight_grad = weight_gradient(
@@ -440,11 +494,9 @@
             blk,
             weight_grad,
         )
-    activation = jnp.concatenate(
-        [jnp.concatenate([activations[k, c] for c in range(slabs)], axis=1) for k in range(parts)],
-        axis=0,
-    )
-    input_grad = jnp.concatenate([input_grads[k] for k in range(parts)], axis=1).reshape(tokens.shape)
+    input_grad = total_input(
+        core, [input_grads[k] for k in range(parts)], col_groups, starts, sizes
+    )
     return (activation, input_grad, weight_grad)
 
 

time: 149 us -> 142 us (0.953); the launches traced: 146 us -> 141 us
  local copies, waits for them, and re-layouts: 1.8 us -> 10.7 us
  waiting for transfers between devices: 53 us -> 47.5 us
  Pallas kernels: 48.3 us -> 44.8 us
  starting transfers between devices: 38.8 us -> 35.7 us
  other arithmetic: 2.75 us -> 0.9 us
    unnamed x4 -> x18, local copies, waits for them, and re-layouts: 0.01 us -> 10.7 us
    ppermute x36 -> x33, waiting for transfers between devices: 53 us -> 47.5 us  [swap(): return lax.ppermute(array, axis, [(i, i ^ bit) for i in range(size)])]
    pallas_call x33 -> x35, Pallas kernels: 48.3 us -> 44.8 us  [__call__(): pl.pallas_call(body, out_shape=[*out_shape, pltpu.VMEM((8, 128), jnp.floa...]
    ppermute x36 -> x33, starting transfers between devices: 38.8 us -> 35.7 us  [swap(): return lax.ppermute(array, axis, [(i, i ^ bit) for i in range(size)])]
    slice x2 -> x0, local copies, waits for them, and re-layouts: 1.79 us -> none  [on_device(): mine = tokens.reshape(col_groups, row_tokens, tall)[:, start:start + rows]]
    concatenate x2 -> x0, other arithmetic: 1.71 us -> none  [the longest x1 0.99 us: on_device(): jnp.concatenate([jnp.concatenate([activations[k, c] for c in range(slabs)...]
  transfers between devices with their start and end apart: 36 -> 33, of which waited for: 13 -> 12; matrix products, arithmetic and copies ran while one was open for 2% -> 1% of each run, Pallas kernels for 30% -> 29%
where the time goes in v3:
time: 142 us; the launch traced here: 141 us
  waiting for transfers between devices  47.5 us (33%)
  Pallas kernels  44.8 us (32%)
  starting transfers between devices  35.7 us (25%)
  local copies, waits for them, and re-layouts  10.7 us (8%)
  between operations  1.71 us (1%)
    ppermute x33, waiting for transfers between devices, swap(): return lax.ppermute(array, axis, [(i, i ^ bit) for i in range(size)])  47.5 us
    pallas_call x35, Pallas kernels, __call__(): pl.pallas_call(body, out_shape=[*out_shape, pltpu.VMEM((8, 128), jnp.floa...  44.8 us
    ppermute x33, starting transfers between devices, swap(): return lax.ppermute(array, axis, [(i, i ^ bit) for i in range(size)])  35.7 us
    unnamed x18, local copies, waits for them, and re-layouts  10.7 us
  transfers between devices with their start and end apart: 33, of which 12 were waited for; matrix products, arithmetic and copies ran while one was open for 1% of the time, Pallas kernels for 29%

profile of v3, /device:TPU:0, one launch (start us, length us, event | category | flops | bytes accessed | tf_op | source)
XLA Modules:
  0.0 141.3 jit_solution(9535995458790574367)
XLA Ops:
  0.7 5.1 %collective-permute-start.2 = (bf16[128,1024]{1,0:T(8,128)(2,1)}, bf16[128,1024]{1,0:T(8,128)(2,1)S(1)}, u32[]{:S(2)}, u32[]{:S(2)}) collective-permute-start(bf16[128,1024]{1,0:T(8,128)(2,1)} %refs_1_.5), channel_id=1, source_target_pairs={{0,3},{1,2},{2,1},{3,0},{4,7},{5,6},{6,5},{7,4},{8,11},{9,10},{10,... | collective-permute-start | bytes 786440 | tf_op jit(solution)/shard_map/ppermute | solution.py:383
  8.0 7.4 %dense_tile.1 = (bf16[1024,7168]{1,0:T(8,128)(2,1)S(1)}, f32[8,128]{1,0:T(8,128)S(1)}) custom-call(s32[448]{0:T(512)S(1)} %select_reduce_fusion.refs_0_, bf16[1,1,448,128,128]{4,3,2,1,0:T(8,128)(2,1)} %refs_1_.3), custom_call_target="tpu_custom_call" | custom-call | flops 1 | bytes 1 | tf_op jit(solution)/shard_map/dense_tile/pallas_call | solution.py:58
  15.4 5.5 %copy-done = bf16[1024,7168]{1,0:T(8,128)(2,1)} copy-done((bf16[1024,7168]{1,0:T(8,128)(2,1)}, bf16[1024,7168]{1,0:T(8,128)(2,1)S(1)}, u32[]{:S(2)}) %copy-start) | copy-done | bytes 14680088
  20.9 7.4 %collective-permute-done.1.refs_3_ = bf16[128,1024]{1,0:T(8,128)(2,1)S(1)} collective-permute-done((bf16[128,1024]{1,0:T(8,128)(2,1)}, bf16[128,1024]{1,0:T(8,128)(2,1)S(1)}, u32[]{:S(2)}, u32[]{:S(2)}) %collective-permute-start.1) | collective-permute-done | bytes 262176 | tf_op jit(solution)/shard_map/ppermute | solution.py:383
  29.1 5.2 %copy-done.1 = bf16[1024,7168]{1,0:T(8,128)(2,1)S(1)} copy-done((bf16[1024,7168]{1,0:T(8,128)(2,1)S(1)}, bf16[1024,7168]{1,0:T(8,128)(2,1)}, u32[]{:S(2)}) %copy-start.1) | copy-done | bytes 14680088
  34.3 2.1 %forward.4 = (f32[128,3584]{1,0:T(8,128)S(1)}, bf16[128,3584]{1,0:T(8,128)(2,1)S(1)}, f32[8,128]{1,0:T(8,128)S(1)}) custom-call(bf16[256,1024]{1,0:T(8,128)(2,1)S(1)} %get-tuple-element.97.refs_0_, bf16[1024,7168]{1,0:T(8,128)(2,1)S(1)} %copy-done.1, f32[8,128]{1,0:T(8,128)S(1)} %get-tuple-element.99.refs_2_), custom_call_target="tpu_custom_call" | custom-call | flops 1 | bytes 1 | tf_op jit(solution)/shard_map/forward/pallas_call | solution.py:58
  36.5 2.1 %forward.5 = (f32[128,3584]{1,0:T(8,128)S(1)}, bf16[128,3584]{1,0:T(8,128)(2,1)S(1)}, f32[8,128]{1,0:T(8,128)S(1)}) custom-call(bf16[256,1024]{1,0:T(8,128)(2,1)S(1)} %get-tuple-element.97.refs_0_, bf16[1024,7168]{1,0:T(8,128)(2,1)S(1)} %copy-done.1, f32[8,128]{1,0:T(8,128)S(1)} %get-tuple-element.102.refs_2_), custom_call_target="tpu_custom_call" | custom-call | flops 1 | bytes 1 | tf_op jit(solution)/shard_map/forward/pallas_call | solution.py:58
  40.0 2.1 %forward.6 = (f32[128,3584]{1,0:T(8,128)S(1)}, bf16[128,3584]{1,0:T(8,128)(2,1)S(1)}, f32[8,128]{1,0:T(8,128)S(1)}) custom-call(bf16[256,1024]{1,0:T(8,128)(2,1)S(1)} %get-tuple-element.104.refs_0_, bf16[1024,7168]{1,0:T(8,128)(2,1)S(1)} %bitcast.4, f32[8,128]{1,0:T(8,128)S(1)} %get-tuple-element.105.refs_2_), custom_call_target="tpu_custom_call" | custom-call | flops 1 | bytes 1 | tf_op jit(solution)/shard_map/forward/pallas_call | solution.py:58
  42.2 2.1 %forward.7 = (f32[128,3584]{1,0:T(8,128)S(1)}, bf16[128,3584]{1,0:T(8,128)(2,1)S(1)}, f32[8,128]{1,0:T(8,128)S(1)}) custom-call(bf16[256,1024]{1,0:T(8,128)(2,1)S(1)} %get-tuple-element.104.refs_0_, bf16[1024,7168]{1,0:T(8,128)(2,1)S(1)} %bitcast.4, f32[8,128]{1,0:T(8,128)S(1)} %get-tuple-element.106.refs_2_), custom_call_target="tpu_custom_call" | custom-call | flops 1 | bytes 1 | tf_op jit(solution)/shard_map/forward/pallas_call | solution.py:58
  45.0 1.6 %collective-permute-start.4 = (bf16[64,3584]{1,0:T(8,128)(2,1)S(1)}, bf16[64,3584]{1,0:T(8,128)(2,1)S(1)}, u32[]{:S(2)}, u32[]{:S(2)}) collective-permute-start(bf16[64,3584]{1,0:T(8,128)(2,1)S(1)} %get-tuple-element.109), channel_id=1, source_target_pairs={{0,8},{4,12},{8,0},{12,4},{16,24},{20,28},{24,16},{28,20},{1,9},{5... | collective-permute-start | bytes 1376264 | tf_op jit(solution)/shard_map/ppermute | solution.py:383
  46.8 1.6 %collective-permute-start.11 = (bf16[64,3584]{1,0:T(8,128)(2,1)S(1)}, bf16[64,3584]{1,0:T(8,128)(2,1)S(1)}, u32[]{:S(2)}, u32[]{:S(2)}) collective-permute-start(bf16[64,3584]{1,0:T(8,128)(2,1)S(1)} %get-tuple-element.127), channel_id=1, source_target_pairs={{0,16},{4,20},{8,24},{12,28},{16,0},{20,4},{24,8},{28,12},{1,17},{... | collective-permute-start | bytes 1376264 | tf_op jit(solution)/shard_map/ppermute | solution.py:383
  49.9 8.5 %collective-permute-done.4.refs_1_ = bf16[64,3584]{1,0:T(8,128)(2,1)S(1)} collective-permute-done((bf16[64,3584]{1,0:T(8,128)(2,1)S(1)}, bf16[64,3584]{1,0:T(8,128)(2,1)S(1)}, u32[]{:S(2)}, u32[]{:S(2)}) %collective-permute-start.4) | collective-permute-done | bytes 458784 | tf_op jit(solution)/shard_map/ppermute | solution.py:383
  58.5 1.6 %collective-permute-start.8 = (bf16[32,3584]{1,0:T(8,128)(2,1)S(1)}, bf16[32,3584]{1,0:T(8,128)(2,1)S(1)}, u32[]{:S(2)}, u32[]{:S(2)}) collective-permute-start(bf16[32,3584]{1,0:T(8,128)(2,1)S(1)} %get-tuple-element.121), channel_id=1, source_target_pairs={{0,16},{4,20},{8,24},{12,28},{16,0},{20,4},{24,8},{28,12},{1,17},{... | collective-permute-start | bytes 688136 | tf_op jit(solution)/shard_map/ppermute | solution.py:383
  61.8 6.5 %collective-permute-done.10.refs_1_ = bf16[64,3584]{1,0:T(8,128)(2,1)S(1)} collective-permute-done((bf16[64,3584]{1,0:T(8,128)(2,1)S(1)}, bf16[64,3584]{1,0:T(8,128)(2,1)S(1)}, u32[]{:S(2)}, u32[]{:S(2)}) %collective-permute-start.10) | collective-permute-done | bytes 458784 | tf_op jit(solution)/shard_map/ppermute | solution.py:383
  68.4 1.6 %collective-permute-start.13 = (bf16[32,3584]{1,0:T(8,128)(2,1)S(1)}, bf16[32,3584]{1,0:T(8,128)(2,1)S(1)}, u32[]{:S(2)}, u32[]{:S(2)}) collective-permute-start(bf16[32,3584]{1,0:T(8,128)(2,1)S(1)} %get-tuple-element.138), channel_id=1, source_target_pairs={{0,16},{4,20},{8,24},{12,28},{16,0},{20,4},{24,8},{28,12},{1,17},{... | collective-permute-start | bytes 688136 | tf_op jit(solution)/shard_map/ppermute | solution.py:383
  71.6 3.4 %collective-permute-done.8.refs_1_ = bf16[32,3584]{1,0:T(8,128)(2,1)S(1)} collective-permute-done((bf16[32,3584]{1,0:T(8,128)(2,1)S(1)}, bf16[32,3584]{1,0:T(8,128)(2,1)S(1)}, u32[]{:S(2)}, u32[]{:S(2)}) %collective-permute-start.8) | collective-permute-done | bytes 229408 | tf_op jit(solution)/shard_map/ppermute | solution.py:383
  75.4 1.6 %collective-permute-start.18 = (bf16[32,3584]{1,0:T(8,128)(2,1)S(1)}, bf16[32,3584]{1,0:T(8,128)(2,1)S(1)}, u32[]{:S(2)}, u32[]{:S(2)}) collective-permute-start(bf16[32,3584]{1,0:T(8,128)(2,1)S(1)} %get-tuple-element.148.refs_0_), channel_id=1, source_target_pairs={{0,16},{4,20},{8,24},{12,28},{16,0},{20,4},{24,8},{28,12},{1,17},{... | collective-permute-start | bytes 688136 | tf_op jit(solution)/shard_map/ppermute | solution.py:383
  78.0 1.9 %collective-permute-done.13.refs_1_ = bf16[32,3584]{1,0:T(8,128)(2,1)S(1)} collective-permute-done((bf16[32,3584]{1,0:T(8,128)(2,1)S(1)}, bf16[32,3584]{1,0:T(8,128)(2,1)S(1)}, u32[]{:S(2)}, u32[]{:S(2)}) %collective-permute-start.13) | collective-permute-done | bytes 229408 | tf_op jit(solution)/shard_map/ppermute | solution.py:383
  80.3 1.6 %collective-permute-start.16 = (bf16[32,3584]{1,0:T(8,128)(2,1)S(1)}, bf16[32,3584]{1,0:T(8,128)(2,1)S(1)}, u32[]{:S(2)}, u32[]{:S(2)}) collective-permute-start(bf16[32,3584]{1,0:T(8,128)(2,1)S(1)} %get-tuple-element.146.refs_0_), channel_id=1, source_target_pairs={{0,16},{4,20},{8,24},{12,28},{16,0},{20,4},{24,8},{28,12},{1,17},{... | collective-permute-start | bytes 688136 | tf_op jit(solution)/shard_map/ppermute | solution.py:383
  82.9 1.9 %collective-permute-done.18.refs_1_ = bf16[32,3584]{1,0:T(8,128)(2,1)S(1)} collective-permute-done((bf16[32,3584]{1,0:T(8,128)(2,1)S(1)}, bf16[32,3584]{1,0:T(8,128)(2,1)S(1)}, u32[]{:S(2)}, u32[]{:S(2)}) %collective-permute-start.18) | collective-permute-done | bytes 229408 | tf_op jit(solution)/shard_map/ppermute | solution.py:383
  85.5 1.6 %collective-permute-start.19 = (bf16[64,3584]{1,0:T(8,128)(2,1)S(1)}, bf16[64,3584]{1,0:T(8,128)(2,1)S(1)}, u32[]{:S(2)}, u32[]{:S(2)}) collective-permute-start(bf16[64,3584]{1,0:T(8,128)(2,1)S(1)} %get-tuple-element.155.refs_0_), channel_id=1, source_target_pairs={{0,16},{4,20},{8,24},{12,28},{16,0},{20,4},{24,8},{28,12},{1,17},{... | collective-permute-start | bytes 1376264 | tf_op jit(solution)/shard_map/ppermute | solution.py:383
  87.1 2.7 %collective-permute-done.16.refs_1_ = bf16[32,3584]{1,0:T(8,128)(2,1)S(1)} collective-permute-done((bf16[32,3584]{1,0:T(8,128)(2,1)S(1)}, bf16[32,3584]{1,0:T(8,128)(2,1)S(1)}, u32[]{:S(2)}, u32[]{:S(2)}) %collective-permute-start.16) | collective-permute-done | bytes 229408 | tf_op jit(solution)/shard_map/ppermute | solution.py:383
  93.0 7.8 %collective-permute-done.20.refs_1_ = bf16[64,3584]{1,0:T(8,128)(2,1)S(1)} collective-permute-done((bf16[64,3584]{1,0:T(8,128)(2,1)S(1)}, bf16[64,3584]{1,0:T(8,128)(2,1)S(1)}, u32[]{:S(2)}, u32[]{:S(2)}) %collective-permute-start.20) | collective-permute-done | bytes 458784 | tf_op jit(solution)/shard_map/ppermute | solution.py:383
  101.5 6.5 %collective-permute-done.24.refs_1_ = bf16[64,3584]{1,0:T(8,128)(2,1)S(1)} collective-permute-done((bf16[64,3584]{1,0:T(8,128)(2,1)S(1)}, bf16[64,3584]{1,0:T(8,128)(2,1)S(1)}, u32[]{:S(2)}, u32[]{:S(2)}) %collective-permute-start.24) | collective-permute-done | bytes 458784 | tf_op jit(solution)/shard_map/ppermute | solution.py:383
  108.8 2.8 %input_partial.4 = (f32[1024,256]{1,0:T(8,128)S(1)}, f32[8,128]{1,0:T(8,128)S(1)}) custom-call(s32[8]{0:T(128)S(1)} %shift-right-arithmetic_add_fusion.refs_0_, bf16[128,3584]{1,0:T(8,128)(2,1)S(1)} %get-tuple-element.160.refs_1_.refs_3_, bf16[128,3584]{1,0:T(8,128)(2,1)S(1)} %collective-permute-done.22.refs_2_.refs_4_, bf16[1024,7168]{1,0:T(8,128)(2,1)S(1)} %bitcast.4, ...), custom_call_target="tpu_custom_call" | custom-call | flops 1 | bytes 1 | tf_op jit(solution)/shard_map/input_partial/pallas_call | solution.py:58
  111.7 2.9 %input_partial.5 = (f32[64,1024]{1,0:T(8,128)S(1)}, bf16[64,1024]{1,0:T(8,128)(2,1)S(1)}, bf16[64,1024]{1,0:T(8,128)(2,1)S(1)}, bf16[64,1024]{1,0:T(8,128)(2,1)S(1)}, f32[8,128]{1,0:T(8,128)S(1)}) custom-call(s32[8]{0:T(128)S(1)} %shift-right-arithmetic_add_fusion.refs_0_, bf16[128,3584]{1,0:T(8,128)(2,1)S(1)} %get-tuple-element.159.refs_1_.refs_3_, ...), custom_call_target="tpu_custom_call" | custom-call | flops 1 | bytes 1 | tf_op jit(solution)/shard_map/input_partial/pallas_call | solution.py:58
  114.7 3.0 %collective-permute-start.26 = (bf16[64,1024]{1,0:T(8,128)(2,1)S(1)}, bf16[64,1024]{1,0:T(8,128)(2,1)S(1)}, u32[]{:S(2)}, u32[]{:S(2)}) collective-permute-start(bf16[64,1024]{1,0:T(8,128)(2,1)S(1)} %get-tuple-element.170), channel_id=1, source_target_pairs={{0,2},{1,3},{2,0},{3,1},{4,6},{5,7},{6,4},{7,5},{8,10},{9,11},{10,... | collective-permute-start | bytes 393224 | tf_op jit(solution)/shard_map/ppermute | solution.py:383
  119.1 2.7 %input_partial.6 = (f32[1024,256]{1,0:T(8,128)S(1)}, f32[8,128]{1,0:T(8,128)S(1)}) custom-call(s32[8]{0:T(128)S(1)} %shift-right-arithmetic_add_fusion.refs_0_, bf16[128,3584]{1,0:T(8,128)(2,1)S(1)} %get-tuple-element.173.refs_1_.refs_5_, bf16[128,3584]{1,0:T(8,128)(2,1)S(1)} %collective-permute-done.29.refs_2_.refs_6_, bf16[1024,7168]{1,0:T(8,128)(2,1)S(1)} %bitcast.4, ...), custom_call_target="tpu_custom_call" | custom-call | flops 1 | bytes 1 | tf_op jit(solution)/shard_map/input_partial/pallas_call | solution.py:58
  121.7 2.9 %input_partial.7 = (f32[64,1024]{1,0:T(8,128)S(1)}, bf16[64,1024]{1,0:T(8,128)(2,1)S(1)}, bf16[64,1024]{1,0:T(8,128)(2,1)S(1)}, bf16[64,1024]{1,0:T(8,128)(2,1)S(1)}, f32[8,128]{1,0:T(8,128)S(1)}) custom-call(s32[8]{0:T(128)S(1)} %shift-right-arithmetic_add_fusion.refs_0_, bf16[128,3584]{1,0:T(8,128)(2,1)S(1)} %get-tuple-element.172.refs_1_.refs_5_, ...), custom_call_target="tpu_custom_call" | custom-call | flops 1 | bytes 1 | tf_op jit(solution)/shard_map/input_partial/pallas_call | solution.py:58
  124.7 3.0 %collective-permute-start.31 = (bf16[64,1024]{1,0:T(8,128)(2,1)S(1)}, bf16[64,1024]{1,0:T(8,128)(2,1)S(1)}, u32[]{:S(2)}, u32[]{:S(2)}) collective-permute-start(bf16[64,1024]{1,0:T(8,128)(2,1)S(1)} %get-tuple-element.179), channel_id=1, source_target_pairs={{0,2},{1,3},{2,0},{3,1},{4,6},{5,7},{6,4},{7,5},{8,10},{9,11},{10,... | collective-permute-start | bytes 393224 | tf_op jit(solution)/shard_map/ppermute | solution.py:383
  129.1 5.6 %weight_gradient.2 = (bf16[1,1,448,128,128]{4,3,2,1,0:T(8,128)(2,1)}, f32[8,128]{1,0:T(8,128)S(1)}) custom-call(s32[448]{0:T(512)S(1)} %select_reduce_fusion.refs_0_, bf16[1024,256]{1,0:T(8,128)(2,1)S(1)} %get-tuple-element.181.refs_1_, bf16[1024,256]{1,0:T(8,128)(2,1)S(1)} %get-tuple-element.182.refs_2_, ...), custom_call_target="tpu_custom_call" | custom-call | flops 1 | bytes 1 | tf_op jit(solution)/shard_map/weight_gradient/pallas_call | solution.py:58
  134.7 5.6 %weight_gradient.3 = (bf16[1,1,448,128,128]{4,3,2,1,0:T(8,128)(2,1)}, f32[8,128]{1,0:T(8,128)S(1)}) custom-call(s32[448]{0:T(512)S(1)} %select_reduce_fusion.refs_0_, bf16[1024,256]{1,0:T(8,128)(2,1)S(1)} %get-tuple-element.181.refs_1_, bf16[1024,256]{1,0:T(8,128)(2,1)S(1)} %get-tuple-element.182.refs_2_, ...), custom_call_target="tpu_custom_call", output_to_operand_aliasing={{0}: (7, {})} | custom-call | flops 1 | bytes 1 | tf_op jit(solution)/shard_map/weight_gradient/pallas_call | solution.py:58
  (93 shorter events, 21.6 us)
Async XLA Ops:
  0.7 20.2 %collective-permute-start.2 = (bf16[128,1024]{1,0:T(8,128)(2,1)}, bf16[128,1024]{1,0:T(8,128)(2,1)S(1)}, u32[]{:S(2)}, u32[]{:S(2)}) collective-permute-start(bf16[128,1024]{1,0:T(8,128)(2,1)} %refs_1_.5), channel_id=1, source_target_pairs={{0,3},{1,2},{2,1},{3,0},{4,7},{5,6},{6,5},{7,4},{8,11},{9,10},{10,... | collective-permute-start | bytes 786440 | tf_op jit(solution)/shard_map/ppermute | solution.py:383
  5.8 22.5 %collective-permute-start.1 = (bf16[128,1024]{1,0:T(8,128)(2,1)}, bf16[128,1024]{1,0:T(8,128)(2,1)S(1)}, u32[]{:S(2)}, u32[]{:S(2)}) collective-permute-start(bf16[128,1024]{1,0:T(8,128)(2,1)} %refs_1_.5), channel_id=1, source_target_pairs={{0,2},{1,3},{2,0},{3,1},{4,6},{5,7},{6,4},{7,5},{8,10},{9,11},{10,... | collective-permute-start | bytes 786440 | tf_op jit(solution)/shard_map/ppermute | solution.py:383
  5.8 22.5 %collective-permute-start = (bf16[128,1024]{1,0:T(8,128)(2,1)}, bf16[128,1024]{1,0:T(8,128)(2,1)S(1)}, u32[]{:S(2)}, u32[]{:S(2)}) collective-permute-start(bf16[128,1024]{1,0:T(8,128)(2,1)} %refs_1_.5), channel_id=1, source_target_pairs={{0,1},{1,0},{2,3},{3,2},{4,5},{5,4},{6,7},{7,6},{8,9},{9,8},{10,11... | collective-permute-start | bytes 786440 | tf_op jit(solution)/shard_map/ppermute | solution.py:383
  36.4 8.5 %collective-permute-start.3 = (bf16[128,3584]{1,0:T(8,128)(2,1)S(1)}, bf16[128,3584]{1,0:T(8,128)(2,1)S(1)}, u32[]{:S(2)}, u32[]{:S(2)}) collective-permute-start(bf16[128,3584]{1,0:T(8,128)(2,1)S(1)} %get-tuple-element.101), channel_id=1, source_target_pairs={{0,4},{4,0},{8,12},{12,8},{16,20},{20,16},{24,28},{28,24},{1,5},{5... | collective-permute-start | bytes 2752520 | tf_op jit(solution)/shard_map/ppermute | solution.py:383
  38.6 8.0 %collective-permute-start.7 = (bf16[128,3584]{1,0:T(8,128)(2,1)S(1)}, bf16[128,3584]{1,0:T(8,128)(2,1)S(1)}, u32[]{:S(2)}, u32[]{:S(2)}) collective-permute-start(bf16[128,3584]{1,0:T(8,128)(2,1)S(1)} %get-tuple-element.115), channel_id=1, source_target_pairs={{0,4},{4,0},{8,12},{12,8},{16,20},{20,16},{24,28},{28,24},{1,5},{5... | collective-permute-start | bytes 2752520 | tf_op jit(solution)/shard_map/ppermute | solution.py:383
  42.1 6.3 %collective-permute-start.6 = (bf16[128,3584]{1,0:T(8,128)(2,1)S(1)}, bf16[128,3584]{1,0:T(8,128)(2,1)S(1)}, u32[]{:S(2)}, u32[]{:S(2)}) collective-permute-start(bf16[128,3584]{1,0:T(8,128)(2,1)S(1)} %get-tuple-element.113), channel_id=1, source_target_pairs={{0,4},{4,0},{8,12},{12,8},{16,20},{20,16},{24,28},{28,24},{1,5},{5... | collective-permute-start | bytes 2752520 | tf_op jit(solution)/shard_map/ppermute | solution.py:383
  45.0 13.4 %collective-permute-start.4 = (bf16[64,3584]{1,0:T(8,128)(2,1)S(1)}, bf16[64,3584]{1,0:T(8,128)(2,1)S(1)}, u32[]{:S(2)}, u32[]{:S(2)}) collective-permute-start(bf16[64,3584]{1,0:T(8,128)(2,1)S(1)} %get-tuple-element.109), channel_id=1, source_target_pairs={{0,8},{4,12},{8,0},{12,4},{16,24},{20,28},{24,16},{28,20},{1,9},{5... | collective-permute-start | bytes 1376264 | tf_op jit(solution)/shard_map/ppermute | solution.py:383
  46.8 13.5 %collective-permute-start.11 = (bf16[64,3584]{1,0:T(8,128)(2,1)S(1)}, bf16[64,3584]{1,0:T(8,128)(2,1)S(1)}, u32[]{:S(2)}, u32[]{:S(2)}) collective-permute-start(bf16[64,3584]{1,0:T(8,128)(2,1)S(1)} %get-tuple-element.127), channel_id=1, source_target_pairs={{0,16},{4,20},{8,24},{12,28},{16,0},{20,4},{24,8},{28,12},{1,17},{... | collective-permute-start | bytes 1376264 | tf_op jit(solution)/shard_map/ppermute | solution.py:383
  48.5 19.8 %collective-permute-start.10 = (bf16[64,3584]{1,0:T(8,128)(2,1)S(1)}, bf16[64,3584]{1,0:T(8,128)(2,1)S(1)}, u32[]{:S(2)}, u32[]{:S(2)}) collective-permute-start(bf16[64,3584]{1,0:T(8,128)(2,1)S(1)} %get-tuple-element.125), channel_id=1, source_target_pairs={{0,8},{4,12},{8,0},{12,4},{16,24},{20,28},{24,16},{28,20},{1,9},{5... | collective-permute-start | bytes 1376264 | tf_op jit(solution)/shard_map/ppermute | solution.py:383
  49.3 20.8 %collective-permute-start.9 = (bf16[64,3584]{1,0:T(8,128)(2,1)S(1)}, bf16[64,3584]{1,0:T(8,128)(2,1)S(1)}, u32[]{:S(2)}, u32[]{:S(2)}) collective-permute-start(bf16[64,3584]{1,0:T(8,128)(2,1)S(1)} %get-tuple-element.123), channel_id=1, source_target_pairs={{0,16},{4,20},{8,24},{12,28},{16,0},{20,4},{24,8},{28,12},{1,17},{... | collective-permute-start | bytes 1376264 | tf_op jit(solution)/shard_map/ppermute | solution.py:383
  58.5 16.5 %collective-permute-start.8 = (bf16[32,3584]{1,0:T(8,128)(2,1)S(1)}, bf16[32,3584]{1,0:T(8,128)(2,1)S(1)}, u32[]{:S(2)}, u32[]{:S(2)}) collective-permute-start(bf16[32,3584]{1,0:T(8,128)(2,1)S(1)} %get-tuple-element.121), channel_id=1, source_target_pairs={{0,16},{4,20},{8,24},{12,28},{16,0},{20,4},{24,8},{28,12},{1,17},{... | collective-permute-start | bytes 688136 | tf_op jit(solution)/shard_map/ppermute | solution.py:383
  60.4 16.6 %collective-permute-start.12 = (bf16[32,3584]{1,0:T(8,128)(2,1)S(1)}, bf16[32,3584]{1,0:T(8,128)(2,1)S(1)}, u32[]{:S(2)}, u32[]{:S(2)}) collective-permute-start(bf16[32,3584]{1,0:T(8,128)(2,1)S(1)} %get-tuple-element.134), channel_id=1, source_target_pairs={{0,8},{4,12},{8,0},{12,4},{16,24},{20,28},{24,16},{28,20},{1,9},{5... | collective-permute-start | bytes 688136 | tf_op jit(solution)/shard_map/ppermute | solution.py:383
  68.4 11.6 %collective-permute-start.13 = (bf16[32,3584]{1,0:T(8,128)(2,1)S(1)}, bf16[32,3584]{1,0:T(8,128)(2,1)S(1)}, u32[]{:S(2)}, u32[]{:S(2)}) collective-permute-start(bf16[32,3584]{1,0:T(8,128)(2,1)S(1)} %get-tuple-element.138), channel_id=1, source_target_pairs={{0,16},{4,20},{8,24},{12,28},{16,0},{20,4},{24,8},{28,12},{1,17},{... | collective-permute-start | bytes 688136 | tf_op jit(solution)/shard_map/ppermute | solution.py:383
  70.2 11.7 %collective-permute-start.14 = (bf16[32,3584]{1,0:T(8,128)(2,1)S(1)}, bf16[32,3584]{1,0:T(8,128)(2,1)S(1)}, u32[]{:S(2)}, u32[]{:S(2)}) collective-permute-start(bf16[32,3584]{1,0:T(8,128)(2,1)S(1)} %get-tuple-element.142), channel_id=1, source_target_pairs={{0,8},{4,12},{8,0},{12,4},{16,24},{20,28},{24,16},{28,20},{1,9},{5... | collective-permute-start | bytes 688136 | tf_op jit(solution)/shard_map/ppermute | solution.py:383
  75.4 9.4 %collective-permute-start.18 = (bf16[32,3584]{1,0:T(8,128)(2,1)S(1)}, bf16[32,3584]{1,0:T(8,128)(2,1)S(1)}, u32[]{:S(2)}, u32[]{:S(2)}) collective-permute-start(bf16[32,3584]{1,0:T(8,128)(2,1)S(1)} %get-tuple-element.148.refs_0_), channel_id=1, source_target_pairs={{0,16},{4,20},{8,24},{12,28},{16,0},{20,4},{24,8},{28,12},{1,17},{... | collective-permute-start | bytes 688136 | tf_op jit(solution)/shard_map/ppermute | solution.py:383
  77.4 8.1 %collective-permute-start.17 = (bf16[32,3584]{1,0:T(8,128)(2,1)S(1)}, bf16[32,3584]{1,0:T(8,128)(2,1)S(1)}, u32[]{:S(2)}, u32[]{:S(2)}) collective-permute-start(bf16[32,3584]{1,0:T(8,128)(2,1)S(1)} %get-tuple-element.147.refs_0_), channel_id=1, source_target_pairs={{0,8},{4,12},{8,0},{12,4},{16,24},{20,28},{24,16},{28,20},{1,9},{5... | collective-permute-start | bytes 688136 | tf_op jit(solution)/shard_map/ppermute | solution.py:383
  80.3 9.4 %collective-permute-start.16 = (bf16[32,3584]{1,0:T(8,128)(2,1)S(1)}, bf16[32,3584]{1,0:T(8,128)(2,1)S(1)}, u32[]{:S(2)}, u32[]{:S(2)}) collective-permute-start(bf16[32,3584]{1,0:T(8,128)(2,1)S(1)} %get-tuple-element.146.refs_0_), channel_id=1, source_target_pairs={{0,16},{4,20},{8,24},{12,28},{16,0},{20,4},{24,8},{28,12},{1,17},{... | collective-permute-start | bytes 688136 | tf_op jit(solution)/shard_map/ppermute | solution.py:383
  82.3 8.6 %collective-permute-start.15 = (bf16[32,3584]{1,0:T(8,128)(2,1)S(1)}, bf16[32,3584]{1,0:T(8,128)(2,1)S(1)}, u32[]{:S(2)}, u32[]{:S(2)}) collective-permute-start(bf16[32,3584]{1,0:T(8,128)(2,1)S(1)} %get-tuple-element.145.refs_0_), channel_id=1, source_target_pairs={{0,8},{4,12},{8,0},{12,4},{16,24},{20,28},{24,16},{28,20},{1,9},{5... | collective-permute-start | bytes 688136 | tf_op jit(solution)/shard_map/ppermute | solution.py:383
  84.9 15.9 %collective-permute-start.20 = (bf16[64,3584]{1,0:T(8,128)(2,1)S(1)}, bf16[64,3584]{1,0:T(8,128)(2,1)S(1)}, u32[]{:S(2)}, u32[]{:S(2)}) collective-permute-start(bf16[64,3584]{1,0:T(8,128)(2,1)S(1)} %get-tuple-element.156.refs_0_), channel_id=1, source_target_pairs={{0,8},{4,12},{8,0},{12,4},{16,24},{20,28},{24,16},{28,20},{1,9},{5... | collective-permute-start | bytes 1376264 | tf_op jit(solution)/shard_map/ppermute | solution.py:383
  85.5 15.4 %collective-permute-start.19 = (bf16[64,3584]{1,0:T(8,128)(2,1)S(1)}, bf16[64,3584]{1,0:T(8,128)(2,1)S(1)}, u32[]{:S(2)}, u32[]{:S(2)}) collective-permute-start(bf16[64,3584]{1,0:T(8,128)(2,1)S(1)} %get-tuple-element.155.refs_0_), channel_id=1, source_target_pairs={{0,16},{4,20},{8,24},{12,28},{16,0},{20,4},{24,8},{28,12},{1,17},{... | collective-permute-start | bytes 1376264 | tf_op jit(solution)/shard_map/ppermute | solution.py:383
  89.8 18.3 %collective-permute-start.24 = (bf16[64,3584]{1,0:T(8,128)(2,1)S(1)}, bf16[64,3584]{1,0:T(8,128)(2,1)S(1)}, u32[]{:S(2)}, u32[]{:S(2)}) collective-permute-start(bf16[64,3584]{1,0:T(8,128)(2,1)S(1)} %get-tuple-element.162.refs_0_), channel_id=1, source_target_pairs={{0,8},{4,12},{8,0},{12,4},{16,24},{20,28},{24,16},{28,20},{1,9},{5... | collective-permute-start | bytes 1376264 | tf_op jit(solution)/shard_map/ppermute | solution.py:383
  90.9 17.3 %collective-permute-start.23 = (bf16[64,3584]{1,0:T(8,128)(2,1)S(1)}, bf16[64,3584]{1,0:T(8,128)(2,1)S(1)}, u32[]{:S(2)}, u32[]{:S(2)}) collective-permute-start(bf16[64,3584]{1,0:T(8,128)(2,1)S(1)} %get-tuple-element.161.refs_0_), channel_id=1, source_target_pairs={{0,16},{4,20},{8,24},{12,28},{16,0},{20,4},{24,8},{28,12},{1,17},{... | collective-permute-start | bytes 1376264 | tf_op jit(solution)/shard_map/ppermute | solution.py:383
  100.8 8.0 %collective-permute-start.22 = (bf16[128,3584]{1,0:T(8,128)(2,1)S(1)}, bf16[128,3584]{1,0:T(8,128)(2,1)S(1)}, u32[]{:S(2)}, u32[]{:S(2)}) collective-permute-start(bf16[128,3584]{1,0:T(8,128)(2,1)S(1)} %get-tuple-element.160.refs_1_.refs_3_), channel_id=1, source_target_pairs={{0,4},{4,0},{8,12},{12,8},{16,20},{20,16},{24,28},{28,24},{1,5},{5... | collective-permute-start | bytes 2752520 | tf_op jit(solution)/shard_map/ppermute | solution.py:383
  101.0 10.7 %collective-permute-start.21 = (bf16[128,3584]{1,0:T(8,128)(2,1)S(1)}, bf16[128,3584]{1,0:T(8,128)(2,1)S(1)}, u32[]{:S(2)}, u32[]{:S(2)}) collective-permute-start(bf16[128,3584]{1,0:T(8,128)(2,1)S(1)} %get-tuple-element.159.refs_1_.refs_3_), channel_id=1, source_target_pairs={{0,4},{4,0},{8,12},{12,8},{16,20},{20,16},{24,28},{28,24},{1,5},{5... | collective-permute-start | bytes 2752520 | tf_op jit(solution)/shard_map/ppermute | solution.py:383
  108.1 10.9 %collective-permute-start.29 = (bf16[128,3584]{1,0:T(8,128)(2,1)S(1)}, bf16[128,3584]{1,0:T(8,128)(2,1)S(1)}, u32[]{:S(2)}, u32[]{:S(2)}) collective-permute-start(bf16[128,3584]{1,0:T(8,128)(2,1)S(1)} %get-tuple-element.173.refs_1_.refs_5_), channel_id=1, source_target_pairs={{0,4},{4,0},{8,12},{12,8},{16,20},{20,16},{24,28},{28,24},{1,5},{5... | collective-permute-start | bytes 2752520 | tf_op jit(solution)/shard_map/ppermute | solution.py:383
  108.3 13.5 %collective-permute-start.28 = (bf16[128,3584]{1,0:T(8,128)(2,1)S(1)}, bf16[128,3584]{1,0:T(8,128)(2,1)S(1)}, u32[]{:S(2)}, u32[]{:S(2)}) collective-permute-start(bf16[128,3584]{1,0:T(8,128)(2,1)S(1)} %get-tuple-element.172.refs_1_.refs_5_), channel_id=1, source_target_pairs={{0,4},{4,0},{8,12},{12,8},{16,20},{20,16},{24,28},{28,24},{1,5},{5... | collective-permute-start | bytes 2752520 | tf_op jit(solution)/shard_map/ppermute | solution.py:383
  114.6 13.2 %collective-permute-start.25 = (bf16[64,1024]{1,0:T(8,128)(2,1)S(1)}, bf16[64,1024]{1,0:T(8,128)(2,1)S(1)}, u32[]{:S(2)}, u32[]{:S(2)}) collective-permute-start(bf16[64,1024]{1,0:T(8,128)(2,1)S(1)} %get-tuple-element.169), channel_id=1, source_target_pairs={{0,1},{1,0},{2,3},{3,2},{4,5},{5,4},{6,7},{7,6},{8,9},{9,8},{10,11... | collective-permute-start | bytes 393224 | tf_op jit(solution)/shard_map/ppermute | solution.py:383
  114.7 25.7 %collective-permute-start.26 = (bf16[64,1024]{1,0:T(8,128)(2,1)S(1)}, bf16[64,1024]{1,0:T(8,128)(2,1)S(1)}, u32[]{:S(2)}, u32[]{:S(2)}) collective-permute-start(bf16[64,1024]{1,0:T(8,128)(2,1)S(1)} %get-tuple-element.170), channel_id=1, source_target_pairs={{0,2},{1,3},{2,0},{3,1},{4,6},{5,7},{6,4},{7,5},{8,10},{9,11},{10,... | collective-permute-start | bytes 393224 | tf_op jit(solution)/shard_map/ppermute | solution.py:383
  117.7 22.7 %collective-permute-start.27 = (bf16[64,1024]{1,0:T(8,128)(2,1)S(1)}, bf16[64,1024]{1,0:T(8,128)(2,1)S(1)}, u32[]{:S(2)}, u32[]{:S(2)}) collective-permute-start(bf16[64,1024]{1,0:T(8,128)(2,1)S(1)} %get-tuple-element.171), channel_id=1, source_target_pairs={{0,3},{1,2},{2,1},{3,0},{4,7},{5,6},{6,5},{7,4},{8,11},{9,10},{10,... | collective-permute-start | bytes 393224 | tf_op jit(solution)/shard_map/ppermute | solution.py:383
  124.7 15.7 %collective-permute-start.30 = (bf16[64,1024]{1,0:T(8,128)(2,1)S(1)}, bf16[64,1024]{1,0:T(8,128)(2,1)S(1)}, u32[]{:S(2)}, u32[]{:S(2)}) collective-permute-start(bf16[64,1024]{1,0:T(8,128)(2,1)S(1)} %get-tuple-element.178), channel_id=1, source_target_pairs={{0,1},{1,0},{2,3},{3,2},{4,5},{5,4},{6,7},{7,6},{8,9},{9,8},{10,11... | collective-permute-start | bytes 393224 | tf_op jit(solution)/shard_map/ppermute | solution.py:383
  124.7 15.7 %collective-permute-start.31 = (bf16[64,1024]{1,0:T(8,128)(2,1)S(1)}, bf16[64,1024]{1,0:T(8,128)(2,1)S(1)}, u32[]{:S(2)}, u32[]{:S(2)}) collective-permute-start(bf16[64,1024]{1,0:T(8,128)(2,1)S(1)} %get-tuple-element.179), channel_id=1, source_target_pairs={{0,2},{1,3},{2,0},{3,1},{4,6},{5,7},{6,4},{7,5},{8,10},{9,11},{10,... | collective-permute-start | bytes 393224 | tf_op jit(solution)/shard_map/ppermute | solution.py:383
  127.8 12.6 %collective-permute-start.32 = (bf16[64,1024]{1,0:T(8,128)(2,1)S(1)}, bf16[64,1024]{1,0:T(8,128)(2,1)S(1)}, u32[]{:S(2)}, u32[]{:S(2)}) collective-permute-start(bf16[64,1024]{1,0:T(8,128)(2,1)S(1)} %get-tuple-element.180), channel_id=1, source_target_pairs={{0,3},{1,2},{2,1},{3,0},{4,7},{5,6},{6,5},{7,4},{8,11},{9,10},{10,... | collective-permute-start | bytes 393224 | tf_op jit(solution)/shard_map/ppermute | solution.py:383
  (10 other events, 114.5 us)
